TPU v7x, 512 devices: a whole 4x4x16 slice. The times are simulated.
512 devices in a mesh: head: 8 (over x, core), seq: 64 (over y, z).
Axes of the slice: x: 4, y: 4, z: 16, core: 2. Of those that a mesh axis runs over, the one named last changes fastest.
Arguments:
- queries: bfloat16 [32768, 4096], P('seq', 'head'), may hold values from -6 to 6
- keys: bfloat16 [32768, 4096], P('seq', 'head'), may hold values from -6 to 6
- values: bfloat16 [32768, 4096], P('seq', 'head'), may hold values from -6 to 6
- out_grad: bfloat16 [32768, 4096], P('seq', 'head'), may hold values from -8 to 8
- inputs: bfloat16 [32768, 2048], P('seq'), may hold values from -100 to 100
- momentum: float32 [2048, 4096], P('seq', 'head'), may hold values from -6 to 6
- level_weight: int32 [18, 32], replicated, may hold values from 1 to 8
Outputs:
- query_grad: bfloat16 [32768, 4096], P('seq', 'head')
- key_grad: bfloat16 [32768, 4096], P('seq', 'head')
- value_grad: bfloat16 [32768, 4096], P('seq', 'head')
- new_momentum: float32 [2048, 4096], P('seq', 'head')
All inputs are finite; a program needn't handle non-finite values.
Results may differ from a plain program's by a relative error of at most 0.0095.
Values may be sent and summed in bfloat16 or wider, within the bound.
No kernel may reach another device: no remote copies, remote signals or barrier semaphores. Data moves between devices by JAX's collectives and lax.ppermute only.
A program may use at most 64 MiB of HBM per device.

v0:
```python
import math

import jax
import jax.numpy as jnp
from jax import lax
from jax.sharding import Mesh
from jax.sharding import PartitionSpec as P

D_HEAD = 128
HEAD = ("head_0", "head_1")
SEQ = ("seq_0", "seq_1")
HEAD_SEQ = ("head_0", "head_1", "seq_0", "seq_1")


clip_norm = 1024.0
momentum_rate = 0.9


def partner(x, axis, apart):
    return lax.ppermute(x, axis, [(i, i ^ 1 << apart) for i in range(lax.axis_size(axis))])


def summed_rows(terms, axes):
    total = terms.astype(jnp.bfloat16)
    for axis in axes:
        total = lax.psum_scatter(total, axis, scatter_dimension=0, tiled=True)
    return total.astype(jnp.float32)


def by_axis(x, axes):
    for axis in axes:
        x = lax.psum(x, axis)
    return x


def bit_length(numbers, count):
    total = jnp.zeros_like(numbers)
    for place in range(count):
        total = total + (jnp.right_shift(numbers, place) > 0).astype(jnp.int32)
    return total


def level_table(level_weight, head_size):
    levels = jnp.arange(level_weight.shape[0], dtype=jnp.float32)
    factor = jnp.exp2(-0.5 * levels) / (8.0 * math.sqrt(head_size))
    return level_weight.astype(jnp.float32) * factor[:, None]


def lookup(level, table):
    onehot = (level[..., None] == jnp.arange(table.shape[0], dtype=jnp.int32)).astype(jnp.float32)
    flat = onehot.reshape(-1, table.shape[0])
    picked = jnp.dot(flat, table, precision=lax.Precision.HIGHEST)
    return picked.reshape(level.shape + (table.shape[1],))


def intra_weights(length, table):
    place = jnp.arange(length, dtype=jnp.int32)
    level = bit_length(jnp.bitwise_xor(place[:, None], place[None, :]), table.shape[0])
    picked = lookup(level, table)
    causal = (place[None, :] <= place[:, None])[..., None]
    return jnp.transpose(jnp.where(causal, picked, jnp.float32(0.0)), (2, 0, 1))


def local_grads(query, key_rows, value_rows, grad_rows, weights):
    scores = jnp.einsum("thd,shd->hts", query, key_rows, preferred_element_type=jnp.float32)
    mixed = (weights * scores).astype(jnp.bfloat16)
    value_part = jnp.einsum("hts,thd->shd", mixed, grad_rows, preferred_element_type=jnp.float32)
    before = jnp.einsum("thd,shd->hts", grad_rows, value_rows, preferred_element_type=jnp.float32)
    dmix = (weights * before).astype(jnp.bfloat16)
    query_part = jnp.einsum("hts,shd->thd", dmix, key_rows, preferred_element_type=jnp.float32)
    key_part = jnp.einsum("hts,thd->shd", dmix, query, preferred_element_type=jnp.float32)
    return (query_part, key_part, value_part)


def body(queries, keys, values, out_grad, inputs, momentum, level_weight):
    length = queries.shape[0]
    per_dev = queries.shape[1] // D_HEAD
    width = per_dev * D_HEAD
    table_all = level_table(level_weight, D_HEAD)
    table = lax.dynamic_slice_in_dim(table_all, lax.axis_index(HEAD) * per_dev, per_dev, 1)
    shape = (length, per_dev, D_HEAD)
    query = queries.reshape(shape)
    key_rows = keys.reshape(shape)
    value_rows = values.reshape(shape)
    grad_rows = out_grad.reshape(shape)
    states = jnp.einsum(
        "thd,the->hde", key_rows, value_rows, preferred_element_type=jnp.float32
    ).astype(jnp.bfloat16)
    grads = jnp.einsum("thd,the->hde", query, grad_rows, preferred_element_type=jnp.float32).astype(
        jnp.bfloat16
    )
    rank = lax.axis_index(SEQ)
    depth = lax.axis_size(SEQ).bit_length() - 1
    base_level = length.bit_length() - 1
    empty = jnp.zeros((per_dev, D_HEAD, D_HEAD), jnp.float32)
    block = (states.astype(jnp.float32), grads.astype(jnp.float32))
    state_sum = empty
    grad_sum = empty
    for bit in range(depth):
        other = (
            partner(block[0].astype(jnp.bfloat16), SEQ, bit).astype(jnp.float32),
            partner(block[1].astype(jnp.bfloat16), SEQ, bit).astype(jnp.float32),
        )
        weight = table[base_level + bit + 1][:, None, None]
        upper = jnp.bitwise_and(jnp.right_shift(rank, bit), 1) == 1
        state_sum = state_sum + jnp.where(upper, weight * other[0], jnp.float32(0.0))
        grad_sum = grad_sum + jnp.where(upper, jnp.float32(0.0), weight * other[1])
        block = (block[0] + other[0], block[1] + other[1])
    carried = state_sum.astype(jnp.bfloat16)
    returned = grad_sum.astype(jnp.bfloat16)
    weights = intra_weights(length, table)
    query_part, key_part, value_part = local_grads(query, key_rows, value_rows, grad_rows, weights)
    query_grad = query_part + jnp.einsum(
        "the,hde->thd", grad_rows, carried, preferred_element_type=jnp.float32
    )
    key_grad = key_part + jnp.einsum(
        "the,hde->thd", value_rows, returned, preferred_element_type=jnp.float32
    )
    value_grad = value_part + jnp.einsum(
        "thd,hde->the", key_rows, returned, preferred_element_type=jnp.float32
    )
    query_grad = query_grad.astype(jnp.bfloat16).reshape(length, width)
    key_grad = key_grad.astype(jnp.bfloat16).reshape(length, width)
    value_grad = value_grad.astype(jnp.bfloat16).reshape(length, width)
    shard = summed_rows(
        lax.dot_general(
            inputs, value_grad, (((0,), (0,)), ((), ())), preferred_element_type=jnp.float32
        ),
        SEQ,
    )
    total = by_axis(jnp.sum(shard * shard), HEAD_SEQ)
    factor = jnp.minimum(jnp.float32(1.0), clip_norm / jnp.sqrt(total + 1e-06))
    new_momentum = momentum_rate * momentum + factor * shard
    return (query_grad, key_grad, value_grad, new_momentum)


def solution(mesh):
    torus = Mesh(mesh.devices.reshape(4, 2, 4, 16), ("head_0", "head_1", "seq_0", "seq_1"))
    placed = (
        P(SEQ, HEAD),
        P(SEQ, HEAD),
        P(SEQ, HEAD),
        P(SEQ, HEAD),
        P(SEQ, None),
        P(SEQ, HEAD),
        P(),
    )
    return jax.shard_map(
        body,
        mesh=torus,
        in_specs=placed,
        out_specs=(P(SEQ, HEAD), P(SEQ, HEAD), P(SEQ, HEAD), P(SEQ, HEAD)),
        check_vma=False,
    )
```

profile of v0, /device:TPU:32, one launch (start us, length us, event | category | flops | bytes accessed | tf_op | source)
XLA Modules:
  0.0 279.5 jit_solution(11662807117163431342)
XLA Ops:
  7.2 1.4 copy.110
  8.6 1.4 convolution_convert_fusion.1
  10.0 7.4 %collective-permute-start.6 = (bf16[4,128,128]{2,1,0:T(8,128)(2,1)S(1)}, bf16[4,128,128]{2,1,0:T(8,128)(2,1)S(1)}, u32[]{:S(2)}, u32[]{:S(2)}) collective-permute-start(bf16[4,128,128]{2,1,0:T(8,128)(2,1)S(1)} %convolution_convert_fusion.1), channel_id=1, source_target_pairs={{0,1},{1,0},{2,3},{3,2},{4,5},{5,4},{6,7},{7,6},{8,9},{9,8},{10,11... | collective-permute-start | bytes 393224 | tf_op jit(solution)/shard_map/ppermute | solution.py:20
  17.4 2.9 %collective-permute-done.6 = bf16[4,128,128]{2,1,0:T(8,128)(2,1)S(1)} collective-permute-done((bf16[4,128,128]{2,1,0:T(8,128)(2,1)S(1)}, bf16[4,128,128]{2,1,0:T(8,128)(2,1)S(1)}, u32[]{:S(2)}, u32[]{:S(2)}) %collective-permute-start.6) | collective-permute-done | bytes 131104 | tf_op jit(solution)/shard_map/ppermute | solution.py:20
  21.0 2.0 collective-permute-start.7
  23.0 3.3 %convert_add_fusion = s32[512,512]{1,0:T(8,128)} fusion(), kind=kLoop, calls=%fused_computation.23 | loop fusion | flops 18874368 | bytes 1048576 | tf_op jit(solution)/shard_map/add | solution.py:39
  26.4 2.7 collective-permute-done.7
  29.2 7.9 %collective-permute-start.8 = (bf16[4,128,128]{2,1,0:T(8,128)(2,1)S(1)}, bf16[4,128,128]{2,1,0:T(8,128)(2,1)S(1)}, u32[]{:S(2)}, u32[]{:S(2)}) collective-permute-start(bf16[4,128,128]{2,1,0:T(8,128)(2,1)S(1)} %fusion.86), channel_id=1, source_target_pairs={{0,4},{1,5},{2,6},{3,7},{4,0},{5,1},{6,2},{7,3},{8,12},{9,13},{10,... | collective-permute-start | bytes 393224 | tf_op jit(solution)/shard_map/ppermute | solution.py:20
  37.9 6.7 %collective-permute-done.8 = bf16[4,128,128]{2,1,0:T(8,128)(2,1)S(1)} collective-permute-done((bf16[4,128,128]{2,1,0:T(8,128)(2,1)S(1)}, bf16[4,128,128]{2,1,0:T(8,128)(2,1)S(1)}, u32[]{:S(2)}, u32[]{:S(2)}) %collective-permute-start.8) | collective-permute-done | bytes 131104 | tf_op jit(solution)/shard_map/ppermute | solution.py:20
  44.7 12.8 %collective-permute-start.9 = (bf16[4,128,128]{2,1,0:T(8,128)(2,1)S(1)}, bf16[4,128,128]{2,1,0:T(8,128)(2,1)S(1)}, u32[]{:S(2)}, u32[]{:S(2)}) collective-permute-start(bf16[4,128,128]{2,1,0:T(8,128)(2,1)S(1)} %fusion.64), channel_id=1, source_target_pairs={{0,8},{1,9},{2,10},{3,11},{4,12},{5,13},{6,14},{7,15},{8,0},{9,1},... | collective-permute-start | bytes 393224 | tf_op jit(solution)/shard_map/ppermute | solution.py:20
  57.6 10.5 %fusion = f32[4,512,512]{2,0,1:T(4,128)} fusion(s32[512,512]{1,0:T(8,128)} %convert_add_fusion, f32[18,4]{1,0:T(8,128)S(1)} %fusion.81), kind=kOutput, calls=%fused_computation.1 | convolution fusion | flops 231211008 | bytes 5243168 | tf_op jit(solution)/shard_map/dot_general | solution.py:52
  69.6 3.5 %collective-permute-start.10 = (bf16[4,128,128]{2,1,0:T(8,128)(2,1)}, bf16[4,128,128]{2,1,0:T(8,128)(2,1)}, u32[]{:S(2)}, u32[]{:S(2)}) collective-permute-start(bf16[4,128,128]{2,1,0:T(8,128)(2,1)} %fusion.80), channel_id=1, source_target_pairs={{0,16},{1,17},{2,18},{3,19},{4,20},{5,21},{6,22},{7,23},{8,24},{9,... | collective-permute-start | bytes 393224 | tf_op jit(solution)/shard_map/ppermute | solution.py:20
  73.1 5.7 %fusion.4 = f32[512,4,128]{0,2,1:T(8,128)} fusion(bf16[512,4,128]{0,2,1:T(8,128)(2,1)S(1)} %bitcast.115, f32[4,512,512]{2,0,1:T(4,128)} %fusion, pred[512,512]{1,0:T(8,128)(4,1)} %iota_compare_fusion.2, bf16[512,512]{1,0:T(8,128)(2,1)} %param.7, bf16[512,512]{1,0:T(8,128)(2,1)S(1)} %copy-done.2), kind=kOutput, calls=%fused_computation.11 | convolution fusion | flops 540016640 | bytes 7077888 | tf_op jit(solution)/shard_map/hts,thd->shd/dot_general | solution.py:67
  78.8 1.1 fusion.58
  79.9 5.0 %collective-permute-start.11 = (bf16[4,128,128]{2,1,0:T(8,128)(2,1)S(1)}, bf16[4,128,128]{2,1,0:T(8,128)(2,1)S(1)}, u32[]{:S(2)}, u32[]{:S(2)}) collective-permute-start(bf16[4,128,128]{2,1,0:T(8,128)(2,1)S(1)} %fusion.58), channel_id=1, source_target_pairs={{0,32},{1,33},{2,34},{3,35},{4,36},{5,37},{6,38},{7,39},{8,40},{9,... | collective-permute-start | bytes 393224 | tf_op jit(solution)/shard_map/ppermute | solution.py:20
  85.0 3.3 %collective-permute-done.11 = bf16[4,128,128]{2,1,0:T(8,128)(2,1)S(1)} collective-permute-done((bf16[4,128,128]{2,1,0:T(8,128)(2,1)S(1)}, bf16[4,128,128]{2,1,0:T(8,128)(2,1)S(1)}, u32[]{:S(2)}, u32[]{:S(2)}) %collective-permute-start.11) | collective-permute-done | bytes 131104 | tf_op jit(solution)/shard_map/ppermute | solution.py:20
  89.0 2.0 fusion.10
  91.8 2.6 fusion.2
  94.5 1.4 convolution_convert_fusion.2
  95.9 6.7 %collective-permute-start = (bf16[4,128,128]{2,1,0:T(8,128)(2,1)S(1)}, bf16[4,128,128]{2,1,0:T(8,128)(2,1)S(1)}, u32[]{:S(2)}, u32[]{:S(2)}) collective-permute-start(bf16[4,128,128]{2,1,0:T(8,128)(2,1)S(1)} %convolution_convert_fusion.2), channel_id=1, source_target_pairs={{0,1},{1,0},{2,3},{3,2},{4,5},{5,4},{6,7},{7,6},{8,9},{9,8},{10,11... | collective-permute-start | bytes 393224 | tf_op jit(solution)/shard_map/ppermute | solution.py:20
  102.6 2.9 %collective-permute-done = bf16[4,128,128]{2,1,0:T(8,128)(2,1)S(1)} collective-permute-done((bf16[4,128,128]{2,1,0:T(8,128)(2,1)S(1)}, bf16[4,128,128]{2,1,0:T(8,128)(2,1)S(1)}, u32[]{:S(2)}, u32[]{:S(2)}) %collective-permute-start) | collective-permute-done | bytes 131104 | tf_op jit(solution)/shard_map/ppermute | solution.py:20
  105.6 1.9 collective-permute-start.1
  107.5 5.9 %collective-permute-done.1 = bf16[4,128,128]{2,1,0:T(8,128)(2,1)S(1)} collective-permute-done((bf16[4,128,128]{2,1,0:T(8,128)(2,1)S(1)}, bf16[4,128,128]{2,1,0:T(8,128)(2,1)S(1)}, u32[]{:S(2)}, u32[]{:S(2)}) %collective-permute-start.1) | collective-permute-done | bytes 131104 | tf_op jit(solution)/shard_map/ppermute | solution.py:20
  113.5 6.9 %collective-permute-start.2 = (bf16[4,128,128]{2,1,0:T(8,128)(2,1)S(1)}, bf16[4,128,128]{2,1,0:T(8,128)(2,1)S(1)}, u32[]{:S(2)}, u32[]{:S(2)}) collective-permute-start(bf16[4,128,128]{2,1,0:T(8,128)(2,1)S(1)} %fusion.85), channel_id=1, source_target_pairs={{0,4},{1,5},{2,6},{3,7},{4,0},{5,1},{6,2},{7,3},{8,12},{9,13},{10,... | collective-permute-start | bytes 393224 | tf_op jit(solution)/shard_map/ppermute | solution.py:20
  120.4 4.2 %multiply_convert_fusion.1 = bf16[4,512,512]{2,1,0:T(8,128)(2,1)S(1)} fusion(f32[4,512,512]{2,0,1:T(4,128)} %fusion, bf16[512,4,128]{0,2,1:T(8,128)(2,1)S(1)} %bitcast.116, pred[512,512]{1,0:T(8,128)(4,1)} %iota_compare_fusion.2, bf16[512,512]{1,0:T(8,128)(2,1)} %param.9), kind=kOutput, calls=%fused_computation.5 | convolution fusion | flops 271581184 | bytes 7602176 | tf_op jit(solution)/shard_map/thd,shd->hts/dot_general | solution.py:68
  124.6 2.6 collective-permute-done.2
  128.0 5.5 %collective-permute-start.3 = (bf16[4,128,128]{2,1,0:T(8,128)(2,1)}, bf16[4,128,128]{2,1,0:T(8,128)(2,1)}, u32[]{:S(2)}, u32[]{:S(2)}) collective-permute-start(bf16[4,128,128]{2,1,0:T(8,128)(2,1)} %fusion.63), channel_id=1, source_target_pairs={{0,8},{1,9},{2,10},{3,11},{4,12},{5,13},{6,14},{7,15},{8,0},{9,1},... | collective-permute-start | bytes 393224 | tf_op jit(solution)/shard_map/ppermute | solution.py:20
  133.5 1.5 convolution_bitcast_fusion
  135.0 2.0 copy.108
  137.1 7.4 %collective-permute-done.3 = bf16[4,128,128]{2,1,0:T(8,128)(2,1)} collective-permute-done((bf16[4,128,128]{2,1,0:T(8,128)(2,1)}, bf16[4,128,128]{2,1,0:T(8,128)(2,1)}, u32[]{:S(2)}, u32[]{:S(2)}) %collective-permute-start.3) | collective-permute-done | bytes 131104 | tf_op jit(solution)/shard_map/ppermute | solution.py:20
  144.5 1.8 fusion.79
  146.3 1.9 collective-permute-start.4
  148.2 3.4 %convolution_bitcast_fusion.1 = f32[512,4,128]{0,2,1:T(8,128)} fusion(bf16[4,512,512]{2,1,0:T(8,128)(2,1)} %copy-done.1, bf16[512,512]{1,0:T(8,128)(2,1)S(1)} %copy-done.2), kind=kOutput, calls=%fused_computation.10 | convolution fusion | flops 268435456 | bytes 3670016 | tf_op jit(solution)/shard_map/hts,shd->thd/dot_general | solution.py:70
  151.6 1.7 copy.100
  153.5 1.9 fusion.46
  155.4 5.0 %collective-permute-start.5 = (bf16[4,128,128]{2,1,0:T(8,128)(2,1)}, bf16[4,128,128]{2,1,0:T(8,128)(2,1)}, u32[]{:S(2)}, u32[]{:S(2)}) collective-permute-start(bf16[4,128,128]{2,1,0:T(8,128)(2,1)} %fusion.46), channel_id=1, source_target_pairs={{0,32},{1,33},{2,34},{3,35},{4,36},{5,37},{6,38},{7,39},{8,40},{9,... | collective-permute-start | bytes 393224 | tf_op jit(solution)/shard_map/ppermute | solution.py:20
  160.5 2.9 %fusion.9 = bf16[512,4,128]{0,2,1:T(8,128)(2,1)} fusion(f32[512,4,128]{0,2,1:T(8,128)} %convolution_bitcast_fusion, bf16[4,128,128]{2,1,0:T(8,128)(2,1)S(1)} %collective-permute-done.6, bf16[4,128,128]{2,1,0:T(8,128)(2,1)S(1)} %collective-permute-done.7, bf16[4,128,128]{2,1,0:T(8,128)(2,1)} %copy-done.4, bf16[4,128,128]{2,1,0:T(8,128)(2,1)} %copy-done.9, ...), kind=kOutput, calls=%fused_computation.19 | convolution fusion | flops 69206016 | bytes 2883686 | tf_op jit(solution)/shard_map/the,hde->thd/dot_general | solution.py:116
  163.4 43.5 %reduce-scatter.7.cloned.1.call-done = bf16[32,512]{1,0:T(8,128)(2,1)} async-done(((bf16[512,512]{1,0:T(8,128)(2,1)}), bf16[32,512]{1,0:T(8,128)(2,1)}) %reduce-scatter.7.cloned.1.call-update) | async-done | bytes 32784
  206.8 0.9 copy.109
  208.4 2.8 fusion.8
  211.2 11.2 %psum.28 = f32[]{:T(128)} all-reduce(f32[]{:T(128)} %fusion.59), channel_id=1, replica_groups=mesh['head_0'=4,'head_1'=2,'seq_0'=4,'seq_1'=16] {'head_0'}, use_global_device_ids=true, to_apply=%region_3.4 | all-reduce | flops 1 | bytes 8 | tf_op jit(solution)/shard_map/psum | solution.py:32
  222.4 1.0 copy.103
  223.4 3.1 %psum.29 = f32[]{:T(128)} all-reduce(f32[]{:T(128)} %psum.28), channel_id=1, replica_groups=mesh['head_0'=4,'head_1'=2,'seq_0'=4,'seq_1'=16] {'head_1'}, use_global_device_ids=true, to_apply=%region_4.5 | all-reduce | flops 1 | bytes 8 | tf_op jit(solution)/shard_map/psum | solution.py:32
  226.4 2.0 copy.102
  228.5 11.0 %psum.30 = f32[]{:T(128)} all-reduce(f32[]{:T(128)} %psum.29), channel_id=1, replica_groups=mesh['head_0'=4,'head_1'=2,'seq_0'=4,'seq_1'=16] {'seq_0'}, use_global_device_ids=true, to_apply=%region_5.6 | all-reduce | flops 1 | bytes 8 | tf_op jit(solution)/shard_map/psum | solution.py:32
  239.5 2.0 copy.101
  241.6 28.7 %psum.31 = f32[]{:T(128)} all-reduce(f32[]{:T(128)} %psum.30), channel_id=1, replica_groups=mesh['head_0'=4,'head_1'=2,'seq_0'=4,'seq_1'=16] {'seq_1'}, use_global_device_ids=true, to_apply=%region_6.7 | all-reduce | flops 1 | bytes 8 | tf_op jit(solution)/shard_map/psum | solution.py:32
  271.0 1.0 fusion.60
  (62 shorter events, 7.2 us)
Async XLA Ops:
  7.2 84.6 %copy-start = (bf16[512,2048]{1,0:T(8,128)(2,1)S(1)}, bf16[512,2048]{1,0:T(8,128)(2,1)}, u32[]{:S(2)}) copy-start(bf16[512,2048]{1,0:T(8,128)(2,1)} %param.11) | copy-start | bytes 6291460
  7.2 127.8 %reduce-scatter.5.cloned.1.call-start = ((), (), s32[]{:S(2)}) async-start(), calls=%async_computation.2 | async-start | bytes 2621440 | tf_op jit(solution)/shard_map/reduce_scatter | solution.py:26
  10.0 10.3 %collective-permute-start.6 = (bf16[4,128,128]{2,1,0:T(8,128)(2,1)S(1)}, bf16[4,128,128]{2,1,0:T(8,128)(2,1)S(1)}, u32[]{:S(2)}, u32[]{:S(2)}) collective-permute-start(bf16[4,128,128]{2,1,0:T(8,128)(2,1)S(1)} %convolution_convert_fusion.1), channel_id=1, source_target_pairs={{0,1},{1,0},{2,3},{3,2},{4,5},{5,4},{6,7},{7,6},{8,9},{9,8},{10,11... | collective-permute-start | bytes 393224 | tf_op jit(solution)/shard_map/ppermute | solution.py:20
  21.0 8.1 %collective-permute-start.7 = (bf16[4,128,128]{2,1,0:T(8,128)(2,1)}, bf16[4,128,128]{2,1,0:T(8,128)(2,1)S(1)}, u32[]{:S(2)}, u32[]{:S(2)}) collective-permute-start(bf16[4,128,128]{2,1,0:T(8,128)(2,1)} %fusion.62), channel_id=1, source_target_pairs={{0,2},{1,3},{2,0},{3,1},{4,6},{5,7},{6,4},{7,5},{8,10},{9,11},{10,... | collective-permute-start | bytes 393224 | tf_op jit(solution)/shard_map/ppermute | solution.py:20
  26.4 46.8 %copy-start.2 = (bf16[512,512]{1,0:T(8,128)(2,1)S(1)}, bf16[512,512]{1,0:T(8,128)(2,1)}, u32[]{:S(2)}) copy-start(bf16[512,512]{1,0:T(8,128)(2,1)} %param.8) | copy-start | bytes 1572868
  29.2 15.5 %collective-permute-start.8 = (bf16[4,128,128]{2,1,0:T(8,128)(2,1)S(1)}, bf16[4,128,128]{2,1,0:T(8,128)(2,1)S(1)}, u32[]{:S(2)}, u32[]{:S(2)}) collective-permute-start(bf16[4,128,128]{2,1,0:T(8,128)(2,1)S(1)} %fusion.86), channel_id=1, source_target_pairs={{0,4},{1,5},{2,6},{3,7},{4,0},{5,1},{6,2},{7,3},{8,12},{9,13},{10,... | collective-permute-start | bytes 393224 | tf_op jit(solution)/shard_map/ppermute | solution.py:20
  44.6 24.3 %copy-start.4 = (bf16[4,128,128]{2,1,0:T(8,128)(2,1)}, bf16[4,128,128]{2,1,0:T(8,128)(2,1)S(1)}, u32[]{:S(2)}) copy-start(bf16[4,128,128]{2,1,0:T(8,128)(2,1)S(1)} %collective-permute-done.8) | copy-start | bytes 393220
  44.7 24.2 %collective-permute-start.9 = (bf16[4,128,128]{2,1,0:T(8,128)(2,1)S(1)}, bf16[4,128,128]{2,1,0:T(8,128)(2,1)S(1)}, u32[]{:S(2)}, u32[]{:S(2)}) collective-permute-start(bf16[4,128,128]{2,1,0:T(8,128)(2,1)S(1)} %fusion.64), channel_id=1, source_target_pairs={{0,8},{1,9},{2,10},{3,11},{4,12},{5,13},{6,14},{7,15},{8,0},{9,1},... | collective-permute-start | bytes 393224 | tf_op jit(solution)/shard_map/ppermute | solution.py:20
  68.9 0.8 copy-start.9
  69.6 9.2 %collective-permute-start.10 = (bf16[4,128,128]{2,1,0:T(8,128)(2,1)}, bf16[4,128,128]{2,1,0:T(8,128)(2,1)}, u32[]{:S(2)}, u32[]{:S(2)}) collective-permute-start(bf16[4,128,128]{2,1,0:T(8,128)(2,1)} %fusion.80), channel_id=1, source_target_pairs={{0,16},{1,17},{2,18},{3,19},{4,20},{5,21},{6,22},{7,23},{8,24},{9,... | collective-permute-start | bytes 393224 | tf_op jit(solution)/shard_map/ppermute | solution.py:20
  79.9 8.4 %collective-permute-start.11 = (bf16[4,128,128]{2,1,0:T(8,128)(2,1)S(1)}, bf16[4,128,128]{2,1,0:T(8,128)(2,1)S(1)}, u32[]{:S(2)}, u32[]{:S(2)}) collective-permute-start(bf16[4,128,128]{2,1,0:T(8,128)(2,1)S(1)} %fusion.58), channel_id=1, source_target_pairs={{0,32},{1,33},{2,34},{3,35},{4,36},{5,37},{6,38},{7,39},{8,40},{9,... | collective-permute-start | bytes 393224 | tf_op jit(solution)/shard_map/ppermute | solution.py:20
  85.0 6.0 %copy-start.12 = (f32[4]{0:T(128)}, f32[4]{0:T(128)S(1)}, u32[]{:S(2)}) copy-start(f32[4]{0:T(128)S(1)} %get-tuple-element.21) | copy-start | bytes 52
  85.0 6.0 %copy-start.14 = (f32[4]{0:T(128)}, f32[4]{0:T(128)S(1)}, u32[]{:S(2)}) copy-start(f32[4]{0:T(128)S(1)} %get-tuple-element.22) | copy-start | bytes 52
  85.0 6.0 %copy-start.16 = (f32[4]{0:T(128)}, f32[4]{0:T(128)S(1)}, u32[]{:S(2)}) copy-start(f32[4]{0:T(128)S(1)} %get-tuple-element.23) | copy-start | bytes 52
  85.0 6.0 %copy-start.18 = (f32[4]{0:T(128)}, f32[4]{0:T(128)S(1)}, u32[]{:S(2)}) copy-start(f32[4]{0:T(128)S(1)} %get-tuple-element.24) | copy-start | bytes 52
  85.0 6.0 %copy-start.19 = (f32[4]{0:T(128)}, f32[4]{0:T(128)S(1)}, u32[]{:S(2)}) copy-start(f32[4]{0:T(128)S(1)} %get-tuple-element.25) | copy-start | bytes 52
  88.3 0.7 copy-start.11
  91.0 0.8 copy-start.7
  94.4 112.4 %reduce-scatter.7.cloned.1.call-start = ((), (), s32[]{:S(2)}) async-start(), calls=%async_computation.3 | async-start | bytes 557056
  95.9 31.4 %copy-start.6 = (bf16[4,128,128]{2,1,0:T(8,128)(2,1)}, bf16[4,128,128]{2,1,0:T(8,128)(2,1)S(1)}, u32[]{:S(2)}) copy-start(bf16[4,128,128]{2,1,0:T(8,128)(2,1)S(1)} %convolution_convert_fusion.2) | copy-start | bytes 393220
  95.9 9.7 %collective-permute-start = (bf16[4,128,128]{2,1,0:T(8,128)(2,1)S(1)}, bf16[4,128,128]{2,1,0:T(8,128)(2,1)S(1)}, u32[]{:S(2)}, u32[]{:S(2)}) collective-permute-start(bf16[4,128,128]{2,1,0:T(8,128)(2,1)S(1)} %convolution_convert_fusion.2), channel_id=1, source_target_pairs={{0,1},{1,0},{2,3},{3,2},{4,5},{5,4},{6,7},{7,6},{8,9},{9,8},{10,11... | collective-permute-start | bytes 393224 | tf_op jit(solution)/shard_map/ppermute | solution.py:20
  105.6 7.9 %collective-permute-start.1 = (bf16[4,128,128]{2,1,0:T(8,128)(2,1)S(1)}, bf16[4,128,128]{2,1,0:T(8,128)(2,1)S(1)}, u32[]{:S(2)}, u32[]{:S(2)}) collective-permute-start(bf16[4,128,128]{2,1,0:T(8,128)(2,1)S(1)} %fusion.61), channel_id=1, source_target_pairs={{0,2},{1,3},{2,0},{3,1},{4,6},{5,7},{6,4},{7,5},{8,10},{9,11},{10,... | collective-permute-start | bytes 393224 | tf_op jit(solution)/shard_map/ppermute | solution.py:20
  113.5 14.5 %copy-start.5 = (bf16[4,128,128]{2,1,0:T(8,128)(2,1)}, bf16[4,128,128]{2,1,0:T(8,128)(2,1)S(1)}, u32[]{:S(2)}) copy-start(bf16[4,128,128]{2,1,0:T(8,128)(2,1)S(1)} %collective-permute-done.1) | copy-start | bytes 393220
  113.5 20.0 %copy-start.3 = (bf16[512,512]{1,0:T(8,128)(2,1)S(1)}, bf16[512,512]{1,0:T(8,128)(2,1)}, u32[]{:S(2)}) copy-start(bf16[512,512]{1,0:T(8,128)(2,1)} %param.7) | copy-start | bytes 1572868
  113.5 13.7 %collective-permute-start.2 = (bf16[4,128,128]{2,1,0:T(8,128)(2,1)S(1)}, bf16[4,128,128]{2,1,0:T(8,128)(2,1)S(1)}, u32[]{:S(2)}, u32[]{:S(2)}) collective-permute-start(bf16[4,128,128]{2,1,0:T(8,128)(2,1)S(1)} %fusion.85), channel_id=1, source_target_pairs={{0,4},{1,5},{2,6},{3,7},{4,0},{5,1},{6,2},{7,3},{8,12},{9,13},{10,... | collective-permute-start | bytes 393224 | tf_op jit(solution)/shard_map/ppermute | solution.py:20
  124.6 8.9 %copy-start.1 = (bf16[4,512,512]{2,1,0:T(8,128)(2,1)}, bf16[4,512,512]{2,1,0:T(8,128)(2,1)S(1)}, u32[]{:S(2)}) copy-start(bf16[4,512,512]{2,1,0:T(8,128)(2,1)S(1)} %multiply_convert_fusion.1) | copy-start | bytes 6291460
  127.2 6.3 %copy-start.10 = (bf16[4,128,128]{2,1,0:T(8,128)(2,1)}, bf16[4,128,128]{2,1,0:T(8,128)(2,1)S(1)}, u32[]{:S(2)}) copy-start(bf16[4,128,128]{2,1,0:T(8,128)(2,1)S(1)} %collective-permute-done.2) | copy-start | bytes 393220
  128.0 16.5 %collective-permute-start.3 = (bf16[4,128,128]{2,1,0:T(8,128)(2,1)}, bf16[4,128,128]{2,1,0:T(8,128)(2,1)}, u32[]{:S(2)}, u32[]{:S(2)}) collective-permute-start(bf16[4,128,128]{2,1,0:T(8,128)(2,1)} %fusion.63), channel_id=1, source_target_pairs={{0,8},{1,9},{2,10},{3,11},{4,12},{5,13},{6,14},{7,15},{8,0},{9,1},... | collective-permute-start | bytes 393224 | tf_op jit(solution)/shard_map/ppermute | solution.py:20
  135.0 25.4 %copy-start.13 = (f32[4]{0:T(128)S(1)}, f32[4]{0:T(128)}, u32[]{:S(2)}) copy-start(f32[4]{0:T(128)} %copy-done.12) | copy-start | bytes 52
  135.0 25.4 %copy-start.15 = (f32[4]{0:T(128)S(1)}, f32[4]{0:T(128)}, u32[]{:S(2)}) copy-start(f32[4]{0:T(128)} %copy-done.14) | copy-start | bytes 52
  135.0 25.4 %copy-start.17 = (f32[4]{0:T(128)S(1)}, f32[4]{0:T(128)}, u32[]{:S(2)}) copy-start(f32[4]{0:T(128)} %copy-done.16) | copy-start | bytes 52
  146.3 7.2 %collective-permute-start.4 = (bf16[4,128,128]{2,1,0:T(8,128)(2,1)}, bf16[4,128,128]{2,1,0:T(8,128)(2,1)}, u32[]{:S(2)}, u32[]{:S(2)}) collective-permute-start(bf16[4,128,128]{2,1,0:T(8,128)(2,1)} %fusion.79), channel_id=1, source_target_pairs={{0,16},{1,17},{2,18},{3,19},{4,20},{5,21},{6,22},{7,23},{8,24},{9,... | collective-permute-start | bytes 393224 | tf_op jit(solution)/shard_map/ppermute | solution.py:20
  151.6 70.8 %copy-start.8 = (bf16[512,4,128]{0,2,1:T(8,128)(2,1)S(1)}, bf16[512,4,128]{0,2,1:T(8,128)(2,1)}, u32[]{:S(2)}) copy-start(bf16[512,4,128]{0,2,1:T(8,128)(2,1)} %copy-done.7) | copy-start | bytes 1572868
  155.4 53.0 %collective-permute-start.5 = (bf16[4,128,128]{2,1,0:T(8,128)(2,1)}, bf16[4,128,128]{2,1,0:T(8,128)(2,1)}, u32[]{:S(2)}, u32[]{:S(2)}) collective-permute-start(bf16[4,128,128]{2,1,0:T(8,128)(2,1)} %fusion.46), channel_id=1, source_target_pairs={{0,32},{1,33},{2,34},{3,35},{4,36},{5,37},{6,38},{7,39},{8,40},{9,... | collective-permute-start | bytes 393224 | tf_op jit(solution)/shard_map/ppermute | solution.py:20
Sparse Core Ops, SparseCore 0:
  94.6 38.4 reduce-scatter.4
  137.2 69.5 reduce-scatter.6
where the time goes:
time: 281 us; the launch traced here: 280 us
  waiting for transfers between devices  78.2 us (28%)
  starting transfers between devices  66.6 us (24%)
  blocking collectives  54 us (19%)
  matrix products  38.3 us (14%)
  between operations  15.1 us (5%)
  other arithmetic  13.9 us (5%)
  local copies, waits for them, and re-layouts  13.4 us (5%)
    ppermute x12, starting transfers between devices, partner(): lax.ppermute(x, axis, [(i, i ^ 1 << apart) for i in range(lax.axis_size(a...  66.5 us
    psum x4, blocking collectives, by_axis(): x = lax.psum(x, axis)  54 us
    unnamed x3, waiting for transfers between devices  43.5 us
    ppermute x12, waiting for transfers between devices, partner(): lax.ppermute(x, axis, [(i, i ^ 1 << apart) for i in range(lax.axis_size(a...  34.7 us
    unnamed x47, local copies, waits for them, and re-layouts  12 us
    dot_general x1, matrix products, lookup(): picked = jnp.dot(flat, table, precision=lax.Precision.HIGHEST)  10.5 us
    dot_general x1, matrix products, local_grads(): jnp.einsum('hts,thd->shd', mixed, grad_rows, preferred_element_type=jnp.f...  5.68 us
  transfers between devices with their start and end apart: 14, of which 10 were waited for; matrix products, arithmetic and copies ran while one was open for 16% of the time, Pallas kernels for 0%

commit v1 on v0

v1 whole, which is shorter than its diff:
```python
import functools
import math

import jax
import jax.numpy as jnp
import numpy as np
from jax import lax
from jax.experimental import pallas as pl
from jax.experimental.pallas import tpu as pltpu
from jax.sharding import Mesh
from jax.sharding import PartitionSpec as P

D = 128
HEAD = ("head_0", "head_1")
Y = "seq_0"
Z = "seq_1"
SEQ = (Y, Z)

clip_norm = 1024.0
momentum_rate = 0.9

bf16 = jnp.bfloat16
f32 = jnp.float32

SMEM = pl.BlockSpec(memory_space=pltpu.SMEM)
VMEM = pl.BlockSpec(memory_space=pltpu.VMEM)


def dot(a, b, ca, cb):
    return lax.dot_general(a, b, (((ca,), (cb,)), ((), ())), preferred_element_type=f32)


def call(kernel, out_shape, operands, flops, scratch=(), vmem=16, scalars=0, after=()):
    n = len(operands)

    def run(*refs):
        kernel(*refs[:n], *refs[n + len(after) :])

    leaves = jax.tree.leaves((operands, out_shape))
    return pl.pallas_call(
        run,
        out_shape=out_shape,
        in_specs=[SMEM] * scalars
        + [VMEM] * (n - scalars)
        + [pl.BlockSpec(memory_space=pl.ANY)] * len(after),
        out_specs=jax.tree.map(lambda _: VMEM, out_shape),
        scratch_shapes=list(scratch),
        compiler_params=pltpu.CompilerParams(vmem_limit_bytes=vmem * 1024 * 1024),
        cost_estimate=pl.CostEstimate(
            flops=flops,
            bytes_accessed=sum(x.size * x.dtype.itemsize for x in leaves),
            transcendentals=0,
        ),
    )(*operands, *after)


def lanes(block):
    if isinstance(block, int):
        return slice(block * D, (block + 1) * D)
    return pl.ds(pl.multiple_of(block * D, D), D)


def lam(level, head, weight_ref):
    factor = np.float32(2.0 ** (-0.5 * level) / (8.0 * math.sqrt(D)))
    return weight_ref[level, head].astype(f32) * factor


def diagonal(head, weight_ref, transposed):
    row = lax.broadcasted_iota(jnp.int32, (D, D), 0)
    col = lax.broadcasted_iota(jnp.int32, (D, D), 1)
    apart = jnp.bitwise_xor(row, col)
    out = jnp.full((D, D), lam(0, head, weight_ref), f32)
    for level in range(1, D.bit_length()):
        out = jnp.where(apart >= 1 << (level - 1), lam(level, head, weight_ref), out)
    keep = row <= col if transposed else col <= row
    return jnp.where(keep, out, f32(0.0))


def far(i, j, head, weight_ref):
    return lam(D.bit_length() - 1 + (i ^ j).bit_length(), head, weight_ref)


def weighted(scores, first, own, head, weight_ref, diag):
    count = scores.shape[1] // D
    parts = []
    for n in range(count):
        part = scores[:, n * D : (n + 1) * D]
        w = diag if first + n == own else far(first + n, own, head, weight_ref)
        parts.append((w * part).astype(bf16))
    return parts[0] if count == 1 else jnp.concatenate(parts, axis=1)


def states_kernel(q_ref, k_ref, v_ref, g_ref, out_ref):
    for h in range(out_ref.shape[0]):
        s = lanes(h)
        out_ref[h, :D, :] = dot(q_ref[:, s], g_ref[:, s], 0, 0).astype(bf16)
        out_ref[h, D:, :] = dot(k_ref[:, s], v_ref[:, s], 0, 0).astype(bf16)


def keyed_kernel(info_ref, x_ref, k_ref, *out_refs):
    y = info_ref[1]
    n_out = len(out_refs)
    heads = [lanes(lax.rem(y + n, n_out)) for n in range(n_out)]
    keys = jnp.concatenate([k_ref[:, s] for s in heads], axis=1)
    width = 512
    for c in range(x_ref.shape[1] // width):
        part = slice(c * width, (c + 1) * width)
        res = dot(x_ref[:, part], keys, 0, 0).astype(bf16)
        for n in range(n_out):
            out_refs[n][part, :] = res[:, lanes(n)]


def local_kernel(info_ref, weight_ref, q_ref, k_ref, g_ref, x_ref, loc_ref, proj_ref, low_ref):
    heads = proj_ref.shape[0]
    blocks = q_ref.shape[0] // D
    for h in range(heads):
        s = lanes(h)
        head = info_ref[0] * heads + h
        diag = diagonal(head, weight_ref, True)
        for j in range(blocks):
            rows = slice(j * D, (j + 1) * D)
            scores = dot(k_ref[rows, s], q_ref[j * D :, s], 1, 1)
            mixed = weighted(scores, j, j, head, weight_ref, diag)
            res = dot(mixed, g_ref[j * D :, s], 1, 0)
            loc_ref[rows, s] = res
            low_ref[rows, s] = res.astype(bf16)
    width = 512
    for c in range(x_ref.shape[1] // width):
        part = slice(c * width, (c + 1) * width)
        res = dot(x_ref[:, part], low_ref[...], 0, 0).astype(bf16)
        for h in range(heads):
            proj_ref[h, part, :] = res[:, lanes(h)]


def tree_kernel(info_ref, weight_ref, in_ref, out_ref):
    nz, ny = in_ref.shape[:2]
    count = nz * ny
    depth = count.bit_length() - 1
    head = info_ref[0] * ny + info_ref[1]
    is_grad = info_ref[2] < nz // 2
    sums = [[in_ref[c % nz, c // nz].astype(f32) for c in range(count)]]
    for bit in range(depth - 1):
        last = sums[-1]
        sums.append([last[2 * b] + last[2 * b + 1] for b in range(len(last) // 2)])
    total = [jnp.zeros(in_ref.shape[2:], f32)]
    for bit in reversed(range(depth)):
        w = lam(D.bit_length() + 2 + bit, head, weight_ref)
        later = jnp.where(is_grad, w, f32(0.0))
        earlier = jnp.where(is_grad, f32(0.0), w)
        last = sums[bit]
        total = [
            total[b // 2] + (later * last[b + 1] if b % 2 == 0 else earlier * last[b - 1])
            for b in range(len(last))
        ]
    for c in range(count):
        out_ref[c % nz, c // nz] = total[c].astype(bf16)


def project_kernel(info_ref, a0, a1, a2, a3, loc_ref, r_ref, out_ref, *own_refs):
    y = info_ref[1]
    keyed = (a0, a1, a2, a3)
    n_y = len(keyed)
    half = r_ref.shape[0] // 2
    nz = out_ref.shape[0]
    each = out_ref.shape[1] // n_y
    states = []
    for n in range(n_y):
        states.append(r_ref[:half, lax.rem(y + n_y - n, n_y)].reshape(D, D))
        own_refs[n][...] = r_ref[:, lax.rem(y + n, n_y)].reshape(2 * D, D)
    rows = nz * each
    both = [jnp.concatenate(states[i : i + 2], axis=0) for i in range(0, n_y, 2)]
    for b in range(n_y):
        part = slice(b * rows, (b + 1) * rows)
        res = loc_ref[part, :].astype(f32)
        for i in range(0, n_y, 2):
            left = jnp.concatenate([keyed[i][part, :], keyed[i + 1][part, :]], axis=1)
            res = res + dot(left, both[i // 2], 1, 0)
        res = res.astype(bf16)
        for z in range(nz):
            out_ref[z, b * each : (b + 1) * each, :] = res[z * each : (z + 1) * each, :]


def outputs_kernel(
    info_ref, weight_ref, q_ref, k_ref, v_ref, g_ref, loc_ref, r0, r1, r2, r3, dq_ref, dk_ref, dv_ref
):
    y = info_ref[1]
    states = (r0, r1, r2, r3)
    n_y = len(states)
    blocks = q_ref.shape[0] // D
    for n in range(n_y):
        h = lax.rem(y + n_y - n, n_y)
        s = lanes(h)
        head = info_ref[0] * n_y + h
        returned = states[n][:D, :]
        carried = states[n][D:, :]
        query, keys, values, grad = q_ref[:, s], k_ref[:, s], v_ref[:, s], g_ref[:, s]
        dv_ref[:, s] = (loc_ref[:, s] + dot(keys, returned, 1, 0)).astype(bf16)
        base_k = dot(values, returned, 1, 1)
        base_q = dot(grad, carried, 1, 1)
        diag = diagonal(head, weight_ref, False)
        diag_t = diagonal(head, weight_ref, True)
        for i in range(blocks):
            rows = slice(i * D, (i + 1) * D)
            upto = (i + 1) * D
            before = dot(grad[rows], values[:upto], 1, 1)
            dmix = weighted(before, 0, i, head, weight_ref, diag)
            dq_ref[rows, s] = (base_q[rows] + dot(dmix, keys[:upto], 1, 0)).astype(bf16)
            after = dot(values[rows], grad[i * D :], 1, 1)
            dmix_t = weighted(after, i, i, head, weight_ref, diag_t)
            dk_ref[rows, s] = (base_k[rows] + dot(dmix_t, query[i * D :], 1, 0)).astype(bf16)


def shard_kernel(in_ref, out_ref):
    n_y, rows = out_ref.shape[0], out_ref.shape[1] - 8
    total = in_ref[0].astype(f32)
    for z in range(1, in_ref.shape[0]):
        total = total + in_ref[z].astype(f32)
    square = jnp.sum(jnp.sum(total * total, axis=0, keepdims=True), axis=1, keepdims=True)
    for b in range(n_y):
        out_ref[b, :rows, :] = total[b * rows : (b + 1) * rows, :]
        out_ref[b, rows:, :] = jnp.broadcast_to(square, (8, D))


def final_kernel(mom_ref, in_ref, total_ref, out_ref):
    rows = mom_ref.shape[0]
    total = jnp.sum(total_ref[...], axis=0)
    factor = jnp.minimum(f32(1.0), clip_norm / jnp.sqrt(total + 1e-06))
    for h in range(in_ref.shape[0]):
        s = lanes(h)
        out_ref[:, s] = momentum_rate * mom_ref[:, s] + factor * in_ref[h, :rows, :]


def shift(x, axis, by):
    n = lax.axis_size(axis)
    return lax.ppermute(x, axis, [(i, (i + by) % n) for i in range(n)])


def swap(x, axes):
    return lax.all_to_all(x, axes, 0, 0, tiled=True)


def body(queries, keys, values, out_grad, inputs, momentum, level_weight):
    length, width = queries.shape
    features = inputs.shape[1]
    n_y, n_z = lax.axis_size(Y), lax.axis_size(Z)
    heads = width // D
    sds = jax.ShapeDtypeStruct
    info = jnp.stack(
        [lax.axis_index(HEAD), lax.axis_index(Y), lax.axis_index(Z), jnp.int32(0)]
    ).astype(jnp.int32)

    both = call(
        states_kernel,
        sds((heads, 2 * D, D), bf16),
        (queries, keys, values, out_grad),
        4 * length * width * D,
    )
    keyed = call(
        keyed_kernel,
        tuple(sds((features, D), bf16) for _ in range(n_y)),
        (info, inputs, keys),
        2 * length * width * features,
        scalars=1,
        after=(both,),
    )
    both = swap(both, Y)
    both = both.reshape(n_y, n_z, 2 * D // n_z, D).transpose(1, 0, 2, 3)

    local, proj = call(
        local_kernel,
        (sds((length, width), f32), sds((heads, features, D), bf16)),
        (info, level_weight, queries, keys, out_grad, inputs),
        2 * length * width * features + 3 * length * length * width,
        [pltpu.VMEM((length, width), bf16)],
        scalars=2,
        after=(keyed[0], both),
    )
    both = swap(both, Z)
    keyed = [keyed[0]] + [shift(keyed[n], Y, n) for n in range(1, n_y)]
    proj = lax.psum_scatter(
        proj.reshape(heads * features, D), Y, scatter_dimension=0, tiled=True
    )

    both = call(
        tree_kernel,
        sds(both.shape, bf16),
        (info, level_weight, both),
        1 << 21,
        vmem=8,
        scalars=2,
        after=(local,),
    )
    both = swap(both, Z)

    parts, *own = call(
        project_kernel,
        (sds((n_z, features // n_z, D), bf16),) + tuple(sds((2 * D, D), bf16) for _ in range(n_y)),
        (info, *keyed, proj, both),
        2 * features * n_y * D * D,
        scalars=1,
    )
    parts = swap(parts, Z)

    own = [own[0]] + [shift(own[n], Y, n) for n in range(1, n_y)]
    query_grad, key_grad, value_grad = call(
        outputs_kernel,
        tuple(sds((length, width), bf16) for _ in range(3)),
        (info, level_weight, queries, keys, values, out_grad, local, *own),
        6 * length * length * width,
        scalars=2,
    )

    rows = momentum.shape[0]
    shard = call(
        shard_kernel,
        sds((n_y, rows + 8, D), f32),
        (parts,),
        1 << 20,
        vmem=8,
        after=(query_grad,),
    )
    shard = swap(shard, Y)
    rest = HEAD + (Z,)
    square = jnp.sum(shard[:, rows : rows + 1, :], axis=0, keepdims=True)
    total = swap(jnp.broadcast_to(square, (lax.axis_size(rest), 1, D)), rest)
    new_momentum = call(
        final_kernel, sds(momentum.shape, f32), (momentum, shard, total), 1 << 16, vmem=4
    )
    return (query_grad, key_grad, value_grad, new_momentum)


def solution(mesh):
    torus = Mesh(mesh.devices.reshape(4, 2, 4, 16), HEAD + SEQ)
    tokens = P(SEQ, HEAD)
    return jax.shard_map(
        body,
        mesh=torus,
        in_specs=(tokens, tokens, tokens, tokens, P(SEQ, None), tokens, P()),
        out_specs=(tokens, tokens, tokens, tokens),
        check_vma=False,
    )
```

time: 281 us -> 197 us (0.70)
  the two profiles are of different devices: /device:TPU:32 before, /device:TPU:1 now
where the time goes in v1:
time: 197 us; the launch traced here: 196 us
  blocking collectives  70.7 us (36%)
  starting transfers between devices  49.8 us (25%)
  waiting for transfers between devices  22.1 us (11%)
  local copies, waits for them, and re-layouts  20.5 us (10%)
  Pallas kernels  18.2 us (9%)
  between operations  14.2 us (7%)
    all_to_all x3, blocking collectives, swap(): return lax.all_to_all(x, axes, 0, 0, tiled=True)  70.7 us
    all_to_all x3, starting transfers between devices, swap(): return lax.all_to_all(x, axes, 0, 0, tiled=True)  26.4 us
    ppermute x6, starting transfers between devices, shift(): return lax.ppermute(x, axis, [(i, (i + by) % n) for i in range(n)])  23.4 us
    unnamed x54, local copies, waits for them, and re-layouts  20.4 us
    ppermute x6, waiting for transfers between devices, shift(): return lax.ppermute(x, axis, [(i, (i + by) % n) for i in range(n)])  19.8 us
    pallas_call x8, Pallas kernels, call(): pl.pallas_call(run, out_shape=out_shape, in_specs=[SMEM] * scalars + [VME...  18.2 us
  transfers between devices with their start and end apart: 10, of which 6 were waited for; matrix products, arithmetic and copies ran while one was open for 0% of the time, Pallas kernels for 5%

profile of v1, /device:TPU:1, one launch (start us, length us, event | category | flops | bytes accessed | tf_op | source)
XLA Modules:
  0.0 195.7 jit_solution(9569840980699419487)
XLA Ops:
  7.2 1.0 copy-done
  8.2 1.0 copy-done.2
  9.3 1.0 copy-done.4
  10.3 1.0 copy-done.6
  11.3 1.2 shard_map.102.refs_3_
  12.5 5.0 %all-to-all-start = ((bf16[4,256,128]{2,1,0:T(8,128)(2,1)}), bf16[4,256,128]{2,1,0:T(8,128)(2,1)S(1)}, u32[]{:S(2)}, u32[]{:S(2)}) async-start(bf16[4,256,128]{2,1,0:T(8,128)(2,1)} %shard_map.102.refs_3_), calls=%async_computation | async-start | bytes 524288 | tf_op jit(solution)/shard_map/all_to_all | solution.py:239
  17.6 0.1 pad_add_fusion.refs_0_
  17.6 1.6 copy-done.20
  19.2 1.8 shard_map.103
  21.1 0.8 copy-done.22
  21.9 0.8 copy-done.23
  22.7 0.8 copy-done.24
  23.5 1.6 copy-done.21
  25.1 5.6 %shard_map.104 = (f32[512,512]{1,0:T(8,128)S(1)}, bf16[4,2048,128]{2,1,0:T(8,128)(2,1)}) custom-call(s32[4]{0:T(128)S(1)} %pad_add_fusion.refs_0_, s32[18,32]{1,0:T(8,128)S(1)} %copy-done.19, bf16[512,512]{1,0:T(8,128)(2,1)S(1)} %copy-done.1, bf16[512,512]{1,0:T(8,128)(2,1)S(1)} %copy-done.3, bf16[512,512]{1,0:T(8,128)(2,1)S(1)} %copy-done.7, ...), custom_call_target="tpu_custom_call" | custom-call | flops 1476395008 | bytes 6818064 | tf_op jit(solution)/shard_map/pallas_call | solution.py:40
  30.7 27.5 %all_to_all.30.refs_2_ = bf16[16,4,16,128]{3,2,1,0:T(8,128)(2,1)S(1)} all-to-all(bf16[16,4,16,128]{3,2,1,0:T(8,128)(2,1)S(1)} %bitcast.9), channel_id=1, replica_groups=mesh['head_0'=4,'head_1'=2,'seq_0'=4,'seq_1'=16] {'seq_1'}, dimensions={0} | all-to-all | bytes 524288 | tf_op jit(solution)/shard_map/all_to_all | solution.py:239
  58.2 1.6 shard_map.105
  59.8 9.9 %all-to-all-start.2 = ((bf16[16,4,16,128]{3,2,1,0:T(8,128)(2,1)}), bf16[16,4,16,128]{3,2,1,0:T(8,128)(2,1)S(1)}, u32[]{:S(2)}, u32[]{:S(2)}) async-start(bf16[16,4,16,128]{3,2,1,0:T(8,128)(2,1)} %shard_map.105), calls=%async_computation.3 | async-start | bytes 524288 | tf_op jit(solution)/shard_map/all_to_all | solution.py:239
  69.8 4.6 %collective-permute-start = (bf16[2048,128]{1,0:T(8,128)(2,1)}, bf16[2048,128]{1,0:T(8,128)(2,1)S(1)}, u32[]{:S(2)}, u32[]{:S(2)}) collective-permute-start(bf16[2048,128]{1,0:T(8,128)(2,1)} %copy-done.24), channel_id=1, source_target_pairs={{0,16},{16,32},{32,48},{48,0},{1,17},{17,33},{33,49},{49,1},{2,18}... | collective-permute-start | bytes 1572872 | tf_op jit(solution)/shard_map/ppermute | solution.py:235
  74.4 4.3 %collective-permute-start.1 = (bf16[2048,128]{1,0:T(8,128)(2,1)}, bf16[2048,128]{1,0:T(8,128)(2,1)S(1)}, u32[]{:S(2)}, u32[]{:S(2)}) collective-permute-start(bf16[2048,128]{1,0:T(8,128)(2,1)} %copy-done.23), channel_id=1, source_target_pairs={{0,32},{16,48},{32,0},{48,16},{1,33},{17,49},{33,1},{49,17},{2,34}... | collective-permute-start | bytes 1572872 | tf_op jit(solution)/shard_map/ppermute | solution.py:235
  78.7 3.1 %collective-permute-start.2 = (bf16[2048,128]{1,0:T(8,128)(2,1)}, bf16[2048,128]{1,0:T(8,128)(2,1)S(1)}, u32[]{:S(2)}, u32[]{:S(2)}) collective-permute-start(bf16[2048,128]{1,0:T(8,128)(2,1)} %copy-done.22), channel_id=1, source_target_pairs={{0,48},{16,0},{32,16},{48,32},{1,49},{17,1},{33,17},{49,33},{2,50}... | collective-permute-start | bytes 1572872 | tf_op jit(solution)/shard_map/ppermute | solution.py:235
  81.8 4.7 %collective-permute-done.refs_2_ = bf16[2048,128]{1,0:T(8,128)(2,1)S(1)} collective-permute-done((bf16[2048,128]{1,0:T(8,128)(2,1)}, bf16[2048,128]{1,0:T(8,128)(2,1)S(1)}, u32[]{:S(2)}, u32[]{:S(2)}) %collective-permute-start) | collective-permute-done | bytes 524320 | tf_op jit(solution)/shard_map/ppermute | solution.py:235
  86.5 0.8 copy-done.12
  87.3 11.6 %collective-permute-done.1.refs_3_ = bf16[2048,128]{1,0:T(8,128)(2,1)S(1)} collective-permute-done((bf16[2048,128]{1,0:T(8,128)(2,1)}, bf16[2048,128]{1,0:T(8,128)(2,1)S(1)}, u32[]{:S(2)}, u32[]{:S(2)}) %collective-permute-start.1) | collective-permute-done | bytes 524320 | tf_op jit(solution)/shard_map/ppermute | solution.py:235
  98.9 0.8 copy-done.14
  99.7 1.3 collective-permute-done.2.refs_4_
  101.0 0.8 copy-done.16
  101.8 1.0 copy-done.11
  102.8 1.0 copy-done.13
  103.9 1.0 copy-done.15
  104.9 1.0 copy-done.17
  106.0 1.3 shard_map.106
  107.3 0.8 copy-done.9
  108.1 0.6 copy-done.25
  108.7 0.6 copy-done.26
  109.3 11.5 %all-to-all-start.3 = ((bf16[16,128,128]{2,1,0:T(8,128)(2,1)}), bf16[16,128,128]{2,1,0:T(8,128)(2,1)S(1)}, u32[]{:S(2)}, u32[]{:S(2)}) async-start(bf16[16,128,128]{2,1,0:T(8,128)(2,1)} %copy-done.9), calls=%async_computation.4 | async-start | bytes 1048576 | tf_op jit(solution)/shard_map/all_to_all | solution.py:239
  120.8 5.2 %collective-permute-start.3 = (bf16[256,128]{1,0:T(8,128)(2,1)}, bf16[256,128]{1,0:T(8,128)(2,1)S(1)}, u32[]{:S(2)}, u32[]{:S(2)}) collective-permute-start(bf16[256,128]{1,0:T(8,128)(2,1)} %copy-done.26), channel_id=1, source_target_pairs={{0,16},{16,32},{32,48},{48,0},{1,17},{17,33},{33,49},{49,1},{2,18}... | collective-permute-start | bytes 196616 | tf_op jit(solution)/shard_map/ppermute | solution.py:235
  126.0 3.1 %collective-permute-start.4 = (bf16[256,128]{1,0:T(8,128)(2,1)}, bf16[256,128]{1,0:T(8,128)(2,1)S(1)}, u32[]{:S(2)}, u32[]{:S(2)}) collective-permute-start(bf16[256,128]{1,0:T(8,128)(2,1)} %copy-done.25), channel_id=1, source_target_pairs={{0,32},{16,48},{32,0},{48,16},{1,33},{17,49},{33,1},{49,17},{2,34}... | collective-permute-start | bytes 196616 | tf_op jit(solution)/shard_map/ppermute | solution.py:235
  129.1 3.1 %collective-permute-start.5 = (bf16[256,128]{1,0:T(8,128)(2,1)S(1)}, bf16[256,128]{1,0:T(8,128)(2,1)S(1)}, u32[]{:S(2)}, u32[]{:S(2)}) collective-permute-start(bf16[256,128]{1,0:T(8,128)(2,1)S(1)} %get-tuple-element.27), channel_id=1, source_target_pairs={{0,48},{16,0},{32,16},{48,32},{1,49},{17,1},{33,17},{49,33},{2,50}... | collective-permute-start | bytes 196616 | tf_op jit(solution)/shard_map/ppermute | solution.py:235
  132.2 0.8 collective-permute-done.4.refs_9_
  133.0 1.4 collective-permute-done.5.refs_10_
  134.4 1.0 copy-done.8
  135.5 5.8 %shard_map.107 = (bf16[512,512]{1,0:T(8,128)(2,1)}, bf16[512,512]{1,0:T(8,128)(2,1)}, bf16[512,512]{1,0:T(8,128)(2,1)}) custom-call(s32[4]{0:T(128)S(1)} %pad_add_fusion.refs_0_, s32[18,32]{1,0:T(8,128)S(1)} %copy-done.19, bf16[512,512]{1,0:T(8,128)(2,1)S(1)} %copy-done.1, bf16[512,512]{1,0:T(8,128)(2,1)S(1)} %copy-done.3, bf16[512,512]{1,0:T(8,128)(2,1)S(1)} %copy-done.5, ...), custom_call_target="tpu_custom_call" | custom-call | flops 805306368 | bytes 4983056 | tf_op jit(solution)/shard_map/pallas_call | solution.py:40
  141.2 2.3 %all-to-all-done.3.refs_0_ = bf16[16,128,128]{2,1,0:T(8,128)(2,1)S(1)} async-done(((bf16[16,128,128]{2,1,0:T(8,128)(2,1)}), bf16[16,128,128]{2,1,0:T(8,128)(2,1)S(1)}, u32[]{:S(2)}, u32[]{:S(2)}) %all-to-all-start.3) | async-done | bytes 524320 | tf_op jit(solution)/shard_map/all_to_all | solution.py:239
  143.5 1.0 copy-done.10
  144.5 0.2 shard_map.108
  144.7 9.0 %all_to_all.31.refs_1_ = f32[4,40,128]{2,1,0:T(8,128)S(1)} all-to-all(f32[4,40,128]{2,1,0:T(8,128)S(1)} %shard_map.108), channel_id=1, replica_groups=mesh['head_0'=4,'head_1'=2,'seq_0'=4,'seq_1'=16] {'seq_0'}, dimensions={0} | all-to-all | bytes 163840 | tf_op jit(solution)/shard_map/all_to_all | solution.py:239
  153.8 34.2 %all_to_all.32.refs_2_ = f32[128,1,128]{2,1,0:T(1,128)S(1)} all-to-all(f32[128,1,128]{2,1,0:T(1,128)S(1)} %broadcast_in_dim.2), channel_id=1, replica_groups=mesh['head_0'=4,'head_1'=2,'seq_0'=4,'seq_1'=16] {'head_0','head_1','seq..., dimensions={0} | all-to-all | bytes 131072 | tf_op jit(solution)/shard_map/all_to_all | solution.py:239
  188.0 0.8 shard_map.109
  (42 shorter events, 0.2 us)
Async XLA Ops:
  7.2 1.0 copy-start
  8.2 1.0 copy-start.2
  9.3 1.0 copy-start.4
  10.3 1.0 copy-start.6
  11.3 6.3 %copy-start.3 = (bf16[512,512]{1,0:T(8,128)(2,1)S(1)}, bf16[512,512]{1,0:T(8,128)(2,1)}, u32[]{:S(2)}) copy-start(bf16[512,512]{1,0:T(8,128)(2,1)} %refs_3_.5) | copy-start | bytes 1572868
  12.5 10.9 %all-to-all-start = ((bf16[4,256,128]{2,1,0:T(8,128)(2,1)}), bf16[4,256,128]{2,1,0:T(8,128)(2,1)S(1)}, u32[]{:S(2)}, u32[]{:S(2)}) async-start(bf16[4,256,128]{2,1,0:T(8,128)(2,1)} %shard_map.102.refs_3_), calls=%async_computation | async-start | bytes 524288 | tf_op jit(solution)/shard_map/all_to_all | solution.py:239
  17.6 84.3 %reduce-scatter.2.cloned.1.call-start = ((), (), s32[]{:S(2)}) async-start(), calls=%async_computation.7 | async-start | bytes 2621440 | tf_op jit(solution)/shard_map/reduce_scatter | solution.py:280
  17.6 1.6 copy-start.20
  19.2 4.3 %copy-start.1 = (bf16[512,512]{1,0:T(8,128)(2,1)S(1)}, bf16[512,512]{1,0:T(8,128)(2,1)}, u32[]{:S(2)}) copy-start(bf16[512,512]{1,0:T(8,128)(2,1)} %refs_2_.7) | copy-start | bytes 1572868
  19.2 4.3 %copy-start.7 = (bf16[512,512]{1,0:T(8,128)(2,1)S(1)}, bf16[512,512]{1,0:T(8,128)(2,1)}, u32[]{:S(2)}) copy-start(bf16[512,512]{1,0:T(8,128)(2,1)} %refs_5_.3) | copy-start | bytes 1572868
  19.2 4.3 %copy-start.19 = (s32[18,32]{1,0:T(8,128)S(1)}, s32[18,32]{1,0:T(8,128)}, u32[]{:S(2)}) copy-start(s32[18,32]{1,0:T(8,128)} %refs_1_.9) | copy-start | bytes 6916
  21.1 0.8 copy-start.22
  21.9 0.8 copy-start.23
  22.7 0.8 copy-start.24
  23.5 1.6 copy-start.21
  59.8 42.0 %all-to-all-start.2 = ((bf16[16,4,16,128]{3,2,1,0:T(8,128)(2,1)}), bf16[16,4,16,128]{3,2,1,0:T(8,128)(2,1)S(1)}, u32[]{:S(2)}, u32[]{:S(2)}) async-start(bf16[16,4,16,128]{3,2,1,0:T(8,128)(2,1)} %shard_map.105), calls=%async_computation.3 | async-start | bytes 524288 | tf_op jit(solution)/shard_map/all_to_all | solution.py:239
  69.7 64.7 %copy-start.5 = (bf16[512,512]{1,0:T(8,128)(2,1)S(1)}, bf16[512,512]{1,0:T(8,128)(2,1)}, u32[]{:S(2)}) copy-start(bf16[512,512]{1,0:T(8,128)(2,1)} %refs_4_.3) | copy-start | bytes 1572868
  69.8 16.8 %collective-permute-start = (bf16[2048,128]{1,0:T(8,128)(2,1)}, bf16[2048,128]{1,0:T(8,128)(2,1)S(1)}, u32[]{:S(2)}, u32[]{:S(2)}) collective-permute-start(bf16[2048,128]{1,0:T(8,128)(2,1)} %copy-done.24), channel_id=1, source_target_pairs={{0,16},{16,32},{32,48},{48,0},{1,17},{17,33},{33,49},{49,1},{2,18}... | collective-permute-start | bytes 1572872 | tf_op jit(solution)/shard_map/ppermute | solution.py:235
  74.4 24.5 %collective-permute-start.1 = (bf16[2048,128]{1,0:T(8,128)(2,1)}, bf16[2048,128]{1,0:T(8,128)(2,1)S(1)}, u32[]{:S(2)}, u32[]{:S(2)}) collective-permute-start(bf16[2048,128]{1,0:T(8,128)(2,1)} %copy-done.23), channel_id=1, source_target_pairs={{0,32},{16,48},{32,0},{48,16},{1,33},{17,49},{33,1},{49,17},{2,34}... | collective-permute-start | bytes 1572872 | tf_op jit(solution)/shard_map/ppermute | solution.py:235
  78.7 22.3 %collective-permute-start.2 = (bf16[2048,128]{1,0:T(8,128)(2,1)}, bf16[2048,128]{1,0:T(8,128)(2,1)S(1)}, u32[]{:S(2)}, u32[]{:S(2)}) collective-permute-start(bf16[2048,128]{1,0:T(8,128)(2,1)} %copy-done.22), channel_id=1, source_target_pairs={{0,48},{16,0},{32,16},{48,32},{1,49},{17,1},{33,17},{49,33},{2,50}... | collective-permute-start | bytes 1572872 | tf_op jit(solution)/shard_map/ppermute | solution.py:235
  86.5 0.8 copy-start.12
  98.9 0.8 copy-start.14
  101.0 0.8 copy-start.16
  101.8 1.0 copy-start.11
  102.8 1.0 copy-start.13
  103.9 1.0 copy-start.15
  104.9 1.0 copy-start.17
  107.3 0.8 copy-start.9
  108.1 0.6 copy-start.25
  108.7 0.6 copy-start.26
  109.3 34.2 %all-to-all-start.3 = ((bf16[16,128,128]{2,1,0:T(8,128)(2,1)}), bf16[16,128,128]{2,1,0:T(8,128)(2,1)S(1)}, u32[]{:S(2)}, u32[]{:S(2)}) async-start(bf16[16,128,128]{2,1,0:T(8,128)(2,1)} %copy-done.9), calls=%async_computation.4 | async-start | bytes 1048576 | tf_op jit(solution)/shard_map/all_to_all | solution.py:239
  120.8 11.4 %collective-permute-start.3 = (bf16[256,128]{1,0:T(8,128)(2,1)}, bf16[256,128]{1,0:T(8,128)(2,1)S(1)}, u32[]{:S(2)}, u32[]{:S(2)}) collective-permute-start(bf16[256,128]{1,0:T(8,128)(2,1)} %copy-done.26), channel_id=1, source_target_pairs={{0,16},{16,32},{32,48},{48,0},{1,17},{17,33},{33,49},{49,1},{2,18}... | collective-permute-start | bytes 196616 | tf_op jit(solution)/shard_map/ppermute | solution.py:235
  126.0 7.0 %collective-permute-start.4 = (bf16[256,128]{1,0:T(8,128)(2,1)}, bf16[256,128]{1,0:T(8,128)(2,1)S(1)}, u32[]{:S(2)}, u32[]{:S(2)}) collective-permute-start(bf16[256,128]{1,0:T(8,128)(2,1)} %copy-done.25), channel_id=1, source_target_pairs={{0,32},{16,48},{32,0},{48,16},{1,33},{17,49},{33,1},{49,17},{2,34}... | collective-permute-start | bytes 196616 | tf_op jit(solution)/shard_map/ppermute | solution.py:235
  129.1 5.3 %collective-permute-start.5 = (bf16[256,128]{1,0:T(8,128)(2,1)S(1)}, bf16[256,128]{1,0:T(8,128)(2,1)S(1)}, u32[]{:S(2)}, u32[]{:S(2)}) collective-permute-start(bf16[256,128]{1,0:T(8,128)(2,1)S(1)} %get-tuple-element.27), channel_id=1, source_target_pairs={{0,48},{16,0},{32,16},{48,32},{1,49},{17,1},{33,17},{49,33},{2,50}... | collective-permute-start | bytes 196616 | tf_op jit(solution)/shard_map/ppermute | solution.py:235
  134.4 1.0 copy-start.8
  135.5 52.6 %copy-start.18 = (f32[32,512]{1,0:T(8,128)S(1)}, f32[32,512]{1,0:T(8,128)}, u32[]{:S(2)}) copy-start(f32[32,512]{1,0:T(8,128)} %refs_0_.3) | copy-start | bytes 196612
  143.5 1.0 copy-start.10
Sparse Core Ops, SparseCore 0:
  30.8 42.4 reduce-scatter.1

commit v2 on v1

v2 whole, which is shorter than its diff:
```python
import functools
import math

import jax
import jax.numpy as jnp
import numpy as np
from jax import lax
from jax.experimental import pallas as pl
from jax.experimental.pallas import tpu as pltpu
from jax.sharding import Mesh
from jax.sharding import PartitionSpec as P

D = 128
HEAD = ("head_0", "head_1")
Y = "seq_0"
Z = "seq_1"
SEQ = (Y, Z)

clip_norm = 1024.0
momentum_rate = 0.9

bf16 = jnp.bfloat16
f32 = jnp.float32


def dot(a, b, ca, cb):
    return lax.dot_general(a, b, (((ca,), (cb,)), ((), ())), preferred_element_type=f32)


def spec(block, index):
    return pl.BlockSpec(block, index)


def call(kernel, out_shape, operands, flops, in_specs=None, out_specs=None, grid=(1,), scratch=(), vmem=60, after=(), scalars=(), gated=()):
    leaves = jax.tree.leaves((operands, out_shape))
    n = len(scalars) + len(operands)
    skip = n + len(after) + len(gated)
    last = skip + len(jax.tree.leaves(out_shape))

    def run(*refs):
        kernel(*refs[:n], *refs[skip:last], *refs[last + len(gated) :])

    def whole(x):
        return spec(x.shape, lambda *_: (0,) * len(x.shape))

    in_specs = list(in_specs or [None] * len(operands))
    in_specs = [whole(x) if i is None else i for x, i in zip(operands, in_specs)]
    if out_specs is None:
        out_specs = jax.tree.map(whole, out_shape)
    anywhere = pl.BlockSpec(memory_space=pl.ANY)
    aliases = {}
    if gated:
        first = len(jax.tree.leaves(out_shape))
        aliases = {n + len(after) + i: first + i for i in range(len(gated))}
        out_shape = (*jax.tree.leaves(out_shape), *(jax.ShapeDtypeStruct(x.shape, x.dtype) for x in gated))
        out_specs = (*jax.tree.leaves(out_specs), *(anywhere for _ in gated))
    return pl.pallas_call(
        run,
        out_shape=out_shape,
        grid_spec=pltpu.PrefetchScalarGridSpec(
            num_scalar_prefetch=len(scalars),
            grid=grid,
            in_specs=in_specs + [anywhere] * (len(after) + len(gated)),
            out_specs=out_specs,
            scratch_shapes=list(scratch),
        ),
        input_output_aliases=aliases,
        compiler_params=pltpu.CompilerParams(vmem_limit_bytes=vmem * 1024 * 1024),
        cost_estimate=pl.CostEstimate(
            flops=flops,
            bytes_accessed=sum(x.size * x.dtype.itemsize for x in leaves),
            transcendentals=0,
        ),
    )(*scalars, *operands, *after, *gated)


def lanes(block):
    if isinstance(block, int):
        return slice(block * D, (block + 1) * D)
    return pl.ds(pl.multiple_of(block * D, D), D)


def lam(level, head, weight_ref):
    factor = np.float32(2.0 ** (-0.5 * level) / (8.0 * math.sqrt(D)))
    return weight_ref[level, head].astype(f32) * factor


def diagonal(head, weight_ref, transposed):
    row = lax.broadcasted_iota(jnp.int32, (D, D), 0)
    col = lax.broadcasted_iota(jnp.int32, (D, D), 1)
    apart = jnp.bitwise_xor(row, col)
    out = jnp.full((D, D), lam(0, head, weight_ref), f32)
    for level in range(1, D.bit_length()):
        out = jnp.where(apart >= 1 << (level - 1), lam(level, head, weight_ref), out)
    keep = row <= col if transposed else col <= row
    return jnp.where(keep, out, f32(0.0))


def far(i, j, head, weight_ref):
    return lam(D.bit_length() - 1 + (i ^ j).bit_length(), head, weight_ref)


def weighted(scores, first, own, head, weight_ref, diag):
    count = scores.shape[1] // D
    parts = []
    for n in range(count):
        part = scores[:, n * D : (n + 1) * D]
        w = diag if first + n == own else far(first + n, own, head, weight_ref)
        parts.append((w * part).astype(bf16))
    return parts[0] if count == 1 else jnp.concatenate(parts, axis=1)


def states_kernel(q_ref, k_ref, v_ref, g_ref, out_ref):
    out_ref[0, :D, :] = dot(q_ref[...], g_ref[...], 0, 0).astype(bf16)
    out_ref[0, D:, :] = dot(k_ref[...], v_ref[...], 0, 0).astype(bf16)


def local_kernel(info_ref, weight_ref, q_ref, k_ref, g_ref, out_ref):
    blocks = q_ref.shape[0] // D
    head = info_ref[0] * pl.num_programs(0) + pl.program_id(0)
    diag = diagonal(head, weight_ref, True)
    for j in range(blocks):
        rows = slice(j * D, (j + 1) * D)
        scores = dot(k_ref[rows, :], q_ref[j * D :, :], 1, 1)
        mixed = weighted(scores, j, j, head, weight_ref, diag)
        out_ref[rows, :] = dot(mixed, g_ref[j * D :, :], 1, 0)


def keyed_kernel(info_ref, x_ref, k_ref, loc_ref, proj_ref, *out_refs):
    y = info_ref[1]
    n_out = len(out_refs)
    heads = [lanes(lax.rem(y + n, n_out)) for n in range(n_out)]
    right = jnp.concatenate([k_ref[:, s] for s in heads] + [loc_ref[...].astype(bf16)], axis=1)
    res = dot(x_ref[...], right, 0, 0).astype(bf16)
    for n in range(n_out):
        out_refs[n][...] = res[:, lanes(n)]
        proj_ref[n, :, :] = res[:, lanes(n_out + n)]


def turn_kernel(in_ref, out_ref):
    each = out_ref.shape[2]
    for z in range(out_ref.shape[0]):
        for y in range(out_ref.shape[1]):
            out_ref[z, y, :, :] = in_ref[y, z * each : (z + 1) * each, :]


def tree_kernel(info_ref, weight_ref, in_ref, out_ref):
    nz, ny = in_ref.shape[:2]
    count = nz * ny
    depth = count.bit_length() - 1
    head = info_ref[0] * ny + info_ref[1]
    is_grad = info_ref[2] < nz // 2
    sums = [[in_ref[c % nz, c // nz].astype(f32) for c in range(count)]]
    for bit in range(depth - 1):
        last = sums[-1]
        sums.append([last[2 * b] + last[2 * b + 1] for b in range(len(last) // 2)])
    total = [jnp.zeros(in_ref.shape[2:], f32)]
    for bit in reversed(range(depth)):
        w = lam(D.bit_length() + 2 + bit, head, weight_ref)
        later = jnp.where(is_grad, w, f32(0.0))
        earlier = jnp.where(is_grad, f32(0.0), w)
        last = sums[bit]
        total = [
            total[b // 2] + (later * last[b + 1] if b % 2 == 0 else earlier * last[b - 1])
            for b in range(len(last))
        ]
    for c in range(count):
        out_ref[c % nz, c // nz] = total[c].astype(bf16)


def project_kernel(info_ref, a0, a1, a2, a3, loc_ref, r_ref, out_ref, *own_refs):
    y = info_ref[1]
    keyed = (a0, a1, a2, a3)
    n_y = len(keyed)
    half = r_ref.shape[0] // 2
    nz, each = out_ref.shape[:2]

    @pl.when(pl.program_id(0) == 0)
    def _():
        for n in range(n_y):
            own_refs[n][...] = r_ref[:, lax.rem(y + n, n_y)].reshape(2 * D, D)

    states = [r_ref[:half, lax.rem(y + n_y - n, n_y)].reshape(D, D) for n in range(n_y)]
    left = jnp.concatenate([a[...] for a in keyed], axis=1)
    res = loc_ref[...].astype(f32) + dot(left, jnp.concatenate(states, axis=0), 1, 0)
    res = res.astype(bf16)
    for z in range(nz):
        out_ref[z, :, :] = res[z * each : (z + 1) * each, :]


def outputs_kernel(
    info_ref, weight_ref, q_ref, k_ref, v_ref, g_ref, loc_ref, r0, r1, r2, r3, dq_ref, dk_ref, dv_ref, r_ref
):
    n = pl.program_id(0)
    n_y = pl.num_programs(0)
    for i, r in enumerate((r0, r1, r2, r3)):

        @pl.when(n == i)
        def _():
            r_ref[...] = r[...]

    blocks = q_ref.shape[0] // D
    head = info_ref[0] * n_y + lax.rem(info_ref[1] + n_y - n, n_y)
    returned = r_ref[:D, :]
    carried = r_ref[D:, :]
    query, keys, values, grad = q_ref[...], k_ref[...], v_ref[...], g_ref[...]
    dv_ref[...] = (loc_ref[...] + dot(keys, returned, 1, 0)).astype(bf16)
    base_k = dot(values, returned, 1, 1)
    base_q = dot(grad, carried, 1, 1)
    diag = diagonal(head, weight_ref, False)
    diag_t = diagonal(head, weight_ref, True)
    for i in range(blocks):
        rows = slice(i * D, (i + 1) * D)
        upto = (i + 1) * D
        before = dot(grad[rows], values[:upto], 1, 1)
        dmix = weighted(before, 0, i, head, weight_ref, diag)
        dq_ref[rows, :] = (base_q[rows] + dot(dmix, keys[:upto], 1, 0)).astype(bf16)
        later = dot(values[rows], grad[i * D :], 1, 1)
        dmix_t = weighted(later, i, i, head, weight_ref, diag_t)
        dk_ref[rows, :] = (base_k[rows] + dot(dmix_t, query[i * D :], 1, 0)).astype(bf16)


def shard_kernel(in_ref, out_ref, square_ref):
    total = in_ref[0].astype(f32)
    for z in range(1, in_ref.shape[0]):
        total = total + in_ref[z].astype(f32)
    out_ref[...] = total
    square = jnp.sum(jnp.sum(total * total, axis=0, keepdims=True), axis=1, keepdims=True)
    square_ref[...] = jnp.broadcast_to(square[None], square_ref.shape)


def stage_kernel(info_ref, square_ref, shard_ref, out_ref, *part_refs):
    n_y = len(part_refs)
    rows = part_refs[0].shape[0]
    square = jnp.sum(square_ref[...], axis=0, keepdims=True)
    out_ref[...] = jnp.broadcast_to(square, out_ref.shape)
    for n in range(n_y):
        first = pl.multiple_of(lax.rem(info_ref[1] + n, n_y) * rows, rows)
        part_refs[n][...] = shard_ref[pl.ds(first, rows), :]


def final_kernel(info_ref, mom_ref, p0, p1, p2, p3, total_ref, out_ref):
    parts = (p0, p1, p2, p3)
    n_y = len(parts)
    total = jnp.sum(total_ref[...], axis=0)
    factor = jnp.minimum(f32(1.0), clip_norm / jnp.sqrt(total + 1e-06))
    for n in range(n_y):
        s = lanes(lax.rem(info_ref[1] + n_y - n, n_y))
        out_ref[:, s] = momentum_rate * mom_ref[:, s] + factor * parts[n][...]


def shift(x, axis, by):
    n = lax.axis_size(axis)
    return lax.ppermute(x, axis, [(i, (i + by) % n) for i in range(n)])


def swap(x, axes):
    return lax.all_to_all(x, axes, 0, 0, tiled=True)


def body(queries, keys, values, out_grad, inputs, momentum, level_weight):
    length, width = queries.shape
    features = inputs.shape[1]
    n_y, n_z = lax.axis_size(Y), lax.axis_size(Z)
    heads = width // D
    sds = jax.ShapeDtypeStruct
    info = jnp.stack(
        [lax.axis_index(HEAD), lax.axis_index(Y), lax.axis_index(Z), jnp.int32(0)]
    ).astype(jnp.int32)

    column = spec((length, D), lambda h, *_: (0, h))
    both = call(
        states_kernel,
        sds((heads, 2 * D, D), bf16),
        (queries, keys, values, out_grad),
        4 * length * width * D,
        [column] * 4,
        spec((1, 2 * D, D), lambda h: (h, 0, 0)),
        (heads,),
    )
    local = call(
        local_kernel,
        sds((length, width), f32),
        (queries, keys, out_grad),
        3 * length * length * width,
        [column] * 3,
        column,
        (heads,),
        scalars=(info, level_weight),
        after=(both,),
    )
    block = 512
    steps = features // block
    proj, *keyed = call(
        keyed_kernel,
        (sds((heads, features, D), bf16),) + tuple(sds((features, D), bf16) for _ in range(n_y)),
        (inputs, keys, local),
        4 * length * width * features,
        [spec((length, block), lambda c, *_: (0, c)), None, None],
        (spec((heads, block, D), lambda c, *_: (0, c, 0)),)
        + (spec((block, D), lambda c, *_: (c, 0)),) * n_y,
        (steps,),
        scalars=(info,),
    )
    both, proj, *keyed[1:] = call(
        turn_kernel,
        sds((n_z, n_y, 2 * D // n_z, D), bf16),
        (swap(both, Y),),
        1 << 16,
        gated=(proj, *keyed[1:]),
    )
    both = swap(both, Z)
    keyed = [keyed[0]] + [shift(keyed[n], Y, n) for n in range(1, n_y)]
    proj = lax.psum_scatter(
        proj.reshape(heads * features, D), Y, scatter_dimension=0, tiled=True
    )

    both = call(
        tree_kernel,
        sds(both.shape, bf16),
        (both,),
        1 << 21,
        scalars=(info, level_weight),
        after=keyed[1:],
        vmem=8,
    )
    both = swap(both, Z)

    row = spec((features // n_y, D), lambda b, *_: (b, 0))
    each = features // n_z // n_y
    parts, *own = call(
        project_kernel,
        (sds((n_z, features // n_z, D), bf16),) + tuple(sds((2 * D, D), bf16) for _ in range(n_y)),
        (*keyed, proj, both),
        2 * features * n_y * D * D,
        [row] * (n_y + 1) + [None],
        (spec((n_z, each, D), lambda b, *_: (0, b, 0)),)
        + (spec((2 * D, D), lambda b, *_: (0, 0)),) * n_y,
        (n_y,),
        scalars=(info,),
    )
    parts = swap(parts, Z)

    own = [own[0]] + [shift(own[n], Y, n) for n in range(1, n_y)]
    turned = spec((length, D), lambda n, info_ref, _: (0, lax.rem(info_ref[1] + n_y - n, n_y)))
    query_grad, key_grad, value_grad = call(
        outputs_kernel,
        tuple(sds((length, width), bf16) for _ in range(3)),
        (queries, keys, values, out_grad, local, *own),
        6 * length * length * width,
        [turned] * 5 + [None] * n_y,
        (turned,) * 3,
        (n_y,),
        [pltpu.VMEM((2 * D, D), bf16)],
        scalars=(info, level_weight),
    )

    near, rest = HEAD + (Y,), (Z,)
    rows = momentum.shape[0]
    shard, square = call(
        shard_kernel,
        (sds((n_y * rows, D), f32), sds((lax.axis_size(near), 1, D), f32)),
        (parts,),
        1 << 20,
        after=(query_grad,),
        vmem=8,
    )
    square = swap(square, near)
    total, *mine = call(
        stage_kernel,
        (sds((lax.axis_size(rest), 1, D), f32),) + tuple(sds((rows, D), f32) for _ in range(n_y)),
        (square, shard),
        1 << 16,
        scalars=(info,),
        vmem=8,
    )
    total = swap(total, rest)
    mine = [mine[0]] + [shift(mine[n], Y, n) for n in range(1, n_y)]
    new_momentum = call(
        final_kernel,
        sds(momentum.shape, f32),
        (momentum, *mine, total),
        1 << 16,
        scalars=(info,),
        vmem=8,
    )
    return (query_grad, key_grad, value_grad, new_momentum)


def solution(mesh):
    torus = Mesh(mesh.devices.reshape(4, 2, 4, 16), HEAD + SEQ)
    tokens = P(SEQ, HEAD)
    return jax.shard_map(
        body,
        mesh=torus,
        in_specs=(tokens, tokens, tokens, tokens, P(SEQ, None), tokens, P()),
        out_specs=(tokens, tokens, tokens, tokens),
        check_vma=False,
    )
```

time: 197 us -> 208 us (1.056)
  blocking collectives: 70.7 us -> 45.5 us
  starting transfers between devices: 49.8 us -> 68.4 us
  local copies, waits for them, and re-layouts: 20.5 us -> 2.4 us
  waiting for transfers between devices: 22.1 us -> 40.2 us
  Pallas kernels: 18.2 us -> 35.2 us
    all_to_all x3 -> x2, blocking collectives: 70.7 us -> 45.5 us  [swap(): return lax.all_to_all(x, axes, 0, 0, tiled=True)]
    ppermute x6 -> x9, waiting for transfers between devices: 19.8 us -> 39.6 us  [shift(): return lax.ppermute(x, axis, [(i, (i + by) % n) for i in range(n)])]
    unnamed x54 -> x30, local copies, waits for them, and re-layouts: 20.4 us -> 2.4 us
    pallas_call x8 -> x10, Pallas kernels: 18.2 us -> 35.2 us  [call(): pl.pallas_call(run, out_shape=out_shape, grid_spec=pltpu.PrefetchScalarGr...]
    all_to_all x3 -> x4, starting transfers between devices: 26.4 us -> 36.5 us  [swap(): return lax.all_to_all(x, axes, 0, 0, tiled=True)]
    ppermute x6 -> x9, starting transfers between devices: 23.4 us -> 31.9 us  [shift(): return lax.ppermute(x, axis, [(i, (i + by) % n) for i in range(n)])]
  transfers between devices with their start and end apart: 10 -> 14, of which waited for: 6 -> 6; matrix products, arithmetic and copies ran while one was open for 0% -> 0% of each run, Pallas kernels for 5% -> 10%
where the time goes in v2:
time: 208 us; the launch traced here: 207 us
  starting transfers between devices  68.4 us (33%)
  blocking collectives  45.5 us (22%)
  waiting for transfers between devices  40.2 us (19%)
  Pallas kernels  35.2 us (17%)
  between operations  14.3 us (7%)
  local copies, waits for them, and re-layouts  2.4 us (1%)
    all_to_all x2, blocking collectives, swap(): return lax.all_to_all(x, axes, 0, 0, tiled=True)  45.5 us
    ppermute x9, waiting for transfers between devices, shift(): return lax.ppermute(x, axis, [(i, (i + by) % n) for i in range(n)])  39.6 us
    all_to_all x4, starting transfers between devices, swap(): return lax.all_to_all(x, axes, 0, 0, tiled=True)  36.5 us
    pallas_call x10, Pallas kernels, call(): pl.pallas_call(run, out_shape=out_shape, grid_spec=pltpu.PrefetchScalarGr...  35.2 us
    ppermute x9, starting transfers between devices, shift(): return lax.ppermute(x, axis, [(i, (i + by) % n) for i in range(n)])  31.9 us
  transfers between devices with their start and end apart: 14, of which 6 were waited for; matrix products, arithmetic and copies ran while one was open for 0% of the time, Pallas kernels for 10%

profile of v2, /device:TPU:1, one launch (start us, length us, event | category | flops | bytes accessed | tf_op | source)
XLA Modules:
  0.0 206.6 jit_solution(11720788858728817173)
XLA Ops:
  7.2 4.0 %shard_map.102.refs_5_ = bf16[4,256,128]{2,1,0:T(8,128)(2,1)} custom-call(bf16[512,512]{1,0:T(8,128)(2,1)} %refs_2_.7, bf16[512,512]{1,0:T(8,128)(2,1)} %refs_3_.5, bf16[512,512]{1,0:T(8,128)(2,1)} %refs_4_.3, bf16[512,512]{1,0:T(8,128)(2,1)} %refs_5_.1), custom_call_target="tpu_custom_call" | custom-call | flops 134217728 | bytes 2359296 | tf_op jit(solution)/shard_map/pallas_call | solution.py:57
  11.2 5.0 %all-to-all-start = ((bf16[4,256,128]{2,1,0:T(8,128)(2,1)}), bf16[4,256,128]{2,1,0:T(8,128)(2,1)S(1)}, u32[]{:S(2)}, u32[]{:S(2)}) async-start(bf16[4,256,128]{2,1,0:T(8,128)(2,1)} %shard_map.102.refs_5_), calls=%async_computation | async-start | bytes 524288 | tf_op jit(solution)/shard_map/all_to_all | solution.py:258
  16.2 0.0 reduce-scatter.2.cloned.1.call-start
  16.2 0.6 pad_add_fusion.refs_0_
  16.8 6.2 %shard_map.103.refs_3_.refs_6_ = f32[512,512]{1,0:T(8,128)} custom-call(s32[4]{0:T(128)} %pad_add_fusion.refs_0_, s32[18,32]{1,0:T(8,128)} %refs_1_.10, bf16[512,512]{1,0:T(8,128)(2,1)} %refs_2_.7, bf16[512,512]{1,0:T(8,128)(2,1)} %refs_3_.5, bf16[512,512]{1,0:T(8,128)(2,1)} %refs_5_.1, bf16[4,256,128]{2,1,0:T(8,128)(2,1)} %shard_map.102.refs_5_), custom_call_target="tpu_custom_call" | custom-call | flops 402653184 | bytes 2621440 | tf_op jit(solution)/shard_map/pallas_call | solution.py:57
  23.0 7.0 %shard_map.104 = (bf16[4,2048,128]{2,1,0:T(8,128)(2,1)}, bf16[2048,128]{1,0:T(8,128)(2,1)}, bf16[2048,128]{1,0:T(8,128)(2,1)}, bf16[2048,128]{1,0:T(8,128)(2,1)}, bf16[2048,128]{1,0:T(8,128)(2,1)}) custom-call(s32[4]{0:T(128)} %pad_add_fusion.refs_0_, bf16[512,2048]{1,0:T(8,128)(2,1)} %refs_1_.8, bf16[512,512]{1,0:T(8,128)(2,1)} %refs_3_.5, ...), custom_call_target="tpu_custom_call" | custom-call | flops 2147483648 | bytes 7864320 | tf_op jit(solution)/shard_map/pallas_call | solution.py:57
  29.9 0.0 all-to-all-done.refs_0_
  29.9 0.7 copy-done.8
  30.6 1.7 shard_map.105
  32.3 0.0 copy-start.6
  32.3 0.0 reduce-scatter.2.cloned.1.call-update
  32.4 15.1 %all-to-all-start.1 = ((bf16[16,4,16,128]{3,2,1,0:T(8,128)(2,1)}), bf16[16,4,16,128]{3,2,1,0:T(8,128)(2,1)S(1)}, u32[]{:S(2)}, u32[]{:S(2)}) async-start(bf16[16,4,16,128]{3,2,1,0:T(8,128)(2,1)} %get-tuple-element.38), calls=%async_computation.2 | async-start | bytes 524288 | tf_op jit(solution)/shard_map/all_to_all | solution.py:258
  47.4 0.0 copy-done.9
  47.4 3.3 %collective-permute-start = (bf16[2048,128]{1,0:T(8,128)(2,1)S(1)}, bf16[2048,128]{1,0:T(8,128)(2,1)S(1)}, u32[]{:S(2)}, u32[]{:S(2)}) collective-permute-start(bf16[2048,128]{1,0:T(8,128)(2,1)S(1)} %copy-done.9), channel_id=1, source_target_pairs={{0,16},{16,32},{32,48},{48,0},{1,17},{17,33},{33,49},{49,1},{2,18}... | collective-permute-start | bytes 1572872 | tf_op jit(solution)/shard_map/ppermute | solution.py:254
  50.8 4.3 %collective-permute-start.1 = (bf16[2048,128]{1,0:T(8,128)(2,1)S(1)}, bf16[2048,128]{1,0:T(8,128)(2,1)S(1)}, u32[]{:S(2)}, u32[]{:S(2)}) collective-permute-start(bf16[2048,128]{1,0:T(8,128)(2,1)S(1)} %copy-done.10), channel_id=1, source_target_pairs={{0,32},{16,48},{32,0},{48,16},{1,33},{17,49},{33,1},{49,17},{2,34}... | collective-permute-start | bytes 1572872 | tf_op jit(solution)/shard_map/ppermute | solution.py:254
  55.2 3.1 %collective-permute-start.2 = (bf16[2048,128]{1,0:T(8,128)(2,1)S(1)}, bf16[2048,128]{1,0:T(8,128)(2,1)S(1)}, u32[]{:S(2)}, u32[]{:S(2)}) collective-permute-start(bf16[2048,128]{1,0:T(8,128)(2,1)S(1)} %copy-done.11), channel_id=1, source_target_pairs={{0,48},{16,0},{32,16},{48,32},{1,49},{17,1},{33,17},{49,33},{2,50}... | collective-permute-start | bytes 1572872 | tf_op jit(solution)/shard_map/ppermute | solution.py:254
  58.2 9.9 %collective-permute-done.refs_3_.refs_2_ = bf16[2048,128]{1,0:T(8,128)(2,1)S(1)} collective-permute-done((bf16[2048,128]{1,0:T(8,128)(2,1)S(1)}, bf16[2048,128]{1,0:T(8,128)(2,1)S(1)}, u32[]{:S(2)}, u32[]{:S(2)}) %collective-permute-start) | collective-permute-done | bytes 524320 | tf_op jit(solution)/shard_map/ppermute | solution.py:254
  68.2 21.9 %collective-permute-done.1.refs_4_.refs_3_ = bf16[2048,128]{1,0:T(8,128)(2,1)S(1)} collective-permute-done((bf16[2048,128]{1,0:T(8,128)(2,1)S(1)}, bf16[2048,128]{1,0:T(8,128)(2,1)S(1)}, u32[]{:S(2)}, u32[]{:S(2)}) %collective-permute-start.1) | collective-permute-done | bytes 524320 | tf_op jit(solution)/shard_map/ppermute | solution.py:254
  90.1 4.2 %collective-permute-done.2.refs_5_.refs_4_ = bf16[2048,128]{1,0:T(8,128)(2,1)S(1)} collective-permute-done((bf16[2048,128]{1,0:T(8,128)(2,1)S(1)}, bf16[2048,128]{1,0:T(8,128)(2,1)S(1)}, u32[]{:S(2)}, u32[]{:S(2)}) %collective-permute-start.2) | collective-permute-done | bytes 524320 | tf_op jit(solution)/shard_map/ppermute | solution.py:254
  94.3 0.0 all-to-all-done.1.refs_2_
  94.3 0.9 shard_map.106
  95.2 22.7 %all_to_all.30.refs_6_ = bf16[16,4,16,128]{3,2,1,0:T(8,128)(2,1)} all-to-all(bf16[16,4,16,128]{3,2,1,0:T(8,128)(2,1)S(1)} %shard_map.106), channel_id=1, replica_groups=mesh['head_0'=4,'head_1'=2,'seq_0'=4,'seq_1'=16] {'seq_1'}, dimensions={0} | all-to-all | bytes 524288 | tf_op jit(solution)/shard_map/all_to_all | solution.py:258
  118.0 5.2 %shard_map.107 = (bf16[16,128,128]{2,1,0:T(8,128)(2,1)}, bf16[256,128]{1,0:T(8,128)(2,1)}, bf16[256,128]{1,0:T(8,128)(2,1)}, bf16[256,128]{1,0:T(8,128)(2,1)}, bf16[256,128]{1,0:T(8,128)(2,1)}) custom-call(s32[4]{0:T(128)} %pad_add_fusion.refs_0_, bf16[2048,128]{1,0:T(8,128)(2,1)} %get-tuple-element.29.refs_1_, bf16[2048,128]{1,0:T(8,128)(2,1)} %copy-done, ...), custom_call_target="tpu_custom_call" | custom-call | flops 268435456 | bytes 3670016 | tf_op jit(solution)/shard_map/pallas_call | solution.py:57
  123.2 10.0 %all-to-all-start.3 = ((bf16[16,128,128]{2,1,0:T(8,128)(2,1)}), bf16[16,128,128]{2,1,0:T(8,128)(2,1)S(1)}, u32[]{:S(2)}, u32[]{:S(2)}) async-start(bf16[16,128,128]{2,1,0:T(8,128)(2,1)} %get-tuple-element.46), calls=%async_computation.4 | async-start | bytes 1048576 | tf_op jit(solution)/shard_map/all_to_all | solution.py:258
  133.2 1.9 collective-permute-start.3
  135.1 6.7 %collective-permute-start.4 = (bf16[256,128]{1,0:T(8,128)(2,1)}, bf16[256,128]{1,0:T(8,128)(2,1)S(1)}, u32[]{:S(2)}, u32[]{:S(2)}) collective-permute-start(bf16[256,128]{1,0:T(8,128)(2,1)} %get-tuple-element.41), channel_id=1, source_target_pairs={{0,32},{16,48},{32,0},{48,16},{1,33},{17,49},{33,1},{49,17},{2,34}... | collective-permute-start | bytes 196616 | tf_op jit(solution)/shard_map/ppermute | solution.py:254
  141.8 4.0 %collective-permute-start.5 = (bf16[256,128]{1,0:T(8,128)(2,1)}, bf16[256,128]{1,0:T(8,128)(2,1)S(1)}, u32[]{:S(2)}, u32[]{:S(2)}) collective-permute-start(bf16[256,128]{1,0:T(8,128)(2,1)} %get-tuple-element.42), channel_id=1, source_target_pairs={{0,48},{16,0},{32,16},{48,32},{1,49},{17,1},{33,17},{49,33},{2,50}... | collective-permute-start | bytes 196616 | tf_op jit(solution)/shard_map/ppermute | solution.py:254
  145.8 0.0 collective-permute-done.3.refs_8_
  145.8 0.0 collective-permute-done.4.refs_9_
  145.8 1.6 collective-permute-done.5.refs_10_
  147.4 0.6 copy-done.14
  148.0 7.7 %shard_map.108 = (bf16[512,512]{1,0:T(8,128)(2,1)}, bf16[512,512]{1,0:T(8,128)(2,1)}, bf16[512,512]{1,0:T(8,128)(2,1)}) custom-call(s32[4]{0:T(128)} %pad_add_fusion.refs_0_, s32[18,32]{1,0:T(8,128)} %refs_1_.10, bf16[512,512]{1,0:T(8,128)(2,1)} %refs_2_.7, bf16[512,512]{1,0:T(8,128)(2,1)} %refs_3_.5, bf16[512,512]{1,0:T(8,128)(2,1)} %refs_4_.3, ...), custom_call_target="tpu_custom_call" | custom-call | flops 805306368 | bytes 4980736 | tf_op jit(solution)/shard_map/pallas_call | solution.py:57
  155.7 0.0 all-to-all-done.3.refs_0_
  155.7 0.0 copy-start.3
  155.7 1.0 copy-done.3
  156.7 0.2 shard_map.109
  156.9 22.8 %all_to_all.31.refs_1_ = f32[32,1,128]{2,1,0:T(1,128)S(1)} all-to-all(f32[32,1,128]{2,1,0:T(1,128)S(1)} %get-tuple-element.47), channel_id=1, replica_groups=mesh['head_0'=4,'head_1'=2,'seq_0'=4,'seq_1'=16] {'head_0','head_1','seq..., dimensions={0} | all-to-all | bytes 32768 | tf_op jit(solution)/shard_map/all_to_all | solution.py:258
  179.7 1.2 shard_map.110
  180.9 6.4 %all-to-all-start.5 = ((f32[16,1,128]{2,1,0:T(1,128)}), f32[16,1,128]{2,1,0:T(1,128)S(1)}, u32[]{:S(2)}, u32[]{:S(2)}) async-start(f32[16,1,128]{2,1,0:T(1,128)} %get-tuple-element.53), calls=%async_computation.6 | async-start | bytes 16384 | tf_op jit(solution)/shard_map/all_to_all | solution.py:258
  187.3 2.2 %collective-permute-start.6 = (f32[32,128]{1,0:T(8,128)S(1)}, f32[32,128]{1,0:T(8,128)S(1)}, u32[]{:S(2)}, u32[]{:S(2)}) collective-permute-start(f32[32,128]{1,0:T(8,128)S(1)} %get-tuple-element.50), channel_id=1, source_target_pairs={{0,16},{16,32},{32,48},{48,0},{1,17},{17,33},{33,49},{49,1},{2,18}... | collective-permute-start | bytes 49160 | tf_op jit(solution)/shard_map/ppermute | solution.py:254
  189.5 3.6 %collective-permute-start.7 = (f32[32,128]{1,0:T(8,128)S(1)}, f32[32,128]{1,0:T(8,128)S(1)}, u32[]{:S(2)}, u32[]{:S(2)}) collective-permute-start(f32[32,128]{1,0:T(8,128)S(1)} %get-tuple-element.51), channel_id=1, source_target_pairs={{0,32},{16,48},{32,0},{48,16},{1,33},{17,49},{33,1},{49,17},{2,34}... | collective-permute-start | bytes 49160 | tf_op jit(solution)/shard_map/ppermute | solution.py:254
  193.2 2.8 %collective-permute-start.8 = (f32[32,128]{1,0:T(8,128)S(1)}, f32[32,128]{1,0:T(8,128)S(1)}, u32[]{:S(2)}, u32[]{:S(2)}) collective-permute-start(f32[32,128]{1,0:T(8,128)S(1)} %get-tuple-element.52), channel_id=1, source_target_pairs={{0,48},{16,0},{32,16},{48,32},{1,49},{17,1},{33,17},{49,33},{2,50}... | collective-permute-start | bytes 49160 | tf_op jit(solution)/shard_map/ppermute | solution.py:254
  196.0 0.0 collective-permute-done.6.refs_3_
  196.0 0.0 collective-permute-done.7.refs_4_
  196.0 2.0 collective-permute-done.8.refs_5_
  198.0 0.6 all-to-all-done.5.refs_6_
  198.6 0.0 copy-done.5
  198.6 1.2 shard_map.111
  (24 shorter events, 0.0 us)
Async XLA Ops:
  11.2 18.7 %all-to-all-start = ((bf16[4,256,128]{2,1,0:T(8,128)(2,1)}), bf16[4,256,128]{2,1,0:T(8,128)(2,1)S(1)}, u32[]{:S(2)}, u32[]{:S(2)}) async-start(bf16[4,256,128]{2,1,0:T(8,128)(2,1)} %shard_map.102.refs_5_), calls=%async_computation | async-start | bytes 524288 | tf_op jit(solution)/shard_map/all_to_all | solution.py:258
  16.2 101.8 %reduce-scatter.2.cloned.1.call-start = ((), (), s32[]{:S(2)}) async-start(), calls=%async_computation.7 | async-start | bytes 2621440 | tf_op jit(solution)/shard_map/reduce_scatter | solution.py:314
  29.9 0.7 copy-start.8
  32.3 15.1 %copy-start.9 = (bf16[2048,128]{1,0:T(8,128)(2,1)S(1)}, bf16[2048,128]{1,0:T(8,128)(2,1)}, u32[]{:S(2)}) copy-start(bf16[2048,128]{1,0:T(8,128)(2,1)} %get-tuple-element.34) | copy-start | bytes 1572868
  32.3 18.5 %copy-start.10 = (bf16[2048,128]{1,0:T(8,128)(2,1)S(1)}, bf16[2048,128]{1,0:T(8,128)(2,1)}, u32[]{:S(2)}) copy-start(bf16[2048,128]{1,0:T(8,128)(2,1)} %get-tuple-element.35) | copy-start | bytes 1572868
  32.3 22.8 %copy-start.11 = (bf16[2048,128]{1,0:T(8,128)(2,1)S(1)}, bf16[2048,128]{1,0:T(8,128)(2,1)}, u32[]{:S(2)}) copy-start(bf16[2048,128]{1,0:T(8,128)(2,1)} %get-tuple-element.36) | copy-start | bytes 1572868
  32.3 62.0 %copy-start.4 = (s32[18,32]{1,0:T(8,128)S(1)}, s32[18,32]{1,0:T(8,128)}, u32[]{:S(2)}) copy-start(s32[18,32]{1,0:T(8,128)} %refs_1_.10) | copy-start | bytes 6916
  32.3 62.0 %copy-start.6 = (s32[4]{0:T(128)S(1)}, s32[4]{0:T(128)}, u32[]{:S(2)}) copy-start(s32[4]{0:T(128)} %pad_add_fusion.refs_0_) | copy-start | bytes 52
  32.4 61.9 %all-to-all-start.1 = ((bf16[16,4,16,128]{3,2,1,0:T(8,128)(2,1)}), bf16[16,4,16,128]{3,2,1,0:T(8,128)(2,1)S(1)}, u32[]{:S(2)}, u32[]{:S(2)}) async-start(bf16[16,4,16,128]{3,2,1,0:T(8,128)(2,1)} %get-tuple-element.38), calls=%async_computation.2 | async-start | bytes 524288 | tf_op jit(solution)/shard_map/all_to_all | solution.py:258
  47.4 20.7 %collective-permute-start = (bf16[2048,128]{1,0:T(8,128)(2,1)S(1)}, bf16[2048,128]{1,0:T(8,128)(2,1)S(1)}, u32[]{:S(2)}, u32[]{:S(2)}) collective-permute-start(bf16[2048,128]{1,0:T(8,128)(2,1)S(1)} %copy-done.9), channel_id=1, source_target_pairs={{0,16},{16,32},{32,48},{48,0},{1,17},{17,33},{33,49},{49,1},{2,18}... | collective-permute-start | bytes 1572872 | tf_op jit(solution)/shard_map/ppermute | solution.py:254
  50.8 39.3 %collective-permute-start.1 = (bf16[2048,128]{1,0:T(8,128)(2,1)S(1)}, bf16[2048,128]{1,0:T(8,128)(2,1)S(1)}, u32[]{:S(2)}, u32[]{:S(2)}) collective-permute-start(bf16[2048,128]{1,0:T(8,128)(2,1)S(1)} %copy-done.10), channel_id=1, source_target_pairs={{0,32},{16,48},{32,0},{48,16},{1,33},{17,49},{33,1},{49,17},{2,34}... | collective-permute-start | bytes 1572872 | tf_op jit(solution)/shard_map/ppermute | solution.py:254
  55.2 39.2 %collective-permute-start.2 = (bf16[2048,128]{1,0:T(8,128)(2,1)S(1)}, bf16[2048,128]{1,0:T(8,128)(2,1)S(1)}, u32[]{:S(2)}, u32[]{:S(2)}) collective-permute-start(bf16[2048,128]{1,0:T(8,128)(2,1)S(1)} %copy-done.11), channel_id=1, source_target_pairs={{0,48},{16,0},{32,16},{48,32},{1,49},{17,1},{33,17},{49,33},{2,50}... | collective-permute-start | bytes 1572872 | tf_op jit(solution)/shard_map/ppermute | solution.py:254
  68.2 49.8 %copy-start = (bf16[2048,128]{1,0:T(8,128)(2,1)}, bf16[2048,128]{1,0:T(8,128)(2,1)S(1)}, u32[]{:S(2)}) copy-start(bf16[2048,128]{1,0:T(8,128)(2,1)S(1)} %collective-permute-done.refs_3_.refs_2_) | copy-start | bytes 1572868
  90.1 27.9 %copy-start.1 = (bf16[2048,128]{1,0:T(8,128)(2,1)}, bf16[2048,128]{1,0:T(8,128)(2,1)S(1)}, u32[]{:S(2)}) copy-start(bf16[2048,128]{1,0:T(8,128)(2,1)S(1)} %collective-permute-done.1.refs_4_.refs_3_) | copy-start | bytes 1572868
  94.3 23.6 %copy-start.2 = (bf16[2048,128]{1,0:T(8,128)(2,1)}, bf16[2048,128]{1,0:T(8,128)(2,1)S(1)}, u32[]{:S(2)}) copy-start(bf16[2048,128]{1,0:T(8,128)(2,1)S(1)} %collective-permute-done.2.refs_5_.refs_4_) | copy-start | bytes 1572868
  123.2 32.5 %all-to-all-start.3 = ((bf16[16,128,128]{2,1,0:T(8,128)(2,1)}), bf16[16,128,128]{2,1,0:T(8,128)(2,1)S(1)}, u32[]{:S(2)}, u32[]{:S(2)}) async-start(bf16[16,128,128]{2,1,0:T(8,128)(2,1)} %get-tuple-element.46), calls=%async_computation.4 | async-start | bytes 1048576 | tf_op jit(solution)/shard_map/all_to_all | solution.py:258
  133.2 12.6 %collective-permute-start.3 = (bf16[256,128]{1,0:T(8,128)(2,1)}, bf16[256,128]{1,0:T(8,128)(2,1)S(1)}, u32[]{:S(2)}, u32[]{:S(2)}) collective-permute-start(bf16[256,128]{1,0:T(8,128)(2,1)} %get-tuple-element.40), channel_id=1, source_target_pairs={{0,16},{16,32},{32,48},{48,0},{1,17},{17,33},{33,49},{49,1},{2,18}... | collective-permute-start | bytes 196616 | tf_op jit(solution)/shard_map/ppermute | solution.py:254
  135.1 10.7 %collective-permute-start.4 = (bf16[256,128]{1,0:T(8,128)(2,1)}, bf16[256,128]{1,0:T(8,128)(2,1)S(1)}, u32[]{:S(2)}, u32[]{:S(2)}) collective-permute-start(bf16[256,128]{1,0:T(8,128)(2,1)} %get-tuple-element.41), channel_id=1, source_target_pairs={{0,32},{16,48},{32,0},{48,16},{1,33},{17,49},{33,1},{49,17},{2,34}... | collective-permute-start | bytes 196616 | tf_op jit(solution)/shard_map/ppermute | solution.py:254
  141.8 5.6 %collective-permute-start.5 = (bf16[256,128]{1,0:T(8,128)(2,1)}, bf16[256,128]{1,0:T(8,128)(2,1)S(1)}, u32[]{:S(2)}, u32[]{:S(2)}) collective-permute-start(bf16[256,128]{1,0:T(8,128)(2,1)} %get-tuple-element.42), channel_id=1, source_target_pairs={{0,48},{16,0},{32,16},{48,32},{1,49},{17,1},{33,17},{49,33},{2,50}... | collective-permute-start | bytes 196616 | tf_op jit(solution)/shard_map/ppermute | solution.py:254
  145.8 1.6 copy-start.12
  145.8 1.6 copy-start.13
  147.4 0.6 copy-start.14
  148.0 31.7 %copy-start.7 = (s32[4]{0:T(128)S(1)}, s32[4]{0:T(128)}, u32[]{:S(2)}) copy-start(s32[4]{0:T(128)} %pad_add_fusion.refs_0_) | copy-start | bytes 52
  148.0 50.5 %copy-start.5 = (f32[32,512]{1,0:T(8,128)S(1)}, f32[32,512]{1,0:T(8,128)}, u32[]{:S(2)}) copy-start(f32[32,512]{1,0:T(8,128)} %refs_1_.11) | copy-start | bytes 196612
  155.7 1.0 copy-start.3
  180.9 17.7 %all-to-all-start.5 = ((f32[16,1,128]{2,1,0:T(1,128)}), f32[16,1,128]{2,1,0:T(1,128)S(1)}, u32[]{:S(2)}, u32[]{:S(2)}) async-start(f32[16,1,128]{2,1,0:T(1,128)} %get-tuple-element.53), calls=%async_computation.6 | async-start | bytes 16384 | tf_op jit(solution)/shard_map/all_to_all | solution.py:258
  187.3 8.7 %collective-permute-start.6 = (f32[32,128]{1,0:T(8,128)S(1)}, f32[32,128]{1,0:T(8,128)S(1)}, u32[]{:S(2)}, u32[]{:S(2)}) collective-permute-start(f32[32,128]{1,0:T(8,128)S(1)} %get-tuple-element.50), channel_id=1, source_target_pairs={{0,16},{16,32},{32,48},{48,0},{1,17},{17,33},{33,49},{49,1},{2,18}... | collective-permute-start | bytes 49160 | tf_op jit(solution)/shard_map/ppermute | solution.py:254
  189.5 6.5 %collective-permute-start.7 = (f32[32,128]{1,0:T(8,128)S(1)}, f32[32,128]{1,0:T(8,128)S(1)}, u32[]{:S(2)}, u32[]{:S(2)}) collective-permute-start(f32[32,128]{1,0:T(8,128)S(1)} %get-tuple-element.51), channel_id=1, source_target_pairs={{0,32},{16,48},{32,0},{48,16},{1,33},{17,49},{33,1},{49,17},{2,34}... | collective-permute-start | bytes 49160 | tf_op jit(solution)/shard_map/ppermute | solution.py:254
  193.2 4.8 %collective-permute-start.8 = (f32[32,128]{1,0:T(8,128)S(1)}, f32[32,128]{1,0:T(8,128)S(1)}, u32[]{:S(2)}, u32[]{:S(2)}) collective-permute-start(f32[32,128]{1,0:T(8,128)S(1)} %get-tuple-element.52), channel_id=1, source_target_pairs={{0,48},{16,0},{32,16},{48,32},{1,49},{17,1},{33,17},{49,33},{2,50}... | collective-permute-start | bytes 49160 | tf_op jit(solution)/shard_map/ppermute | solution.py:254
Sparse Core Ops, SparseCore 0:
  32.5 61.5 reduce-scatter.1

commit v3 on v2

--- a/solution.py
+++ b/solution.py
@@ -16,6 +16,8 @@
 Z = "seq_1"
 SEQ = (Y, Z)
 
+VMEM_ALL = 60
+
 clip_norm = 1024.0
 momentum_rate = 0.9
 
@@ -27,11 +29,11 @@
     return lax.dot_general(a, b, (((ca,), (cb,)), ((), ())), preferred_element_type=f32)
 
 
-def spec(block, index):
-    return pl.BlockSpec(block, index)
-
-
-def call(kernel, out_shape, operands, flops, in_specs=None, out_specs=None, grid=(1,), scratch=(), vmem=60, after=(), scalars=(), gated=()):
+VMEM = pl.BlockSpec(memory_space=pltpu.VMEM)
+ANY = pl.BlockSpec(memory_space=pl.ANY)
+
+
+def call(kernel, out_shape, operands, flops, in_specs=None, out_specs=None, grid=(), scratch=(), vmem=16, after=(), scalars=(), gated=()):
     leaves = jax.tree.leaves((operands, out_shape))
     n = len(scalars) + len(operands)
     skip = n + len(after) + len(gated)
@@ -40,14 +42,11 @@
     def run(*refs):
         kernel(*refs[:n], *refs[skip:last], *refs[last + len(gated) :])
 
-    def whole(x):
-        return spec(x.shape, lambda *_: (0,) * len(x.shape))
-
     in_specs = list(in_specs or [None] * len(operands))
-    in_specs = [whole(x) if i is None else i for x, i in zip(operands, in_specs)]
+    in_specs = [VMEM if i is None else i for i in in_specs]
     if out_specs is None:
-        out_specs = jax.tree.map(whole, out_shape)
-    anywhere = pl.BlockSpec(memory_space=pl.ANY)
+        out_specs = jax.tree.map(lambda _: VMEM, out_shape)
+    anywhere = ANY
     aliases = {}
     if gated:
         first = len(jax.tree.leaves(out_shape))
@@ -110,31 +109,72 @@
     return parts[0] if count == 1 else jnp.concatenate(parts, axis=1)
 
 
-def states_kernel(q_ref, k_ref, v_ref, g_ref, out_ref):
-    out_ref[0, :D, :] = dot(q_ref[...], g_ref[...], 0, 0).astype(bf16)
-    out_ref[0, D:, :] = dot(k_ref[...], v_ref[...], 0, 0).astype(bf16)
-
-
-def local_kernel(info_ref, weight_ref, q_ref, k_ref, g_ref, out_ref):
+def start_all(pairs, sems):
+    moves = [pltpu.make_async_copy(source, to, sems.at[i]) for i, (source, to) in enumerate(pairs)]
+    for move in moves:
+        move.start()
+    return moves
+
+
+def states_kernel(q_hbm, g_hbm, k_hbm, v_hbm, out_ref, q_ref, g_ref, k_ref, v_ref, sems):
+    moves = start_all(
+        [(q_hbm, q_ref), (g_hbm, g_ref), (k_hbm, k_ref), (v_hbm, v_ref)], sems
+    )
+    moves[0].wait()
+    moves[1].wait()
+    for h in range(out_ref.shape[0]):
+        s = lanes(h)
+        out_ref[h, :D, :] = dot(q_ref[:, s], g_ref[:, s], 0, 0).astype(bf16)
+    moves[2].wait()
+    moves[3].wait()
+    for h in range(out_ref.shape[0]):
+        s = lanes(h)
+        out_ref[h, D:, :] = dot(k_ref[:, s], v_ref[:, s], 0, 0).astype(bf16)
+
+
+def local_kernel(info_ref, weight_ref, q_hbm, k_hbm, g_hbm, x_hbm, loc_ref, proj_hbm, *refs):
+    keyed_hbm = refs[:-8]
+    q_ref, k_ref, g_ref, x_ref, right_ref, done_ref, in_sems, out_sems = refs[-8:]
+    n_y = len(keyed_hbm)
+    width = k_ref.shape[1]
+    chunks, _, chunk = x_ref.shape
+    moves = start_all(
+        [(k_hbm, k_ref), (q_hbm, q_ref), (g_hbm, g_ref)]
+        + [(x_hbm.at[:, pl.ds(c * chunk, chunk)], x_ref.at[c]) for c in range(chunks)],
+        in_sems,
+    )
+    y = info_ref[1]
+    moves[0].wait()
+    for n in range(n_y):
+        right_ref[:, lanes(n)] = k_ref[:, lanes(lax.rem(y + n, n_y))]
+    moves[1].wait()
+    moves[2].wait()
     blocks = q_ref.shape[0] // D
-    head = info_ref[0] * pl.num_programs(0) + pl.program_id(0)
-    diag = diagonal(head, weight_ref, True)
-    for j in range(blocks):
-        rows = slice(j * D, (j + 1) * D)
-        scores = dot(k_ref[rows, :], q_ref[j * D :, :], 1, 1)
-        mixed = weighted(scores, j, j, head, weight_ref, diag)
-        out_ref[rows, :] = dot(mixed, g_ref[j * D :, :], 1, 0)
-
-
-def keyed_kernel(info_ref, x_ref, k_ref, loc_ref, proj_ref, *out_refs):
-    y = info_ref[1]
-    n_out = len(out_refs)
-    heads = [lanes(lax.rem(y + n, n_out)) for n in range(n_out)]
-    right = jnp.concatenate([k_ref[:, s] for s in heads] + [loc_ref[...].astype(bf16)], axis=1)
-    res = dot(x_ref[...], right, 0, 0).astype(bf16)
-    for n in range(n_out):
-        out_refs[n][...] = res[:, lanes(n)]
-        proj_ref[n, :, :] = res[:, lanes(n_out + n)]
+    for h in range(n_y):
+        s = lanes(h)
+        head = info_ref[0] * n_y + h
+        diag = diagonal(head, weight_ref, True)
+        for j in range(blocks):
+            rows = slice(j * D, (j + 1) * D)
+            scores = dot(k_ref[rows, s], q_ref[j * D :, s], 1, 1)
+            mixed = weighted(scores, j, j, head, weight_ref, diag)
+            res = dot(mixed, g_ref[j * D :, s], 1, 0)
+            loc_ref[rows, s] = res
+            right_ref[rows, width + h * D : width + (h + 1) * D] = res.astype(bf16)
+    sent = []
+    for c in range(chunks):
+        moves[3 + c].wait()
+        part = pl.ds(c * chunk, chunk)
+        res = dot(x_ref[c], right_ref[...], 0, 0).astype(bf16)
+        for n in range(2 * n_y):
+            done_ref[c, n, :, :] = res[:, lanes(n)]
+        sent += start_all(
+            [(done_ref.at[c, n], keyed_hbm[n].at[part, :]) for n in range(n_y)]
+            + [(done_ref.at[c, pl.ds(n_y, n_y)], proj_hbm.at[:, part, :])],
+            out_sems.at[c],
+        )
+    for move in sent:
+        move.wait()
 
 
 def turn_kernel(in_ref, out_ref):
@@ -168,56 +208,81 @@
         out_ref[c % nz, c // nz] = total[c].astype(bf16)
 
 
-def project_kernel(info_ref, a0, a1, a2, a3, loc_ref, r_ref, out_ref, *own_refs):
-    y = info_ref[1]
+def project_kernel(info_ref, a0, a1, a2, a3, loc_hbm, r_hbm, out_hbm, *refs):
+    own_hbm = refs[:-8]
+    a_ref, loc_ref, r_ref, done_ref, r_sem, a_sems, out_sems, own_sems = refs[-8:]
     keyed = (a0, a1, a2, a3)
     n_y = len(keyed)
+    chunks, rows = loc_ref.shape[:2]
+    got = start_all([(r_hbm, r_ref)], r_sem)
+    moves = []
+    for c in range(chunks):
+        part = pl.ds(c * rows, rows)
+        moves.append(
+            start_all(
+                [(keyed[n].at[part, :], a_ref.at[c, n]) for n in range(n_y)]
+                + [(loc_hbm.at[part, :], loc_ref.at[c])],
+                a_sems.at[c],
+            )
+        )
+    y = info_ref[1]
     half = r_ref.shape[0] // 2
-    nz, each = out_ref.shape[:2]
-
-    @pl.when(pl.program_id(0) == 0)
-    def _():
-        for n in range(n_y):
-            own_refs[n][...] = r_ref[:, lax.rem(y + n, n_y)].reshape(2 * D, D)
-
+    nz = out_hbm.shape[0]
+    each = out_hbm.shape[1] // n_y
+    got[0].wait()
     states = [r_ref[:half, lax.rem(y + n_y - n, n_y)].reshape(D, D) for n in range(n_y)]
-    left = jnp.concatenate([a[...] for a in keyed], axis=1)
-    res = loc_ref[...].astype(f32) + dot(left, jnp.concatenate(states, axis=0), 1, 0)
-    res = res.astype(bf16)
-    for z in range(nz):
-        out_ref[z, :, :] = res[z * each : (z + 1) * each, :]
+    states = jnp.concatenate(states, axis=0)
+    sent = []
+    for c in range(chunks):
+        for move in moves[c]:
+            move.wait()
+        left = jnp.concatenate([a_ref[c, n] for n in range(n_y)], axis=1)
+        res = (loc_ref[c].astype(f32) + dot(left, states, 1, 0)).astype(bf16)
+        inner = rows // (nz * each)
+        for b in range(inner):
+            for z in range(nz):
+                done_ref[c, z, b * each : (b + 1) * each, :] = res[
+                    (b * nz + z) * each : (b * nz + z + 1) * each, :
+                ]
+        sent += start_all(
+            [(done_ref.at[c], out_hbm.at[:, pl.ds(c * inner * each, inner * each), :])],
+            out_sems.at[pl.ds(c, 1)],
+        )
+    sent += start_all(
+        [(r_ref.at[:, lax.rem(y + n, n_y)], own_hbm[n]) for n in range(n_y)], own_sems
+    )
+    for move in sent:
+        move.wait()
 
 
 def outputs_kernel(
-    info_ref, weight_ref, q_ref, k_ref, v_ref, g_ref, loc_ref, r0, r1, r2, r3, dq_ref, dk_ref, dv_ref, r_ref
+    info_ref, weight_ref, q_ref, k_ref, v_ref, g_ref, loc_ref, r0, r1, r2, r3, dq_ref, dk_ref, dv_ref, end_ref
 ):
-    n = pl.program_id(0)
-    n_y = pl.num_programs(0)
-    for i, r in enumerate((r0, r1, r2, r3)):
-
-        @pl.when(n == i)
-        def _():
-            r_ref[...] = r[...]
-
+    states = (r0, r1, r2, r3)
+    n_y = len(states)
+    end_ref[...] = jnp.zeros_like(end_ref)
     blocks = q_ref.shape[0] // D
-    head = info_ref[0] * n_y + lax.rem(info_ref[1] + n_y - n, n_y)
-    returned = r_ref[:D, :]
-    carried = r_ref[D:, :]
-    query, keys, values, grad = q_ref[...], k_ref[...], v_ref[...], g_ref[...]
-    dv_ref[...] = (loc_ref[...] + dot(keys, returned, 1, 0)).astype(bf16)
-    base_k = dot(values, returned, 1, 1)
-    base_q = dot(grad, carried, 1, 1)
-    diag = diagonal(head, weight_ref, False)
-    diag_t = diagonal(head, weight_ref, True)
-    for i in range(blocks):
-        rows = slice(i * D, (i + 1) * D)
-        upto = (i + 1) * D
-        before = dot(grad[rows], values[:upto], 1, 1)
-        dmix = weighted(before, 0, i, head, weight_ref, diag)
-        dq_ref[rows, :] = (base_q[rows] + dot(dmix, keys[:upto], 1, 0)).astype(bf16)
-        later = dot(values[rows], grad[i * D :], 1, 1)
-        dmix_t = weighted(later, i, i, head, weight_ref, diag_t)
-        dk_ref[rows, :] = (base_k[rows] + dot(dmix_t, query[i * D :], 1, 0)).astype(bf16)
+    for n in range(n_y):
+        h = lax.rem(info_ref[1] + n_y - n, n_y)
+        s = lanes(h)
+        head = info_ref[0] * n_y + h
+        both = states[n][...].reshape(2 * D, D)
+        returned, carried = both[:D], both[D:]
+        query, keys, values, grad = q_ref[:, s], k_ref[:, s], v_ref[:, s], g_ref[:, s]
+        dv_ref[:, s] = (loc_ref[:, s] + dot(keys, returned, 1, 0)).astype(bf16)
+        base_k = dot(values, returned, 1, 1)
+        base_q = dot(grad, carried, 1, 1)
+        diag = diagonal(head, weight_ref, False)
+        diag_t = diagonal(head, weight_ref, True)
+        for i in range(blocks):
+            rows = slice(i * D, (i + 1) * D)
+            upto = (i + 1) * D
+            before = dot(grad[rows], values[:upto], 1, 1)
+            dmix = weighted(before, 0, i, head, weight_ref, diag)
+            dq_ref[rows, s] = (base_q[rows] + dot(dmix, keys[:upto], 1, 0)).astype(bf16)
+            later = dot(values[rows], grad[i * D :], 1, 1)
+            dmix_t = weighted(later, i, i, head, weight_ref, diag_t)
+            dk_ref[rows, s] = (base_k[rows] + dot(dmix_t, query[i * D :], 1, 0)).astype(bf16)
 
 
 def shard_kernel(in_ref, out_ref, square_ref):
@@ -268,39 +333,38 @@
         [lax.axis_index(HEAD), lax.axis_index(Y), lax.axis_index(Z), jnp.int32(0)]
     ).astype(jnp.int32)
 
-    column = spec((length, D), lambda h, *_: (0, h))
+    square_sds = sds((length, width), bf16)
+    held = pltpu.VMEM((length, width), bf16)
+    dma = pltpu.SemaphoreType.DMA
     both = call(
         states_kernel,
         sds((heads, 2 * D, D), bf16),
-        (queries, keys, values, out_grad),
+        (queries, out_grad, keys, values),
         4 * length * width * D,
-        [column] * 4,
-        spec((1, 2 * D, D), lambda h: (h, 0, 0)),
-        (heads,),
-    )
-    local = call(
+        [ANY] * 4,
+        scratch=[held] * 4 + [dma((4,))],
+        vmem=VMEM_ALL,
+    )
+    chunk = 512
+    chunks = features // chunk
+    local, proj, *keyed = call(
         local_kernel,
-        sds((length, width), f32),
-        (queries, keys, out_grad),
-        3 * length * length * width,
-        [column] * 3,
-        column,
-        (heads,),
+        (sds((length, width), f32), sds((heads, features, D), bf16))
+        + tuple(sds((features, D), bf16) for _ in range(n_y)),
+        (queries, keys, out_grad, inputs),
+        4 * length * width * features + 3 * length * length * width,
+        [ANY] * 4,
+        (VMEM,) + (ANY,) * (n_y + 1),
+        scratch=[held] * 3
+        + [
+            pltpu.VMEM((chunks, length, chunk), bf16),
+            pltpu.VMEM((length, 2 * width), bf16),
+            pltpu.VMEM((chunks, 2 * n_y, chunk, D), bf16),
+            dma((3 + chunks,)),
+            dma((chunks, n_y + 1)),
+        ],
         scalars=(info, level_weight),
-        after=(both,),
-    )
-    block = 512
-    steps = features // block
-    proj, *keyed = call(
-        keyed_kernel,
-        (sds((heads, features, D), bf16),) + tuple(sds((features, D), bf16) for _ in range(n_y)),
-        (inputs, keys, local),
-        4 * length * width * features,
-        [spec((length, block), lambda c, *_: (0, c)), None, None],
-        (spec((heads, block, D), lambda c, *_: (0, c, 0)),)
-        + (spec((block, D), lambda c, *_: (c, 0)),) * n_y,
-        (steps,),
-        scalars=(info,),
+        vmem=VMEM_ALL,
     )
     both, proj, *keyed[1:] = call(
         turn_kernel,
@@ -308,6 +372,7 @@
         (swap(both, Y),),
         1 << 16,
         gated=(proj, *keyed[1:]),
+        vmem=VMEM_ALL,
     )
     both = swap(both, Z)
     keyed = [keyed[0]] + [shift(keyed[n], Y, n) for n in range(1, n_y)]
@@ -321,38 +386,43 @@
         (both,),
         1 << 21,
         scalars=(info, level_weight),
-        after=keyed[1:],
+        after=(keyed[1],),
         vmem=8,
     )
     both = swap(both, Z)
 
-    row = spec((features // n_y, D), lambda b, *_: (b, 0))
-    each = features // n_z // n_y
+    rows = features // 2
     parts, *own = call(
         project_kernel,
-        (sds((n_z, features // n_z, D), bf16),) + tuple(sds((2 * D, D), bf16) for _ in range(n_y)),
+        (sds((n_z, features // n_z, D), bf16),)
+        + tuple(sds((n_z, 2 * D // n_z, D), bf16) for _ in range(n_y)),
         (*keyed, proj, both),
         2 * features * n_y * D * D,
-        [row] * (n_y + 1) + [None],
-        (spec((n_z, each, D), lambda b, *_: (0, b, 0)),)
-        + (spec((2 * D, D), lambda b, *_: (0, 0)),) * n_y,
-        (n_y,),
+        [ANY] * (n_y + 2),
+        (ANY,) * (n_y + 1),
+        scratch=[
+            pltpu.VMEM((2, n_y, rows, D), bf16),
+            pltpu.VMEM((2, rows, D), bf16),
+            pltpu.VMEM(both.shape, bf16),
+            pltpu.VMEM((2, n_z, rows // n_z, D), bf16),
+            dma((1,)),
+            dma((2, n_y + 1)),
+            dma((2,)),
+            dma((n_y,)),
+        ],
         scalars=(info,),
+        vmem=VMEM_ALL,
     )
     parts = swap(parts, Z)
 
     own = [own[0]] + [shift(own[n], Y, n) for n in range(1, n_y)]
-    turned = spec((length, D), lambda n, info_ref, _: (0, lax.rem(info_ref[1] + n_y - n, n_y)))
-    query_grad, key_grad, value_grad = call(
+    query_grad, key_grad, value_grad, end = call(
         outputs_kernel,
-        tuple(sds((length, width), bf16) for _ in range(3)),
+        (sds((length, width), bf16),) * 3 + (sds((8, D), f32),),
         (queries, keys, values, out_grad, local, *own),
         6 * length * length * width,
-        [turned] * 5 + [None] * n_y,
-        (turned,) * 3,
-        (n_y,),
-        [pltpu.VMEM((2 * D, D), bf16)],
         scalars=(info, level_weight),
+        vmem=VMEM_ALL,
     )
 
     near, rest = HEAD + (Y,), (Z,)
@@ -362,7 +432,7 @@
         (sds((n_y * rows, D), f32), sds((lax.axis_size(near), 1, D), f32)),
         (parts,),
         1 << 20,
-        after=(query_grad,),
+        after=(end,),
         vmem=8,
     )
     square = swap(square, near)

time: 208 us -> 191 us (0.918)
  blocking collectives: 45.5 us -> 21.9 us
  starting transfers between devices: 68.4 us -> 82.1 us
  Pallas kernels: 35.2 us -> 30.1 us
  waiting for transfers between devices: 40.2 us -> 37.6 us
    all_to_all x2 -> x1, blocking collectives: 45.5 us -> 21.9 us  [swap(): return lax.all_to_all(x, axes, 0, 0, tiled=True)]
    all_to_all x4 -> x5, starting transfers between devices: 36.5 us -> 51.1 us  [swap(): return lax.all_to_all(x, axes, 0, 0, tiled=True)]
    pallas_call x10 -> x9, Pallas kernels: 35.2 us -> 30.1 us  [call(): pl.pallas_call(run, out_shape=out_shape, grid_spec=pltpu.PrefetchScalarGr...]
    ppermute x9, waiting for transfers between devices: 39.6 us -> 37 us  [shift(): return lax.ppermute(x, axis, [(i, (i + by) % n) for i in range(n)])]
  transfers between devices with their start and end apart: 14 -> 15, of which waited for: 6 -> 7; matrix products, arithmetic and copies ran while one was open for 0% -> 0% of each run, Pallas kernels for 10% -> 10%
where the time goes in v3:
time: 191 us; the launch traced here: 190 us
  starting transfers between devices  82.1 us (43%)
  waiting for transfers between devices  37.6 us (20%)
  Pallas kernels  30.1 us (16%)
  blocking collectives  21.9 us (11%)
  between operations  14.3 us (7%)
  local copies, waits for them, and re-layouts  2.87 us (2%)
    all_to_all x5, starting transfers between devices, swap(): return lax.all_to_all(x, axes, 0, 0, tiled=True)  51.1 us
    ppermute x9, waiting for transfers between devices, shift(): return lax.ppermute(x, axis, [(i, (i + by) % n) for i in range(n)])  37 us
    ppermute x9, starting transfers between devices, shift(): return lax.ppermute(x, axis, [(i, (i + by) % n) for i in range(n)])  31 us
    pallas_call x9, Pallas kernels, call(): pl.pallas_call(run, out_shape=out_shape, grid_spec=pltpu.PrefetchScalarGr...  30.1 us
    all_to_all x1, blocking collectives, swap(): return lax.all_to_all(x, axes, 0, 0, tiled=True)  21.9 us
  transfers between devices with their start and end apart: 15, of which 7 were waited for; matrix products, arithmetic and copies ran while one was open for 0% of the time, Pallas kernels for 10%

profile of v3, /device:TPU:1, one launch (start us, length us, event | category | flops | bytes accessed | tf_op | source)
XLA Modules:
  0.0 189.5 jit_solution(13001032356268660202)
XLA Ops:
  7.2 2.6 %shard_map.103 = bf16[4,256,128]{2,1,0:T(8,128)(2,1)} custom-call(bf16[512,512]{1,0:T(8,128)(2,1)} %refs_2_.5, bf16[512,512]{1,0:T(8,128)(2,1)} %refs_5_.3, bf16[512,512]{1,0:T(8,128)(2,1)} %refs_3_.5, bf16[512,512]{1,0:T(8,128)(2,1)} %refs_4_.3), custom_call_target="tpu_custom_call" | custom-call | flops 134217728 | bytes 2359296 | tf_op jit(solution)/shard_map/pallas_call | solution.py:56
  9.8 5.0 %all-to-all-start = ((bf16[4,256,128]{2,1,0:T(8,128)(2,1)}), bf16[4,256,128]{2,1,0:T(8,128)(2,1)S(1)}, u32[]{:S(2)}, u32[]{:S(2)}) async-start(bf16[4,256,128]{2,1,0:T(8,128)(2,1)} %shard_map.103), calls=%async_computation | async-start | bytes 524288 | tf_op jit(solution)/shard_map/all_to_all | solution.py:323
  14.8 0.7 pad_add_fusion.refs_0_
  15.5 9.7 %shard_map.102 = (f32[512,512]{1,0:T(8,128)}, bf16[4,2048,128]{2,1,0:T(8,128)(2,1)}, bf16[2048,128]{1,0:T(8,128)(2,1)}, bf16[2048,128]{1,0:T(8,128)(2,1)}, bf16[...) custom-call(s32[4]{0:T(128)} %pad_add_fusion.refs_0_, s32[18,32]{1,0:T(8,128)} %refs_1_.8, bf16[512,512]{1,0:T(8,128)(2,1)} %refs_2_.5, ...), custom_call_target="tpu_custom_call" | custom-call | flops 2550136832 | bytes 8912896 | tf_op jit(solution)/shard_map/pallas_call | solution.py:56
  25.2 0.0 all-to-all-done.refs_0_
  25.3 0.7 copy-done.7
  26.0 1.7 shard_map.104
  27.7 0.0 reduce-scatter.2.cloned.1.call-update
  27.7 15.1 %all-to-all-start.1 = ((bf16[16,4,16,128]{3,2,1,0:T(8,128)(2,1)}), bf16[16,4,16,128]{3,2,1,0:T(8,128)(2,1)S(1)}, u32[]{:S(2)}, u32[]{:S(2)}) async-start(bf16[16,4,16,128]{3,2,1,0:T(8,128)(2,1)} %get-tuple-element.41), calls=%async_computation.2 | async-start | bytes 524288 | tf_op jit(solution)/shard_map/all_to_all | solution.py:323
  42.7 0.0 copy-done.8
  42.8 3.4 %collective-permute-start = (bf16[2048,128]{1,0:T(8,128)(2,1)S(1)}, bf16[2048,128]{1,0:T(8,128)(2,1)S(1)}, u32[]{:S(2)}, u32[]{:S(2)}) collective-permute-start(bf16[2048,128]{1,0:T(8,128)(2,1)S(1)} %copy-done.8), channel_id=1, source_target_pairs={{0,16},{16,32},{32,48},{48,0},{1,17},{17,33},{33,49},{49,1},{2,18}... | collective-permute-start | bytes 1572872 | tf_op jit(solution)/shard_map/ppermute | solution.py:319
  46.1 17.3 %collective-permute-done.refs_3_.refs_2_ = bf16[2048,128]{1,0:T(8,128)(2,1)S(1)} collective-permute-done((bf16[2048,128]{1,0:T(8,128)(2,1)S(1)}, bf16[2048,128]{1,0:T(8,128)(2,1)S(1)}, u32[]{:S(2)}, u32[]{:S(2)}) %collective-permute-start) | collective-permute-done | bytes 524320 | tf_op jit(solution)/shard_map/ppermute | solution.py:319
  63.4 0.0 all-to-all-done.1.refs_2_
  63.5 1.6 shard_map.105
  65.1 10.3 %all-to-all-start.2 = ((bf16[16,4,16,128]{3,2,1,0:T(8,128)(2,1)}), bf16[16,4,16,128]{3,2,1,0:T(8,128)(2,1)S(1)}, u32[]{:S(2)}, u32[]{:S(2)}) async-start(bf16[16,4,16,128]{3,2,1,0:T(8,128)(2,1)} %shard_map.105), calls=%async_computation.3 | async-start | bytes 524288 | tf_op jit(solution)/shard_map/all_to_all | solution.py:323
  75.4 4.4 %collective-permute-start.1 = (bf16[2048,128]{1,0:T(8,128)(2,1)S(1)}, bf16[2048,128]{1,0:T(8,128)(2,1)S(1)}, u32[]{:S(2)}, u32[]{:S(2)}) collective-permute-start(bf16[2048,128]{1,0:T(8,128)(2,1)S(1)} %copy-done.9), channel_id=1, source_target_pairs={{0,32},{16,48},{32,0},{48,16},{1,33},{17,49},{33,1},{49,17},{2,34}... | collective-permute-start | bytes 1572872 | tf_op jit(solution)/shard_map/ppermute | solution.py:319
  79.9 2.8 %collective-permute-start.2 = (bf16[2048,128]{1,0:T(8,128)(2,1)S(1)}, bf16[2048,128]{1,0:T(8,128)(2,1)S(1)}, u32[]{:S(2)}, u32[]{:S(2)}) collective-permute-start(bf16[2048,128]{1,0:T(8,128)(2,1)S(1)} %copy-done.10), channel_id=1, source_target_pairs={{0,48},{16,0},{32,16},{48,32},{1,49},{17,1},{33,17},{49,33},{2,50}... | collective-permute-start | bytes 1572872 | tf_op jit(solution)/shard_map/ppermute | solution.py:319
  82.7 4.2 %collective-permute-done.1.refs_3_ = bf16[2048,128]{1,0:T(8,128)(2,1)S(1)} collective-permute-done((bf16[2048,128]{1,0:T(8,128)(2,1)S(1)}, bf16[2048,128]{1,0:T(8,128)(2,1)S(1)}, u32[]{:S(2)}, u32[]{:S(2)}) %collective-permute-start.1) | collective-permute-done | bytes 524320 | tf_op jit(solution)/shard_map/ppermute | solution.py:319
  86.8 11.2 %collective-permute-done.2.refs_4_ = bf16[2048,128]{1,0:T(8,128)(2,1)S(1)} collective-permute-done((bf16[2048,128]{1,0:T(8,128)(2,1)S(1)}, bf16[2048,128]{1,0:T(8,128)(2,1)S(1)}, u32[]{:S(2)}, u32[]{:S(2)}) %collective-permute-start.2) | collective-permute-done | bytes 524320 | tf_op jit(solution)/shard_map/ppermute | solution.py:319
  98.0 0.0 all-to-all-done.2.refs_6_
  98.0 0.0 reduce-scatter.2.cloned.1.call-done.refs_5_
  98.0 0.8 copy-done.12
  98.8 0.1 copy-done.6
  98.9 4.1 %shard_map.106 = (bf16[16,128,128]{2,1,0:T(8,128)(2,1)}, bf16[16,16,128]{2,1,0:T(8,128)(2,1)}, bf16[16,16,128]{2,1,0:T(8,128)(2,1)}, bf16[16,16,128]{2,1,0:T(8,128)(2,1)}, bf16[16,16,128]{2,1,0:T(8,128)(2,1)}) custom-call(s32[4]{0:T(128)} %pad_add_fusion.refs_0_, bf16[2048,128]{1,0:T(8,128)(2,1)} %get-tuple-element.32.refs_1_, bf16[2048,128]{1,0:T(8,128)(2,1)} %copy-done, ...), custom_call_target="tpu_custom_call" | custom-call | flops 268435456 | bytes 3670016 | tf_op jit(solution)/shard_map/pallas_call | solution.py:56
  103.0 11.2 %all-to-all-start.3 = ((bf16[16,128,128]{2,1,0:T(8,128)(2,1)}), bf16[16,128,128]{2,1,0:T(8,128)(2,1)S(1)}, u32[]{:S(2)}, u32[]{:S(2)}) async-start(bf16[16,128,128]{2,1,0:T(8,128)(2,1)} %get-tuple-element.49), calls=%async_computation.4 | async-start | bytes 1048576 | tf_op jit(solution)/shard_map/all_to_all | solution.py:323
  114.2 0.0 copy-start.1
  114.2 5.5 %collective-permute-start.3 = (bf16[16,16,128]{2,1,0:T(8,128)(2,1)}, bf16[16,16,128]{2,1,0:T(8,128)(2,1)S(1)}, u32[]{:S(2)}, u32[]{:S(2)}) collective-permute-start(bf16[16,16,128]{2,1,0:T(8,128)(2,1)} %get-tuple-element.43), channel_id=1, source_target_pairs={{0,16},{16,32},{32,48},{48,0},{1,17},{17,33},{33,49},{49,1},{2,18}... | collective-permute-start | bytes 196616 | tf_op jit(solution)/shard_map/ppermute | solution.py:319
  119.7 3.2 %collective-permute-start.4 = (bf16[16,16,128]{2,1,0:T(8,128)(2,1)}, bf16[16,16,128]{2,1,0:T(8,128)(2,1)S(1)}, u32[]{:S(2)}, u32[]{:S(2)}) collective-permute-start(bf16[16,16,128]{2,1,0:T(8,128)(2,1)} %get-tuple-element.44), channel_id=1, source_target_pairs={{0,32},{16,48},{32,0},{48,16},{1,33},{17,49},{33,1},{49,17},{2,34}... | collective-permute-start | bytes 196616 | tf_op jit(solution)/shard_map/ppermute | solution.py:319
  122.9 3.1 %collective-permute-start.5 = (bf16[16,16,128]{2,1,0:T(8,128)(2,1)}, bf16[16,16,128]{2,1,0:T(8,128)(2,1)S(1)}, u32[]{:S(2)}, u32[]{:S(2)}) collective-permute-start(bf16[16,16,128]{2,1,0:T(8,128)(2,1)} %get-tuple-element.45), channel_id=1, source_target_pairs={{0,48},{16,0},{32,16},{48,32},{1,49},{17,1},{33,17},{49,33},{2,50}... | collective-permute-start | bytes 196616 | tf_op jit(solution)/shard_map/ppermute | solution.py:319
  126.0 0.0 collective-permute-done.3.refs_8_
  126.0 0.5 collective-permute-done.4.refs_9_
  126.5 2.0 %collective-permute-done.5.refs_10_ = bf16[16,16,128]{2,1,0:T(8,128)(2,1)S(1)} collective-permute-done((bf16[16,16,128]{2,1,0:T(8,128)(2,1)}, bf16[16,16,128]{2,1,0:T(8,128)(2,1)S(1)}, u32[]{:S(2)}, u32[]{:S(2)}) %collective-permute-start.5) | collective-permute-done | bytes 65568 | tf_op jit(solution)/shard_map/ppermute | solution.py:319
  128.4 0.6 copy-done.15
  129.0 7.8 %shard_map.107 = (bf16[512,512]{1,0:T(8,128)(2,1)}, bf16[512,512]{1,0:T(8,128)(2,1)}, bf16[512,512]{1,0:T(8,128)(2,1)}, f32[8,128]{1,0:T(8,128)}) custom-call(s32[4]{0:T(128)} %pad_add_fusion.refs_0_, s32[18,32]{1,0:T(8,128)} %refs_1_.8, bf16[512,512]{1,0:T(8,128)(2,1)} %refs_2_.5, bf16[512,512]{1,0:T(8,128)(2,1)} %refs_3_.5, bf16[512,512]{1,0:T(8,128)(2,1)} %refs_4_.3, ...), custom_call_target="tpu_custom_call" | custom-call | flops 805306368 | bytes 4984832 | tf_op jit(solution)/shard_map/pallas_call | solution.py:56
  136.9 0.0 all-to-all-done.3.refs_0_
  136.9 0.7 copy-done.5
  137.5 0.2 shard_map.108
  137.7 21.9 %all_to_all.30.refs_1_ = f32[32,1,128]{2,1,0:T(1,128)S(1)} all-to-all(f32[32,1,128]{2,1,0:T(1,128)S(1)} %get-tuple-element.51), channel_id=1, replica_groups=mesh['head_0'=4,'head_1'=2,'seq_0'=4,'seq_1'=16] {'head_0','head_1','seq..., dimensions={0} | all-to-all | bytes 32768 | tf_op jit(solution)/shard_map/all_to_all | solution.py:323
  159.6 1.2 shard_map.109
  160.8 9.4 %all-to-all-start.5 = ((f32[16,1,128]{2,1,0:T(1,128)}), f32[16,1,128]{2,1,0:T(1,128)S(1)}, u32[]{:S(2)}, u32[]{:S(2)}) async-start(f32[16,1,128]{2,1,0:T(1,128)} %get-tuple-element.57), calls=%async_computation.6 | async-start | bytes 16384 | tf_op jit(solution)/shard_map/all_to_all | solution.py:323
  170.2 2.2 %collective-permute-start.6 = (f32[32,128]{1,0:T(8,128)S(1)}, f32[32,128]{1,0:T(8,128)S(1)}, u32[]{:S(2)}, u32[]{:S(2)}) collective-permute-start(f32[32,128]{1,0:T(8,128)S(1)} %get-tuple-element.54), channel_id=1, source_target_pairs={{0,16},{16,32},{32,48},{48,0},{1,17},{17,33},{33,49},{49,1},{2,18}... | collective-permute-start | bytes 49160 | tf_op jit(solution)/shard_map/ppermute | solution.py:319
  172.4 3.6 %collective-permute-start.7 = (f32[32,128]{1,0:T(8,128)S(1)}, f32[32,128]{1,0:T(8,128)S(1)}, u32[]{:S(2)}, u32[]{:S(2)}) collective-permute-start(f32[32,128]{1,0:T(8,128)S(1)} %get-tuple-element.55), channel_id=1, source_target_pairs={{0,32},{16,48},{32,0},{48,16},{1,33},{17,49},{33,1},{49,17},{2,34}... | collective-permute-start | bytes 49160 | tf_op jit(solution)/shard_map/ppermute | solution.py:319
  176.1 2.8 %collective-permute-start.8 = (f32[32,128]{1,0:T(8,128)S(1)}, f32[32,128]{1,0:T(8,128)S(1)}, u32[]{:S(2)}, u32[]{:S(2)}) collective-permute-start(f32[32,128]{1,0:T(8,128)S(1)} %get-tuple-element.56), channel_id=1, source_target_pairs={{0,48},{16,0},{32,16},{48,32},{1,49},{17,1},{33,17},{49,33},{2,50}... | collective-permute-start | bytes 49160 | tf_op jit(solution)/shard_map/ppermute | solution.py:319
  178.9 0.0 collective-permute-done.6.refs_3_
  178.9 0.0 collective-permute-done.7.refs_4_
  178.9 2.0 %collective-permute-done.8.refs_5_ = f32[32,128]{1,0:T(8,128)S(1)} collective-permute-done((f32[32,128]{1,0:T(8,128)S(1)}, f32[32,128]{1,0:T(8,128)S(1)}, u32[]{:S(2)}, u32[]{:S(2)}) %collective-permute-start.8) | collective-permute-done | bytes 16416 | tf_op jit(solution)/shard_map/ppermute | solution.py:319
  180.9 0.6 all-to-all-done.5.refs_6_
  181.4 1.2 shard_map.110
  (26 shorter events, 0.0 us)
Async XLA Ops:
  9.8 15.4 %all-to-all-start = ((bf16[4,256,128]{2,1,0:T(8,128)(2,1)}), bf16[4,256,128]{2,1,0:T(8,128)(2,1)S(1)}, u32[]{:S(2)}, u32[]{:S(2)}) async-start(bf16[4,256,128]{2,1,0:T(8,128)(2,1)} %shard_map.103), calls=%async_computation | async-start | bytes 524288 | tf_op jit(solution)/shard_map/all_to_all | solution.py:323
  14.8 83.2 %reduce-scatter.2.cloned.1.call-start = ((), (), s32[]{:S(2)}) async-start(), calls=%async_computation.7 | async-start | bytes 2621440 | tf_op jit(solution)/shard_map/reduce_scatter | solution.py:379
  25.3 0.7 copy-start.7
  27.6 15.1 %copy-start.8 = (bf16[2048,128]{1,0:T(8,128)(2,1)S(1)}, bf16[2048,128]{1,0:T(8,128)(2,1)}, u32[]{:S(2)}) copy-start(bf16[2048,128]{1,0:T(8,128)(2,1)} %get-tuple-element.37) | copy-start | bytes 1572868
  27.6 35.8 %copy-start.2 = (s32[18,32]{1,0:T(8,128)S(1)}, s32[18,32]{1,0:T(8,128)}, u32[]{:S(2)}) copy-start(s32[18,32]{1,0:T(8,128)} %refs_1_.8) | copy-start | bytes 6916
  27.6 35.8 %copy-start.3 = (s32[4]{0:T(128)S(1)}, s32[4]{0:T(128)}, u32[]{:S(2)}) copy-start(s32[4]{0:T(128)} %pad_add_fusion.refs_0_) | copy-start | bytes 52
  27.6 47.8 %copy-start.9 = (bf16[2048,128]{1,0:T(8,128)(2,1)S(1)}, bf16[2048,128]{1,0:T(8,128)(2,1)}, u32[]{:S(2)}) copy-start(bf16[2048,128]{1,0:T(8,128)(2,1)} %get-tuple-element.38) | copy-start | bytes 1572868
  27.6 52.2 %copy-start.10 = (bf16[2048,128]{1,0:T(8,128)(2,1)S(1)}, bf16[2048,128]{1,0:T(8,128)(2,1)}, u32[]{:S(2)}) copy-start(bf16[2048,128]{1,0:T(8,128)(2,1)} %get-tuple-element.39) | copy-start | bytes 1572868
  27.7 35.8 %all-to-all-start.1 = ((bf16[16,4,16,128]{3,2,1,0:T(8,128)(2,1)}), bf16[16,4,16,128]{3,2,1,0:T(8,128)(2,1)S(1)}, u32[]{:S(2)}, u32[]{:S(2)}) async-start(bf16[16,4,16,128]{3,2,1,0:T(8,128)(2,1)} %get-tuple-element.41), calls=%async_computation.2 | async-start | bytes 524288 | tf_op jit(solution)/shard_map/all_to_all | solution.py:323
  42.8 20.7 %collective-permute-start = (bf16[2048,128]{1,0:T(8,128)(2,1)S(1)}, bf16[2048,128]{1,0:T(8,128)(2,1)S(1)}, u32[]{:S(2)}, u32[]{:S(2)}) collective-permute-start(bf16[2048,128]{1,0:T(8,128)(2,1)S(1)} %copy-done.8), channel_id=1, source_target_pairs={{0,16},{16,32},{32,48},{48,0},{1,17},{17,33},{33,49},{49,1},{2,18}... | collective-permute-start | bytes 1572872 | tf_op jit(solution)/shard_map/ppermute | solution.py:319
  63.4 34.6 %copy-start = (bf16[2048,128]{1,0:T(8,128)(2,1)}, bf16[2048,128]{1,0:T(8,128)(2,1)S(1)}, u32[]{:S(2)}) copy-start(bf16[2048,128]{1,0:T(8,128)(2,1)S(1)} %collective-permute-done.refs_3_.refs_2_) | copy-start | bytes 1572868
  65.1 33.0 %all-to-all-start.2 = ((bf16[16,4,16,128]{3,2,1,0:T(8,128)(2,1)}), bf16[16,4,16,128]{3,2,1,0:T(8,128)(2,1)S(1)}, u32[]{:S(2)}, u32[]{:S(2)}) async-start(bf16[16,4,16,128]{3,2,1,0:T(8,128)(2,1)} %shard_map.105), calls=%async_computation.3 | async-start | bytes 524288 | tf_op jit(solution)/shard_map/all_to_all | solution.py:323
  75.4 11.4 %collective-permute-start.1 = (bf16[2048,128]{1,0:T(8,128)(2,1)S(1)}, bf16[2048,128]{1,0:T(8,128)(2,1)S(1)}, u32[]{:S(2)}, u32[]{:S(2)}) collective-permute-start(bf16[2048,128]{1,0:T(8,128)(2,1)S(1)} %copy-done.9), channel_id=1, source_target_pairs={{0,32},{16,48},{32,0},{48,16},{1,33},{17,49},{33,1},{49,17},{2,34}... | collective-permute-start | bytes 1572872 | tf_op jit(solution)/shard_map/ppermute | solution.py:319
  79.9 18.1 %collective-permute-start.2 = (bf16[2048,128]{1,0:T(8,128)(2,1)S(1)}, bf16[2048,128]{1,0:T(8,128)(2,1)S(1)}, u32[]{:S(2)}, u32[]{:S(2)}) collective-permute-start(bf16[2048,128]{1,0:T(8,128)(2,1)S(1)} %copy-done.10), channel_id=1, source_target_pairs={{0,48},{16,0},{32,16},{48,32},{1,49},{17,1},{33,17},{49,33},{2,50}... | collective-permute-start | bytes 1572872 | tf_op jit(solution)/shard_map/ppermute | solution.py:319
  86.8 11.2 %copy-start.11 = (bf16[2048,128]{1,0:T(8,128)(2,1)}, bf16[2048,128]{1,0:T(8,128)(2,1)S(1)}, u32[]{:S(2)}) copy-start(bf16[2048,128]{1,0:T(8,128)(2,1)S(1)} %collective-permute-done.1.refs_3_) | copy-start | bytes 1572868
  98.0 0.8 copy-start.12
  98.0 0.9 copy-start.6
  103.0 33.9 %all-to-all-start.3 = ((bf16[16,128,128]{2,1,0:T(8,128)(2,1)}), bf16[16,128,128]{2,1,0:T(8,128)(2,1)S(1)}, u32[]{:S(2)}, u32[]{:S(2)}) async-start(bf16[16,128,128]{2,1,0:T(8,128)(2,1)} %get-tuple-element.49), calls=%async_computation.4 | async-start | bytes 1048576 | tf_op jit(solution)/shard_map/all_to_all | solution.py:323
  114.2 45.4 %copy-start.4 = (s32[4]{0:T(128)S(1)}, s32[4]{0:T(128)}, u32[]{:S(2)}) copy-start(s32[4]{0:T(128)} %pad_add_fusion.refs_0_) | copy-start | bytes 52
  114.2 67.3 %copy-start.1 = (f32[32,512]{1,0:T(8,128)S(1)}, f32[32,512]{1,0:T(8,128)}, u32[]{:S(2)}) copy-start(f32[32,512]{1,0:T(8,128)} %refs_1_.9) | copy-start | bytes 196612
  114.2 11.8 %collective-permute-start.3 = (bf16[16,16,128]{2,1,0:T(8,128)(2,1)}, bf16[16,16,128]{2,1,0:T(8,128)(2,1)S(1)}, u32[]{:S(2)}, u32[]{:S(2)}) collective-permute-start(bf16[16,16,128]{2,1,0:T(8,128)(2,1)} %get-tuple-element.43), channel_id=1, source_target_pairs={{0,16},{16,32},{32,48},{48,0},{1,17},{17,33},{33,49},{49,1},{2,18}... | collective-permute-start | bytes 196616 | tf_op jit(solution)/shard_map/ppermute | solution.py:319
  119.7 6.7 %collective-permute-start.4 = (bf16[16,16,128]{2,1,0:T(8,128)(2,1)}, bf16[16,16,128]{2,1,0:T(8,128)(2,1)S(1)}, u32[]{:S(2)}, u32[]{:S(2)}) collective-permute-start(bf16[16,16,128]{2,1,0:T(8,128)(2,1)} %get-tuple-element.44), channel_id=1, source_target_pairs={{0,32},{16,48},{32,0},{48,16},{1,33},{17,49},{33,1},{49,17},{2,34}... | collective-permute-start | bytes 196616 | tf_op jit(solution)/shard_map/ppermute | solution.py:319
  122.9 5.5 %collective-permute-start.5 = (bf16[16,16,128]{2,1,0:T(8,128)(2,1)}, bf16[16,16,128]{2,1,0:T(8,128)(2,1)S(1)}, u32[]{:S(2)}, u32[]{:S(2)}) collective-permute-start(bf16[16,16,128]{2,1,0:T(8,128)(2,1)} %get-tuple-element.45), channel_id=1, source_target_pairs={{0,48},{16,0},{32,16},{48,32},{1,49},{17,1},{33,17},{49,33},{2,50}... | collective-permute-start | bytes 196616 | tf_op jit(solution)/shard_map/ppermute | solution.py:319
  126.0 2.4 %copy-start.13 = (bf16[16,16,128]{2,1,0:T(8,128)(2,1)}, bf16[16,16,128]{2,1,0:T(8,128)(2,1)S(1)}, u32[]{:S(2)}) copy-start(bf16[16,16,128]{2,1,0:T(8,128)(2,1)S(1)} %collective-permute-done.3.refs_8_) | copy-start | bytes 196612
  126.5 2.0 %copy-start.14 = (bf16[16,16,128]{2,1,0:T(8,128)(2,1)}, bf16[16,16,128]{2,1,0:T(8,128)(2,1)S(1)}, u32[]{:S(2)}) copy-start(bf16[16,16,128]{2,1,0:T(8,128)(2,1)S(1)} %collective-permute-done.4.refs_9_) | copy-start | bytes 196612
  128.4 0.6 copy-start.15
  136.9 0.7 copy-start.5
  160.8 20.7 %all-to-all-start.5 = ((f32[16,1,128]{2,1,0:T(1,128)}), f32[16,1,128]{2,1,0:T(1,128)S(1)}, u32[]{:S(2)}, u32[]{:S(2)}) async-start(f32[16,1,128]{2,1,0:T(1,128)} %get-tuple-element.57), calls=%async_computation.6 | async-start | bytes 16384 | tf_op jit(solution)/shard_map/all_to_all | solution.py:323
  170.2 8.7 %collective-permute-start.6 = (f32[32,128]{1,0:T(8,128)S(1)}, f32[32,128]{1,0:T(8,128)S(1)}, u32[]{:S(2)}, u32[]{:S(2)}) collective-permute-start(f32[32,128]{1,0:T(8,128)S(1)} %get-tuple-element.54), channel_id=1, source_target_pairs={{0,16},{16,32},{32,48},{48,0},{1,17},{17,33},{33,49},{49,1},{2,18}... | collective-permute-start | bytes 49160 | tf_op jit(solution)/shard_map/ppermute | solution.py:319
  172.4 6.5 %collective-permute-start.7 = (f32[32,128]{1,0:T(8,128)S(1)}, f32[32,128]{1,0:T(8,128)S(1)}, u32[]{:S(2)}, u32[]{:S(2)}) collective-permute-start(f32[32,128]{1,0:T(8,128)S(1)} %get-tuple-element.55), channel_id=1, source_target_pairs={{0,32},{16,48},{32,0},{48,16},{1,33},{17,49},{33,1},{49,17},{2,34}... | collective-permute-start | bytes 49160 | tf_op jit(solution)/shard_map/ppermute | solution.py:319
  176.1 4.8 %collective-permute-start.8 = (f32[32,128]{1,0:T(8,128)S(1)}, f32[32,128]{1,0:T(8,128)S(1)}, u32[]{:S(2)}, u32[]{:S(2)}) collective-permute-start(f32[32,128]{1,0:T(8,128)S(1)} %get-tuple-element.56), channel_id=1, source_target_pairs={{0,48},{16,0},{32,16},{48,32},{1,49},{17,1},{33,17},{49,33},{2,50}... | collective-permute-start | bytes 49160 | tf_op jit(solution)/shard_map/ppermute | solution.py:319
Sparse Core Ops, SparseCore 0:
  27.8 49.9 reduce-scatter.1

commit v4 on v3

--- a/solution.py
+++ b/solution.py
@@ -133,9 +133,10 @@
 
 
 def local_kernel(info_ref, weight_ref, q_hbm, k_hbm, g_hbm, x_hbm, loc_ref, proj_hbm, *refs):
-    keyed_hbm = refs[:-8]
-    q_ref, k_ref, g_ref, x_ref, right_ref, done_ref, in_sems, out_sems = refs[-8:]
+    keyed_hbm = refs[:-9]
+    q_ref, k_ref, g_ref, x_ref, right_ref, done_ref, summed_ref, in_sems, out_sems = refs[-9:]
     n_y = len(keyed_hbm)
+    nz, each = summed_ref.shape[1], summed_ref.shape[3]
     width = k_ref.shape[1]
     chunks, _, chunk = x_ref.shape
     moves = start_all(
@@ -166,11 +167,13 @@
         moves[3 + c].wait()
         part = pl.ds(c * chunk, chunk)
         res = dot(x_ref[c], right_ref[...], 0, 0).astype(bf16)
-        for n in range(2 * n_y):
+        for n in range(n_y):
             done_ref[c, n, :, :] = res[:, lanes(n)]
+            for z in range(nz):
+                summed_ref[c, z, n, :, :] = res[z * each : (z + 1) * each, lanes(n_y + n)]
         sent += start_all(
             [(done_ref.at[c, n], keyed_hbm[n].at[part, :]) for n in range(n_y)]
-            + [(done_ref.at[c, pl.ds(n_y, n_y)], proj_hbm.at[:, part, :])],
+            + [(summed_ref.at[c], proj_hbm.at[:, :, pl.ds(c * each, each), :])],
             out_sems.at[c],
         )
     for move in sent:
@@ -208,21 +211,19 @@
         out_ref[c % nz, c // nz] = total[c].astype(bf16)
 
 
-def project_kernel(info_ref, a0, a1, a2, a3, loc_hbm, r_hbm, out_hbm, *refs):
-    own_hbm = refs[:-8]
-    a_ref, loc_ref, r_ref, done_ref, r_sem, a_sems, out_sems, own_sems = refs[-8:]
+def project_kernel(info_ref, a0, a1, a2, a3, r_hbm, out_hbm, *refs):
+    own_hbm = refs[:-7]
+    a_ref, r_ref, done_ref, r_sem, a_sems, out_sems, own_sems = refs[-7:]
     keyed = (a0, a1, a2, a3)
     n_y = len(keyed)
-    chunks, rows = loc_ref.shape[:2]
+    chunks, _, rows = a_ref.shape[:3]
     got = start_all([(r_hbm, r_ref)], r_sem)
     moves = []
     for c in range(chunks):
         part = pl.ds(c * rows, rows)
         moves.append(
             start_all(
-                [(keyed[n].at[part, :], a_ref.at[c, n]) for n in range(n_y)]
-                + [(loc_hbm.at[part, :], loc_ref.at[c])],
-                a_sems.at[c],
+                [(keyed[n].at[part, :], a_ref.at[c, n]) for n in range(n_y)], a_sems.at[c]
             )
         )
     y = info_ref[1]
@@ -237,7 +238,7 @@
         for move in moves[c]:
             move.wait()
         left = jnp.concatenate([a_ref[c, n] for n in range(n_y)], axis=1)
-        res = (loc_ref[c].astype(f32) + dot(left, states, 1, 0)).astype(bf16)
+        res = dot(left, states, 1, 0).astype(bf16)
         inner = rows // (nz * each)
         for b in range(inner):
             for z in range(nz):
@@ -285,23 +286,24 @@
             dk_ref[rows, s] = (base_k[rows] + dot(dmix_t, query[i * D :], 1, 0)).astype(bf16)
 
 
-def shard_kernel(in_ref, out_ref, square_ref):
-    total = in_ref[0].astype(f32)
-    for z in range(1, in_ref.shape[0]):
+def shard_kernel(info_ref, in_ref, loc_ref, square_ref, *refs):
+    part_refs, total_ref = refs[:-1], refs[-1]
+    n_y = len(part_refs)
+    rows = part_refs[0].shape[0]
+    total = loc_ref[...].astype(f32)
+    for z in range(in_ref.shape[0]):
         total = total + in_ref[z].astype(f32)
-    out_ref[...] = total
+    total_ref[...] = total
     square = jnp.sum(jnp.sum(total * total, axis=0, keepdims=True), axis=1, keepdims=True)
     square_ref[...] = jnp.broadcast_to(square[None], square_ref.shape)
-
-
-def stage_kernel(info_ref, square_ref, shard_ref, out_ref, *part_refs):
-    n_y = len(part_refs)
-    rows = part_refs[0].shape[0]
+    for n in range(n_y):
+        first = pl.multiple_of(lax.rem(info_ref[1] + n, n_y) * rows, rows)
+        part_refs[n][...] = total_ref[pl.ds(first, rows), :]
+
+
+def stage_kernel(square_ref, out_ref):
     square = jnp.sum(square_ref[...], axis=0, keepdims=True)
     out_ref[...] = jnp.broadcast_to(square, out_ref.shape)
-    for n in range(n_y):
-        first = pl.multiple_of(lax.rem(info_ref[1] + n, n_y) * rows, rows)
-        part_refs[n][...] = shard_ref[pl.ds(first, rows), :]
 
 
 def final_kernel(info_ref, mom_ref, p0, p1, p2, p3, total_ref, out_ref):
@@ -349,7 +351,7 @@
     chunks = features // chunk
     local, proj, *keyed = call(
         local_kernel,
-        (sds((length, width), f32), sds((heads, features, D), bf16))
+        (sds((length, width), f32), sds((n_z, heads, features // n_z, D), bf16))
         + tuple(sds((features, D), bf16) for _ in range(n_y)),
         (queries, keys, out_grad, inputs),
         4 * length * width * features + 3 * length * length * width,
@@ -359,7 +361,8 @@
         + [
             pltpu.VMEM((chunks, length, chunk), bf16),
             pltpu.VMEM((length, 2 * width), bf16),
-            pltpu.VMEM((chunks, 2 * n_y, chunk, D), bf16),
+            pltpu.VMEM((chunks, n_y, chunk, D), bf16),
+            pltpu.VMEM((chunks, n_z, heads, chunk // n_z, D), bf16),
             dma((3 + chunks,)),
             dma((chunks, n_y + 1)),
         ],
@@ -376,9 +379,9 @@
     )
     both = swap(both, Z)
     keyed = [keyed[0]] + [shift(keyed[n], Y, n) for n in range(1, n_y)]
-    proj = lax.psum_scatter(
-        proj.reshape(heads * features, D), Y, scatter_dimension=0, tiled=True
-    )
+    proj = proj.reshape(heads * features, D)
+    for axis in (Z, Y):
+        proj = lax.psum_scatter(proj, axis, scatter_dimension=0, tiled=True)
 
     both = call(
         tree_kernel,
@@ -386,7 +389,7 @@
         (both,),
         1 << 21,
         scalars=(info, level_weight),
-        after=(keyed[1],),
+        after=(keyed[1], keyed[3]),
         vmem=8,
     )
     both = swap(both, Z)
@@ -396,17 +399,16 @@
         project_kernel,
         (sds((n_z, features // n_z, D), bf16),)
         + tuple(sds((n_z, 2 * D // n_z, D), bf16) for _ in range(n_y)),
-        (*keyed, proj, both),
+        (*keyed, both),
         2 * features * n_y * D * D,
-        [ANY] * (n_y + 2),
+        [ANY] * (n_y + 1),
         (ANY,) * (n_y + 1),
         scratch=[
             pltpu.VMEM((2, n_y, rows, D), bf16),
-            pltpu.VMEM((2, rows, D), bf16),
             pltpu.VMEM(both.shape, bf16),
             pltpu.VMEM((2, n_z, rows // n_z, D), bf16),
             dma((1,)),
-            dma((2, n_y + 1)),
+            dma((2, n_y)),
             dma((2,)),
             dma((n_y,)),
         ],
@@ -427,25 +429,27 @@
 
     near, rest = HEAD + (Y,), (Z,)
     rows = momentum.shape[0]
-    shard, square = call(
+    square, *mine = call(
         shard_kernel,
-        (sds((n_y * rows, D), f32), sds((lax.axis_size(near), 1, D), f32)),
-        (parts,),
+        (sds((lax.axis_size(near), 1, D), f32),) + (sds((rows, D), f32),) * n_y,
+        (parts, proj),
         1 << 20,
+        scratch=[pltpu.VMEM((n_y * rows, D), f32)],
+        scalars=(info,),
         after=(end,),
         vmem=8,
     )
+    mine = [mine[0]] + [shift(mine[n], Y, n) for n in range(1, n_y)]
     square = swap(square, near)
-    total, *mine = call(
+    total = call(
         stage_kernel,
-        (sds((lax.axis_size(rest), 1, D), f32),) + tuple(sds((rows, D), f32) for _ in range(n_y)),
-        (square, shard),
+        sds((lax.axis_size(rest), 1, D), f32),
+        (square,),
         1 << 16,
-        scalars=(info,),
+        after=(mine[1],),
         vmem=8,
     )
     total = swap(total, rest)
-    mine = [mine[0]] + [shift(mine[n], Y, n) for n in range(1, n_y)]
     new_momentum = call(
         final_kernel,
         sds(momentum.shape, f32),

time: 191 us -> 207 us (1.084)
  waiting for transfers between devices: 37.6 us -> 57.8 us
  blocking collectives: 21.9 us -> 16.7 us
    reduce_scatter x1 -> x2, waiting for transfers between devices: 0.01 us -> 27.7 us  [body(): proj = lax.psum_scatter(proj, axis, scatter_dimension=0, tiled=True)]
    ppermute x9, waiting for transfers between devices: 37 us -> 23.7 us  [shift(): return lax.ppermute(x, axis, [(i, (i + by) % n) for i in range(n)])]
    all_to_all x5, waiting for transfers between devices: 0.59 us -> 6.34 us  [swap(): return lax.all_to_all(x, axes, 0, 0, tiled=True)]
    all_to_all x1, blocking collectives: 21.9 us -> 16.7 us  [swap(): return lax.all_to_all(x, axes, 0, 0, tiled=True)]
    all_to_all x5, starting transfers between devices: 51.1 us -> 53.4 us  [swap(): return lax.all_to_all(x, axes, 0, 0, tiled=True)]
  transfers between devices with their start and end apart: 15 -> 16, of which waited for: 7 -> 9; matrix products, arithmetic and copies ran while one was open for 0% -> 0% of each run, Pallas kernels for 10% -> 11%
where the time goes in v4:
time: 207 us; the launch traced here: 206 us
  starting transfers between devices  83.1 us (40%)
  waiting for transfers between devices  57.8 us (28%)
  Pallas kernels  30.3 us (15%)
  blocking collectives  16.7 us (8%)
  between operations  14.3 us (7%)
  local copies, waits for them, and re-layouts  3.49 us (2%)
    all_to_all x5, starting transfers between devices, swap(): return lax.all_to_all(x, axes, 0, 0, tiled=True)  53.4 us
    pallas_call x9, Pallas kernels, call(): pl.pallas_call(run, out_shape=out_shape, grid_spec=pltpu.PrefetchScalarGr...  30.3 us
    ppermute x9, starting transfers between devices, shift(): return lax.ppermute(x, axis, [(i, (i + by) % n) for i in range(n)])  29.7 us
    reduce_scatter x2, waiting for transfers between devices, body(): proj = lax.psum_scatter(proj, axis, scatter_dimension=0, tiled=True)  27.7 us
    ppermute x9, waiting for transfers between devices, shift(): return lax.ppermute(x, axis, [(i, (i + by) % n) for i in range(n)])  23.7 us
    all_to_all x1, blocking collectives, swap(): return lax.all_to_all(x, axes, 0, 0, tiled=True)  16.7 us
    all_to_all x5, waiting for transfers between devices, swap(): return lax.all_to_all(x, axes, 0, 0, tiled=True)  6.34 us
  transfers between devices with their start and end apart: 16, of which 9 were waited for; matrix products, arithmetic and copies ran while one was open for 0% of the time, Pallas kernels for 11%

profile of v4, /device:TPU:1, one launch (start us, length us, event | category | flops | bytes accessed | tf_op | source)
XLA Modules:
  0.0 206.3 jit_solution(17122472074338846291)
XLA Ops:
  7.2 2.6 %shard_map.103 = bf16[4,256,128]{2,1,0:T(8,128)(2,1)} custom-call(bf16[512,512]{1,0:T(8,128)(2,1)} %refs_2_.5, bf16[512,512]{1,0:T(8,128)(2,1)} %refs_5_.3, bf16[512,512]{1,0:T(8,128)(2,1)} %refs_3_.5, bf16[512,512]{1,0:T(8,128)(2,1)} %refs_4_.3), custom_call_target="tpu_custom_call" | custom-call | flops 134217728 | bytes 2359296 | tf_op jit(solution)/shard_map/pallas_call | solution.py:56
  9.8 5.0 %all-to-all-start = ((bf16[4,256,128]{2,1,0:T(8,128)(2,1)}), bf16[4,256,128]{2,1,0:T(8,128)(2,1)S(1)}, u32[]{:S(2)}, u32[]{:S(2)}) async-start(bf16[4,256,128]{2,1,0:T(8,128)(2,1)} %shard_map.103), calls=%async_computation | async-start | bytes 524288 | tf_op jit(solution)/shard_map/all_to_all | solution.py:325
  14.8 0.6 pad_add_fusion.refs_0_
  15.4 9.6 %shard_map.102 = (f32[512,512]{1,0:T(8,128)}, bf16[16,4,128,128]{3,2,1,0:T(8,128)(2,1)}, bf16[2048,128]{1,0:T(8,128)(2,1)}, bf16[2048,128]{1,0:T(8,128)(2,1)}, b...) custom-call(s32[4]{0:T(128)} %pad_add_fusion.refs_0_, s32[18,32]{1,0:T(8,128)} %refs_1_.8, bf16[512,512]{1,0:T(8,128)(2,1)} %refs_2_.5, ...), custom_call_target="tpu_custom_call" | custom-call | flops 2550136832 | bytes 8912896 | tf_op jit(solution)/shard_map/pallas_call | solution.py:56
  25.1 0.0 all-to-all-done.refs_0_
  25.1 0.7 copy-done.9
  25.8 1.7 shard_map.104
  27.5 0.0 copy-start.12
  27.5 0.0 reduce-scatter.3.cloned.1.call-update
  27.5 15.1 %all-to-all-start.1 = ((bf16[16,4,16,128]{3,2,1,0:T(8,128)(2,1)}), bf16[16,4,16,128]{3,2,1,0:T(8,128)(2,1)S(1)}, u32[]{:S(2)}, u32[]{:S(2)}) async-start(bf16[16,4,16,128]{3,2,1,0:T(8,128)(2,1)} %get-tuple-element.38), calls=%async_computation.1 | async-start | bytes 524288 | tf_op jit(solution)/shard_map/all_to_all | solution.py:325
  42.6 3.4 %collective-permute-start = (bf16[2048,128]{1,0:T(8,128)(2,1)S(1)}, bf16[2048,128]{1,0:T(8,128)(2,1)S(1)}, u32[]{:S(2)}, u32[]{:S(2)}) collective-permute-start(bf16[2048,128]{1,0:T(8,128)(2,1)S(1)} %copy-done.11), channel_id=1, source_target_pairs={{0,16},{16,32},{32,48},{48,0},{1,17},{17,33},{33,49},{49,1},{2,18}... | collective-permute-start | bytes 1572872 | tf_op jit(solution)/shard_map/ppermute | solution.py:321
  46.0 3.1 %collective-permute-start.2 = (bf16[2048,128]{1,0:T(8,128)(2,1)S(1)}, bf16[2048,128]{1,0:T(8,128)(2,1)S(1)}, u32[]{:S(2)}, u32[]{:S(2)}) collective-permute-start(bf16[2048,128]{1,0:T(8,128)(2,1)S(1)} %copy-done.13), channel_id=1, source_target_pairs={{0,48},{16,0},{32,16},{48,32},{1,49},{17,1},{33,17},{49,33},{2,50}... | collective-permute-start | bytes 1572872 | tf_op jit(solution)/shard_map/ppermute | solution.py:321
  49.1 8.9 %collective-permute-done.refs_3_.refs_2_ = bf16[2048,128]{1,0:T(8,128)(2,1)S(1)} collective-permute-done((bf16[2048,128]{1,0:T(8,128)(2,1)S(1)}, bf16[2048,128]{1,0:T(8,128)(2,1)S(1)}, u32[]{:S(2)}, u32[]{:S(2)}) %collective-permute-start) | collective-permute-done | bytes 524320 | tf_op jit(solution)/shard_map/ppermute | solution.py:321
  58.0 1.6 collective-permute-done.2.refs_4_
  59.6 1.6 shard_map.105
  61.2 11.2 %all-to-all-start.2 = ((bf16[16,4,16,128]{3,2,1,0:T(8,128)(2,1)}), bf16[16,4,16,128]{3,2,1,0:T(8,128)(2,1)S(1)}, u32[]{:S(2)}, u32[]{:S(2)}) async-start(bf16[16,4,16,128]{3,2,1,0:T(8,128)(2,1)} %shard_map.105), calls=%async_computation.2 | async-start | bytes 524288 | tf_op jit(solution)/shard_map/all_to_all | solution.py:325
  72.4 4.3 %collective-permute-start.1 = (bf16[2048,128]{1,0:T(8,128)(2,1)S(1)}, bf16[2048,128]{1,0:T(8,128)(2,1)S(1)}, u32[]{:S(2)}, u32[]{:S(2)}) collective-permute-start(bf16[2048,128]{1,0:T(8,128)(2,1)S(1)} %copy-done.12), channel_id=1, source_target_pairs={{0,32},{16,48},{32,0},{48,16},{1,33},{17,49},{33,1},{49,17},{2,34}... | collective-permute-start | bytes 1572872 | tf_op jit(solution)/shard_map/ppermute | solution.py:321
  76.7 9.3 %collective-permute-done.1.refs_3_ = bf16[2048,128]{1,0:T(8,128)(2,1)S(1)} collective-permute-done((bf16[2048,128]{1,0:T(8,128)(2,1)S(1)}, bf16[2048,128]{1,0:T(8,128)(2,1)S(1)}, u32[]{:S(2)}, u32[]{:S(2)}) %collective-permute-start.1) | collective-permute-done | bytes 524320 | tf_op jit(solution)/shard_map/ppermute | solution.py:321
  86.0 2.6 %all-to-all-done.2.refs_5_ = bf16[16,4,16,128]{3,2,1,0:T(8,128)(2,1)S(1)} async-done(((bf16[16,4,16,128]{3,2,1,0:T(8,128)(2,1)}), bf16[16,4,16,128]{3,2,1,0:T(8,128)(2,1)S(1)}, u32[]{:S(2)}, u32[]{:S(2)}) %all-to-all-start.2) | async-done | bytes 262176 | tf_op jit(solution)/shard_map/all_to_all | solution.py:325
  88.7 0.7 copy-done.8
  89.4 4.4 %shard_map.106 = (bf16[16,128,128]{2,1,0:T(8,128)(2,1)}, bf16[16,16,128]{2,1,0:T(8,128)(2,1)}, bf16[16,16,128]{2,1,0:T(8,128)(2,1)}, bf16[16,16,128]{2,1,0:T(8,128)(2,1)}, bf16[16,16,128]{2,1,0:T(8,128)(2,1)}) custom-call(s32[4]{0:T(128)} %pad_add_fusion.refs_0_, bf16[2048,128]{1,0:T(8,128)(2,1)} %get-tuple-element.30.refs_1_, bf16[2048,128]{1,0:T(8,128)(2,1)} %copy-done, ...), custom_call_target="tpu_custom_call" | custom-call | flops 268435456 | bytes 3145728 | tf_op jit(solution)/shard_map/pallas_call | solution.py:56
  93.8 10.1 %all-to-all-start.3 = ((bf16[16,128,128]{2,1,0:T(8,128)(2,1)}), bf16[16,128,128]{2,1,0:T(8,128)(2,1)S(1)}, u32[]{:S(2)}, u32[]{:S(2)}) async-start(bf16[16,128,128]{2,1,0:T(8,128)(2,1)} %get-tuple-element.46), calls=%async_computation.3 | async-start | bytes 1048576 | tf_op jit(solution)/shard_map/all_to_all | solution.py:325
  104.0 0.0 reduce-scatter.5.cloned.1.call-start
  104.0 3.5 %reduce-scatter.3.cloned.1.call-done = bf16[512,128]{1,0:T(8,128)(2,1)} async-done(((bf16[8192,128]{1,0:T(8,128)(2,1)}), bf16[512,128]{1,0:T(8,128)(2,1)}) %reduce-scatter.3.cloned.1.call-update) | async-done | bytes 131088 | tf_op jit(solution)/shard_map/reduce_scatter | solution.py:384
  107.5 0.0 reduce-scatter.5.cloned.1.call-update
  107.5 2.9 %collective-permute-start.3 = (bf16[16,16,128]{2,1,0:T(8,128)(2,1)}, bf16[16,16,128]{2,1,0:T(8,128)(2,1)S(1)}, u32[]{:S(2)}, u32[]{:S(2)}) collective-permute-start(bf16[16,16,128]{2,1,0:T(8,128)(2,1)} %get-tuple-element.40), channel_id=1, source_target_pairs={{0,16},{16,32},{32,48},{48,0},{1,17},{17,33},{33,49},{49,1},{2,18}... | collective-permute-start | bytes 196616 | tf_op jit(solution)/shard_map/ppermute | solution.py:321
  110.4 4.9 %collective-permute-start.4 = (bf16[16,16,128]{2,1,0:T(8,128)(2,1)}, bf16[16,16,128]{2,1,0:T(8,128)(2,1)S(1)}, u32[]{:S(2)}, u32[]{:S(2)}) collective-permute-start(bf16[16,16,128]{2,1,0:T(8,128)(2,1)} %get-tuple-element.41), channel_id=1, source_target_pairs={{0,32},{16,48},{32,0},{48,16},{1,33},{17,49},{33,1},{49,17},{2,34}... | collective-permute-start | bytes 196616 | tf_op jit(solution)/shard_map/ppermute | solution.py:321
  115.3 2.7 %collective-permute-start.5 = (bf16[16,16,128]{2,1,0:T(8,128)(2,1)}, bf16[16,16,128]{2,1,0:T(8,128)(2,1)S(1)}, u32[]{:S(2)}, u32[]{:S(2)}) collective-permute-start(bf16[16,16,128]{2,1,0:T(8,128)(2,1)} %get-tuple-element.42), channel_id=1, source_target_pairs={{0,48},{16,0},{32,16},{48,32},{1,49},{17,1},{33,17},{49,33},{2,50}... | collective-permute-start | bytes 196616 | tf_op jit(solution)/shard_map/ppermute | solution.py:321
  118.0 0.0 collective-permute-done.3.refs_8_
  118.0 0.0 collective-permute-done.4.refs_9_
  118.1 2.9 %collective-permute-done.5.refs_10_ = bf16[16,16,128]{2,1,0:T(8,128)(2,1)S(1)} collective-permute-done((bf16[16,16,128]{2,1,0:T(8,128)(2,1)}, bf16[16,16,128]{2,1,0:T(8,128)(2,1)S(1)}, u32[]{:S(2)}, u32[]{:S(2)}) %collective-permute-start.5) | collective-permute-done | bytes 65568 | tf_op jit(solution)/shard_map/ppermute | solution.py:321
  120.9 0.6 copy-done.16
  121.6 7.8 %shard_map.107 = (bf16[512,512]{1,0:T(8,128)(2,1)}, bf16[512,512]{1,0:T(8,128)(2,1)}, bf16[512,512]{1,0:T(8,128)(2,1)}, f32[8,128]{1,0:T(8,128)}) custom-call(s32[4]{0:T(128)} %pad_add_fusion.refs_0_, s32[18,32]{1,0:T(8,128)} %refs_1_.8, bf16[512,512]{1,0:T(8,128)(2,1)} %refs_2_.5, bf16[512,512]{1,0:T(8,128)(2,1)} %refs_3_.5, bf16[512,512]{1,0:T(8,128)(2,1)} %refs_4_.3, ...), custom_call_target="tpu_custom_call" | custom-call | flops 805306368 | bytes 4984832 | tf_op jit(solution)/shard_map/pallas_call | solution.py:56
  129.4 0.0 all-to-all-done.3.refs_1_
  129.4 24.2 %reduce-scatter.5.cloned.1.call-done.refs_2_ = bf16[128,128]{1,0:T(8,128)(2,1)} async-done(((bf16[512,128]{1,0:T(8,128)(2,1)}), bf16[128,128]{1,0:T(8,128)(2,1)}) %reduce-scatter.5.cloned.1.call-update) | async-done | bytes 32784 | tf_op jit(solution)/shard_map/reduce_scatter | solution.py:384
  153.6 0.8 copy-done.4
  154.3 0.7 copy-done.7
  155.0 0.7 shard_map.108
  155.7 1.9 collective-permute-start.6
  157.7 16.7 %all_to_all.30.refs_0_ = f32[32,1,128]{2,1,0:T(1,128)S(1)} all-to-all(f32[32,1,128]{2,1,0:T(1,128)S(1)} %get-tuple-element.53), channel_id=1, replica_groups=mesh['head_0'=4,'head_1'=2,'seq_0'=4,'seq_1'=16] {'head_0','head_1','seq..., dimensions={0} | all-to-all | bytes 32768 | tf_op jit(solution)/shard_map/all_to_all | solution.py:325
  174.3 0.0 collective-permute-done.6.refs_1_.refs_3_
  174.3 0.6 shard_map.109
  175.0 12.0 %all-to-all-start.5 = ((f32[16,1,128]{2,1,0:T(1,128)}), f32[16,1,128]{2,1,0:T(1,128)S(1)}, u32[]{:S(2)}, u32[]{:S(2)}) async-start(f32[16,1,128]{2,1,0:T(1,128)} %shard_map.109), calls=%async_computation.7 | async-start | bytes 16384 | tf_op jit(solution)/shard_map/all_to_all | solution.py:325
  187.0 2.8 %collective-permute-start.7 = (f32[32,128]{1,0:T(8,128)S(1)}, f32[32,128]{1,0:T(8,128)S(1)}, u32[]{:S(2)}, u32[]{:S(2)}) collective-permute-start(f32[32,128]{1,0:T(8,128)S(1)} %get-tuple-element.51), channel_id=1, source_target_pairs={{0,32},{16,48},{32,0},{48,16},{1,33},{17,49},{33,1},{49,17},{2,34}... | collective-permute-start | bytes 49160 | tf_op jit(solution)/shard_map/ppermute | solution.py:321
  189.7 3.8 %collective-permute-start.8 = (f32[32,128]{1,0:T(8,128)S(1)}, f32[32,128]{1,0:T(8,128)S(1)}, u32[]{:S(2)}, u32[]{:S(2)}) collective-permute-start(f32[32,128]{1,0:T(8,128)S(1)} %get-tuple-element.52), channel_id=1, source_target_pairs={{0,48},{16,0},{32,16},{48,32},{1,49},{17,1},{33,17},{49,33},{2,50}... | collective-permute-start | bytes 49160 | tf_op jit(solution)/shard_map/ppermute | solution.py:321
  193.5 1.0 collective-permute-done.8.refs_5_
  194.5 3.7 %all-to-all-done.5.refs_6_ = f32[16,1,128]{2,1,0:T(1,128)S(1)} async-done(((f32[16,1,128]{2,1,0:T(1,128)}), f32[16,1,128]{2,1,0:T(1,128)S(1)}, u32[]{:S(2)}, u32[]{:S(2)}) %all-to-all-start.5) | async-done | bytes 8224 | tf_op jit(solution)/shard_map/all_to_all | solution.py:325
  198.2 1.2 shard_map.110
  (31 shorter events, 0.1 us)
Async XLA Ops:
  9.8 15.3 %all-to-all-start = ((bf16[4,256,128]{2,1,0:T(8,128)(2,1)}), bf16[4,256,128]{2,1,0:T(8,128)(2,1)S(1)}, u32[]{:S(2)}, u32[]{:S(2)}) async-start(bf16[4,256,128]{2,1,0:T(8,128)(2,1)} %shard_map.103), calls=%async_computation | async-start | bytes 524288 | tf_op jit(solution)/shard_map/all_to_all | solution.py:325
  14.8 92.7 %reduce-scatter.3.cloned.1.call-start = ((), (), s32[]{:S(2)}) async-start(), calls=%async_computation.8 | async-start | bytes 2228224 | tf_op jit(solution)/shard_map/reduce_scatter | solution.py:384
  25.1 0.7 copy-start.9
  27.4 15.1 %copy-start.11 = (bf16[2048,128]{1,0:T(8,128)(2,1)S(1)}, bf16[2048,128]{1,0:T(8,128)(2,1)}, u32[]{:S(2)}) copy-start(bf16[2048,128]{1,0:T(8,128)(2,1)} %get-tuple-element.35) | copy-start | bytes 1572868
  27.4 18.5 %copy-start.13 = (bf16[2048,128]{1,0:T(8,128)(2,1)S(1)}, bf16[2048,128]{1,0:T(8,128)(2,1)}, u32[]{:S(2)}) copy-start(bf16[2048,128]{1,0:T(8,128)(2,1)} %get-tuple-element.37) | copy-start | bytes 1572868
  27.4 32.1 %copy-start.3 = (s32[18,32]{1,0:T(8,128)S(1)}, s32[18,32]{1,0:T(8,128)}, u32[]{:S(2)}) copy-start(s32[18,32]{1,0:T(8,128)} %refs_1_.8) | copy-start | bytes 6916
  27.4 32.1 %copy-start.5 = (s32[4]{0:T(128)S(1)}, s32[4]{0:T(128)}, u32[]{:S(2)}) copy-start(s32[4]{0:T(128)} %pad_add_fusion.refs_0_) | copy-start | bytes 52
  27.5 44.9 %copy-start.12 = (bf16[2048,128]{1,0:T(8,128)(2,1)S(1)}, bf16[2048,128]{1,0:T(8,128)(2,1)}, u32[]{:S(2)}) copy-start(bf16[2048,128]{1,0:T(8,128)(2,1)} %get-tuple-element.36) | copy-start | bytes 1572868
  27.5 32.1 %all-to-all-start.1 = ((bf16[16,4,16,128]{3,2,1,0:T(8,128)(2,1)}), bf16[16,4,16,128]{3,2,1,0:T(8,128)(2,1)S(1)}, u32[]{:S(2)}, u32[]{:S(2)}) async-start(bf16[16,4,16,128]{3,2,1,0:T(8,128)(2,1)} %get-tuple-element.38), calls=%async_computation.1 | async-start | bytes 524288 | tf_op jit(solution)/shard_map/all_to_all | solution.py:325
  42.6 15.4 %collective-permute-start = (bf16[2048,128]{1,0:T(8,128)(2,1)S(1)}, bf16[2048,128]{1,0:T(8,128)(2,1)S(1)}, u32[]{:S(2)}, u32[]{:S(2)}) collective-permute-start(bf16[2048,128]{1,0:T(8,128)(2,1)S(1)} %copy-done.11), channel_id=1, source_target_pairs={{0,16},{16,32},{32,48},{48,0},{1,17},{17,33},{33,49},{49,1},{2,18}... | collective-permute-start | bytes 1572872 | tf_op jit(solution)/shard_map/ppermute | solution.py:321
  46.0 13.6 %collective-permute-start.2 = (bf16[2048,128]{1,0:T(8,128)(2,1)S(1)}, bf16[2048,128]{1,0:T(8,128)(2,1)S(1)}, u32[]{:S(2)}, u32[]{:S(2)}) collective-permute-start(bf16[2048,128]{1,0:T(8,128)(2,1)S(1)} %copy-done.13), channel_id=1, source_target_pairs={{0,48},{16,0},{32,16},{48,32},{1,49},{17,1},{33,17},{49,33},{2,50}... | collective-permute-start | bytes 1572872 | tf_op jit(solution)/shard_map/ppermute | solution.py:321
  58.0 30.7 %copy-start = (bf16[2048,128]{1,0:T(8,128)(2,1)}, bf16[2048,128]{1,0:T(8,128)(2,1)S(1)}, u32[]{:S(2)}) copy-start(bf16[2048,128]{1,0:T(8,128)(2,1)S(1)} %collective-permute-done.refs_3_.refs_2_) | copy-start | bytes 1572868
  59.6 29.1 %copy-start.1 = (bf16[2048,128]{1,0:T(8,128)(2,1)}, bf16[2048,128]{1,0:T(8,128)(2,1)S(1)}, u32[]{:S(2)}) copy-start(bf16[2048,128]{1,0:T(8,128)(2,1)S(1)} %collective-permute-done.2.refs_4_) | copy-start | bytes 1572868
  61.2 27.5 %all-to-all-start.2 = ((bf16[16,4,16,128]{3,2,1,0:T(8,128)(2,1)}), bf16[16,4,16,128]{3,2,1,0:T(8,128)(2,1)S(1)}, u32[]{:S(2)}, u32[]{:S(2)}) async-start(bf16[16,4,16,128]{3,2,1,0:T(8,128)(2,1)} %shard_map.105), calls=%async_computation.2 | async-start | bytes 524288 | tf_op jit(solution)/shard_map/all_to_all | solution.py:325
  72.4 13.6 %collective-permute-start.1 = (bf16[2048,128]{1,0:T(8,128)(2,1)S(1)}, bf16[2048,128]{1,0:T(8,128)(2,1)S(1)}, u32[]{:S(2)}, u32[]{:S(2)}) collective-permute-start(bf16[2048,128]{1,0:T(8,128)(2,1)S(1)} %copy-done.12), channel_id=1, source_target_pairs={{0,32},{16,48},{32,0},{48,16},{1,33},{17,49},{33,1},{49,17},{2,34}... | collective-permute-start | bytes 1572872 | tf_op jit(solution)/shard_map/ppermute | solution.py:321
  86.0 2.7 %copy-start.10 = (bf16[2048,128]{1,0:T(8,128)(2,1)}, bf16[2048,128]{1,0:T(8,128)(2,1)S(1)}, u32[]{:S(2)}) copy-start(bf16[2048,128]{1,0:T(8,128)(2,1)S(1)} %collective-permute-done.1.refs_3_) | copy-start | bytes 1572868
  88.7 0.7 copy-start.8
  93.8 59.8 %copy-start.6 = (s32[4]{0:T(128)S(1)}, s32[4]{0:T(128)}, u32[]{:S(2)}) copy-start(s32[4]{0:T(128)} %pad_add_fusion.refs_0_) | copy-start | bytes 52
  93.8 35.6 %all-to-all-start.3 = ((bf16[16,128,128]{2,1,0:T(8,128)(2,1)}), bf16[16,128,128]{2,1,0:T(8,128)(2,1)S(1)}, u32[]{:S(2)}, u32[]{:S(2)}) async-start(bf16[16,128,128]{2,1,0:T(8,128)(2,1)} %get-tuple-element.46), calls=%async_computation.3 | async-start | bytes 1048576 | tf_op jit(solution)/shard_map/all_to_all | solution.py:325
  104.0 49.6 %reduce-scatter.5.cloned.1.call-start = ((), (), s32[]{:S(2)}) async-start(), calls=%async_computation.9 | async-start | bytes 163840 | tf_op jit(solution)/shard_map/reduce_scatter | solution.py:384
  107.5 90.7 %copy-start.2 = (f32[32,512]{1,0:T(8,128)S(1)}, f32[32,512]{1,0:T(8,128)}, u32[]{:S(2)}) copy-start(f32[32,512]{1,0:T(8,128)} %refs_1_.9) | copy-start | bytes 196612
  107.5 10.5 %collective-permute-start.3 = (bf16[16,16,128]{2,1,0:T(8,128)(2,1)}, bf16[16,16,128]{2,1,0:T(8,128)(2,1)S(1)}, u32[]{:S(2)}, u32[]{:S(2)}) collective-permute-start(bf16[16,16,128]{2,1,0:T(8,128)(2,1)} %get-tuple-element.40), channel_id=1, source_target_pairs={{0,16},{16,32},{32,48},{48,0},{1,17},{17,33},{33,49},{49,1},{2,18}... | collective-permute-start | bytes 196616 | tf_op jit(solution)/shard_map/ppermute | solution.py:321
  110.4 7.6 %collective-permute-start.4 = (bf16[16,16,128]{2,1,0:T(8,128)(2,1)}, bf16[16,16,128]{2,1,0:T(8,128)(2,1)S(1)}, u32[]{:S(2)}, u32[]{:S(2)}) collective-permute-start(bf16[16,16,128]{2,1,0:T(8,128)(2,1)} %get-tuple-element.41), channel_id=1, source_target_pairs={{0,32},{16,48},{32,0},{48,16},{1,33},{17,49},{33,1},{49,17},{2,34}... | collective-permute-start | bytes 196616 | tf_op jit(solution)/shard_map/ppermute | solution.py:321
  115.3 5.6 %collective-permute-start.5 = (bf16[16,16,128]{2,1,0:T(8,128)(2,1)}, bf16[16,16,128]{2,1,0:T(8,128)(2,1)S(1)}, u32[]{:S(2)}, u32[]{:S(2)}) collective-permute-start(bf16[16,16,128]{2,1,0:T(8,128)(2,1)} %get-tuple-element.42), channel_id=1, source_target_pairs={{0,48},{16,0},{32,16},{48,32},{1,49},{17,1},{33,17},{49,33},{2,50}... | collective-permute-start | bytes 196616 | tf_op jit(solution)/shard_map/ppermute | solution.py:321
  118.0 2.9 %copy-start.14 = (bf16[16,16,128]{2,1,0:T(8,128)(2,1)}, bf16[16,16,128]{2,1,0:T(8,128)(2,1)S(1)}, u32[]{:S(2)}) copy-start(bf16[16,16,128]{2,1,0:T(8,128)(2,1)S(1)} %collective-permute-done.3.refs_8_) | copy-start | bytes 196612
  118.1 2.9 %copy-start.15 = (bf16[16,16,128]{2,1,0:T(8,128)(2,1)}, bf16[16,16,128]{2,1,0:T(8,128)(2,1)S(1)}, u32[]{:S(2)}) copy-start(bf16[16,16,128]{2,1,0:T(8,128)(2,1)S(1)} %collective-permute-done.4.refs_9_) | copy-start | bytes 196612
  120.9 0.6 copy-start.16
  153.6 0.8 copy-start.4
  154.3 0.7 copy-start.7
  155.7 18.6 %collective-permute-start.6 = (f32[32,128]{1,0:T(8,128)S(1)}, f32[32,128]{1,0:T(8,128)S(1)}, u32[]{:S(2)}, u32[]{:S(2)}) collective-permute-start(f32[32,128]{1,0:T(8,128)S(1)} %get-tuple-element.50), channel_id=1, source_target_pairs={{0,16},{16,32},{32,48},{48,0},{1,17},{17,33},{33,49},{49,1},{2,18}... | collective-permute-start | bytes 49160 | tf_op jit(solution)/shard_map/ppermute | solution.py:321
  175.0 23.2 %all-to-all-start.5 = ((f32[16,1,128]{2,1,0:T(1,128)}), f32[16,1,128]{2,1,0:T(1,128)S(1)}, u32[]{:S(2)}, u32[]{:S(2)}) async-start(f32[16,1,128]{2,1,0:T(1,128)} %shard_map.109), calls=%async_computation.7 | async-start | bytes 16384 | tf_op jit(solution)/shard_map/all_to_all | solution.py:325
  187.0 6.5 %collective-permute-start.7 = (f32[32,128]{1,0:T(8,128)S(1)}, f32[32,128]{1,0:T(8,128)S(1)}, u32[]{:S(2)}, u32[]{:S(2)}) collective-permute-start(f32[32,128]{1,0:T(8,128)S(1)} %get-tuple-element.51), channel_id=1, source_target_pairs={{0,32},{16,48},{32,0},{48,16},{1,33},{17,49},{33,1},{49,17},{2,34}... | collective-permute-start | bytes 49160 | tf_op jit(solution)/shard_map/ppermute | solution.py:321
  189.7 4.8 %collective-permute-start.8 = (f32[32,128]{1,0:T(8,128)S(1)}, f32[32,128]{1,0:T(8,128)S(1)}, u32[]{:S(2)}, u32[]{:S(2)}) collective-permute-start(f32[32,128]{1,0:T(8,128)S(1)} %get-tuple-element.52), channel_id=1, source_target_pairs={{0,48},{16,0},{32,16},{48,32},{1,49},{17,1},{33,17},{49,33},{2,50}... | collective-permute-start | bytes 49160 | tf_op jit(solution)/shard_map/ppermute | solution.py:321
Sparse Core Ops, SparseCore 0:
  27.6 79.8 reduce-scatter.2
  110.3 43.2 reduce-scatter.4

commit v5 on v4

--- a/solution.py
+++ b/solution.py
@@ -132,49 +132,43 @@
         out_ref[h, D:, :] = dot(k_ref[:, s], v_ref[:, s], 0, 0).astype(bf16)
 
 
-def local_kernel(info_ref, weight_ref, q_hbm, k_hbm, g_hbm, x_hbm, loc_ref, proj_hbm, *refs):
-    keyed_hbm = refs[:-9]
-    q_ref, k_ref, g_ref, x_ref, right_ref, done_ref, summed_ref, in_sems, out_sems = refs[-9:]
-    n_y = len(keyed_hbm)
-    nz, each = summed_ref.shape[1], summed_ref.shape[3]
-    width = k_ref.shape[1]
+def local_kernel(info_ref, weight_ref, q_hbm, k_hbm, g_hbm, x_hbm, loc_ref, *refs):
+    out_hbm = refs[:-8]
+    q_ref, k_ref, g_ref, x_ref, right_ref, done_ref, in_sems, out_sems = refs[-8:]
+    n_y = len(out_hbm)
     chunks, _, chunk = x_ref.shape
     moves = start_all(
         [(k_hbm, k_ref), (q_hbm, q_ref), (g_hbm, g_ref)]
         + [(x_hbm.at[:, pl.ds(c * chunk, chunk)], x_ref.at[c]) for c in range(chunks)],
         in_sems,
     )
-    y = info_ref[1]
-    moves[0].wait()
+    for move in moves[:3]:
+        move.wait()
+    blocks = q_ref.shape[0] // D
     for n in range(n_y):
-        right_ref[:, lanes(n)] = k_ref[:, lanes(lax.rem(y + n, n_y))]
-    moves[1].wait()
-    moves[2].wait()
-    blocks = q_ref.shape[0] // D
-    for h in range(n_y):
+        h = lax.rem(info_ref[1] + n, n_y)
         s = lanes(h)
         head = info_ref[0] * n_y + h
+        keys, query, grad = k_ref[:, s], q_ref[:, s], g_ref[:, s]
+        right_ref[:, lanes(2 * n)] = keys
         diag = diagonal(head, weight_ref, True)
         for j in range(blocks):
             rows = slice(j * D, (j + 1) * D)
-            scores = dot(k_ref[rows, s], q_ref[j * D :, s], 1, 1)
+            scores = dot(keys[rows], query[j * D :], 1, 1)
             mixed = weighted(scores, j, j, head, weight_ref, diag)
-            res = dot(mixed, g_ref[j * D :, s], 1, 0)
+            res = dot(mixed, grad[j * D :], 1, 0)
             loc_ref[rows, s] = res
-            right_ref[rows, width + h * D : width + (h + 1) * D] = res.astype(bf16)
+            right_ref[rows, lanes(2 * n + 1)] = res.astype(bf16)
     sent = []
     for c in range(chunks):
         moves[3 + c].wait()
-        part = pl.ds(c * chunk, chunk)
         res = dot(x_ref[c], right_ref[...], 0, 0).astype(bf16)
         for n in range(n_y):
-            done_ref[c, n, :, :] = res[:, lanes(n)]
-            for z in range(nz):
-                summed_ref[c, z, n, :, :] = res[z * each : (z + 1) * each, lanes(n_y + n)]
+            done_ref[c, n, 0, :, :] = res[:, lanes(2 * n)]
+            done_ref[c, n, 1, :, :] = res[:, lanes(2 * n + 1)]
+        part = pl.ds(c * chunk, chunk)
         sent += start_all(
-            [(done_ref.at[c, n], keyed_hbm[n].at[part, :]) for n in range(n_y)]
-            + [(summed_ref.at[c], proj_hbm.at[:, :, pl.ds(c * each, each), :])],
-            out_sems.at[c],
+            [(done_ref.at[c, n], out_hbm[n].at[:, part, :]) for n in range(n_y)], out_sems.at[c]
         )
     for move in sent:
         move.wait()
@@ -216,14 +210,14 @@
     a_ref, r_ref, done_ref, r_sem, a_sems, out_sems, own_sems = refs[-7:]
     keyed = (a0, a1, a2, a3)
     n_y = len(keyed)
-    chunks, _, rows = a_ref.shape[:3]
+    chunks, _, _, rows, _ = a_ref.shape
     got = start_all([(r_hbm, r_ref)], r_sem)
     moves = []
     for c in range(chunks):
         part = pl.ds(c * rows, rows)
         moves.append(
             start_all(
-                [(keyed[n].at[part, :], a_ref.at[c, n]) for n in range(n_y)], a_sems.at[c]
+                [(keyed[n].at[:, part, :], a_ref.at[c, n]) for n in range(n_y)], a_sems.at[c]
             )
         )
     y = info_ref[1]
@@ -237,8 +231,11 @@
     for c in range(chunks):
         for move in moves[c]:
             move.wait()
-        left = jnp.concatenate([a_ref[c, n] for n in range(n_y)], axis=1)
-        res = dot(left, states, 1, 0).astype(bf16)
+        left = jnp.concatenate([a_ref[c, n, 0] for n in range(n_y)], axis=1)
+        res = dot(left, states, 1, 0)
+        for n in range(n_y):
+            res = res + a_ref[c, n, 1].astype(f32)
+        res = res.astype(bf16)
         inner = rows // (nz * each)
         for b in range(inner):
             for z in range(nz):
@@ -286,19 +283,17 @@
             dk_ref[rows, s] = (base_k[rows] + dot(dmix_t, query[i * D :], 1, 0)).astype(bf16)
 
 
-def shard_kernel(info_ref, in_ref, loc_ref, square_ref, *refs):
-    part_refs, total_ref = refs[:-1], refs[-1]
-    n_y = len(part_refs)
-    rows = part_refs[0].shape[0]
-    total = loc_ref[...].astype(f32)
-    for z in range(in_ref.shape[0]):
+def shard_kernel(info_ref, in_ref, square_ref, out_ref, total_ref):
+    n_y, heads, rows = out_ref.shape[:3]
+    total = in_ref[0].astype(f32)
+    for z in range(1, in_ref.shape[0]):
         total = total + in_ref[z].astype(f32)
     total_ref[...] = total
     square = jnp.sum(jnp.sum(total * total, axis=0, keepdims=True), axis=1, keepdims=True)
     square_ref[...] = jnp.broadcast_to(square[None], square_ref.shape)
-    for n in range(n_y):
-        first = pl.multiple_of(lax.rem(info_ref[1] + n, n_y) * rows, rows)
-        part_refs[n][...] = total_ref[pl.ds(first, rows), :]
+    out_ref[...] = jnp.zeros_like(out_ref)
+    for y in range(n_y):
+        out_ref[y, info_ref[1], :, :] = total_ref[y * rows : (y + 1) * rows, :]
 
 
 def stage_kernel(square_ref, out_ref):
@@ -306,14 +301,12 @@
     out_ref[...] = jnp.broadcast_to(square, out_ref.shape)
 
 
-def final_kernel(info_ref, mom_ref, p0, p1, p2, p3, total_ref, out_ref):
-    parts = (p0, p1, p2, p3)
-    n_y = len(parts)
+def final_kernel(mom_ref, in_ref, total_ref, out_ref):
     total = jnp.sum(total_ref[...], axis=0)
     factor = jnp.minimum(f32(1.0), clip_norm / jnp.sqrt(total + 1e-06))
-    for n in range(n_y):
-        s = lanes(lax.rem(info_ref[1] + n_y - n, n_y))
-        out_ref[:, s] = momentum_rate * mom_ref[:, s] + factor * parts[n][...]
+    for h in range(in_ref.shape[0]):
+        s = lanes(h)
+        out_ref[:, s] = momentum_rate * mom_ref[:, s] + factor * in_ref[h]
 
 
 def shift(x, axis, by):
@@ -349,39 +342,34 @@
     )
     chunk = 512
     chunks = features // chunk
-    local, proj, *keyed = call(
+    local, *keyed = call(
         local_kernel,
-        (sds((length, width), f32), sds((n_z, heads, features // n_z, D), bf16))
-        + tuple(sds((features, D), bf16) for _ in range(n_y)),
+        (sds((length, width), f32),) + tuple(sds((2, features, D), bf16) for _ in range(n_y)),
         (queries, keys, out_grad, inputs),
         4 * length * width * features + 3 * length * length * width,
         [ANY] * 4,
-        (VMEM,) + (ANY,) * (n_y + 1),
+        (VMEM,) + (ANY,) * n_y,
         scratch=[held] * 3
         + [
             pltpu.VMEM((chunks, length, chunk), bf16),
             pltpu.VMEM((length, 2 * width), bf16),
-            pltpu.VMEM((chunks, n_y, chunk, D), bf16),
-            pltpu.VMEM((chunks, n_z, heads, chunk // n_z, D), bf16),
+            pltpu.VMEM((chunks, n_y, 2, chunk, D), bf16),
             dma((3 + chunks,)),
-            dma((chunks, n_y + 1)),
+            dma((chunks, n_y)),
         ],
         scalars=(info, level_weight),
         vmem=VMEM_ALL,
     )
-    both, proj, *keyed[1:] = call(
+    both, *keyed[1:] = call(
         turn_kernel,
         sds((n_z, n_y, 2 * D // n_z, D), bf16),
         (swap(both, Y),),
         1 << 16,
-        gated=(proj, *keyed[1:]),
+        gated=keyed[1:],
         vmem=VMEM_ALL,
     )
     both = swap(both, Z)
     keyed = [keyed[0]] + [shift(keyed[n], Y, n) for n in range(1, n_y)]
-    proj = proj.reshape(heads * features, D)
-    for axis in (Z, Y):
-        proj = lax.psum_scatter(proj, axis, scatter_dimension=0, tiled=True)
 
     both = call(
         tree_kernel,
@@ -389,7 +377,6 @@
         (both,),
         1 << 21,
         scalars=(info, level_weight),
-        after=(keyed[1], keyed[3]),
         vmem=8,
     )
     both = swap(both, Z)
@@ -404,7 +391,7 @@
         [ANY] * (n_y + 1),
         (ANY,) * (n_y + 1),
         scratch=[
-            pltpu.VMEM((2, n_y, rows, D), bf16),
+            pltpu.VMEM((2, n_y, 2, rows, D), bf16),
             pltpu.VMEM(both.shape, bf16),
             pltpu.VMEM((2, n_z, rows // n_z, D), bf16),
             dma((1,)),
@@ -429,34 +416,26 @@
 
     near, rest = HEAD + (Y,), (Z,)
     rows = momentum.shape[0]
-    square, *mine = call(
+    square, shard = call(
         shard_kernel,
-        (sds((lax.axis_size(near), 1, D), f32),) + (sds((rows, D), f32),) * n_y,
-        (parts, proj),
+        (sds((lax.axis_size(near), 1, D), f32), sds((n_y, heads, rows, D), f32)),
+        (parts,),
         1 << 20,
         scratch=[pltpu.VMEM((n_y * rows, D), f32)],
         scalars=(info,),
         after=(end,),
         vmem=8,
     )
-    mine = [mine[0]] + [shift(mine[n], Y, n) for n in range(1, n_y)]
+    shard = lax.psum_scatter(
+        shard.reshape(n_y * heads * rows, D), Y, scatter_dimension=0, tiled=True
+    ).reshape(heads, rows, D)
     square = swap(square, near)
     total = call(
-        stage_kernel,
-        sds((lax.axis_size(rest), 1, D), f32),
-        (square,),
-        1 << 16,
-        after=(mine[1],),
-        vmem=8,
+        stage_kernel, sds((lax.axis_size(rest), 1, D), f32), (square,), 1 << 16, vmem=8
     )
     total = swap(total, rest)
     new_momentum = call(
-        final_kernel,
-        sds(momentum.shape, f32),
-        (momentum, *mine, total),
-        1 << 16,
-        scalars=(info,),
-        vmem=8,
+        final_kernel, sds(momentum.shape, f32), (momentum, shard, total), 1 << 16, vmem=8
     )
     return (query_grad, key_grad, value_grad, new_momentum)
 

time: 207 us -> 185 us (0.89)
  waiting for transfers between devices: 57.8 us -> 31.4 us
  blocking collectives: 16.7 us -> 38.9 us
  starting transfers between devices: 83.1 us -> 64.8 us
    reduce_scatter x2 -> x1, waiting for transfers between devices: 27.7 us -> 0.01 us  [body(): lax.psum_scatter(shard.reshape(n_y * heads * rows, D), Y, scatter_dimensi...]
    all_to_all x1 -> x2, blocking collectives: 16.7 us -> 38.9 us  [swap(): return lax.all_to_all(x, axes, 0, 0, tiled=True)]
    all_to_all x5 -> x4, starting transfers between devices: 53.4 us -> 42.5 us  [swap(): return lax.all_to_all(x, axes, 0, 0, tiled=True)]
    ppermute x9 -> x6, starting transfers between devices: 29.7 us -> 22.2 us  [shift(): return lax.ppermute(x, axis, [(i, (i + by) % n) for i in range(n)])]
    ppermute x9 -> x6, waiting for transfers between devices: 23.7 us -> 29.2 us  [shift(): return lax.ppermute(x, axis, [(i, (i + by) % n) for i in range(n)])]
    all_to_all x5 -> x4, waiting for transfers between devices: 6.34 us -> 2.18 us  [swap(): return lax.all_to_all(x, axes, 0, 0, tiled=True)]
  transfers between devices with their start and end apart: 16 -> 11, of which waited for: 9 -> 6; matrix products, arithmetic and copies ran while one was open for 0% -> 0% of each run, Pallas kernels for 11% -> 11%
where the time goes in v5:
time: 185 us; the launch traced here: 184 us
  starting transfers between devices  64.8 us (35%)
  blocking collectives  38.9 us (21%)
  waiting for transfers between devices  31.4 us (17%)
  Pallas kernels  30.1 us (16%)
  between operations  14.2 us (8%)
  local copies, waits for them, and re-layouts  3.54 us (2%)
    all_to_all x4, starting transfers between devices, swap(): return lax.all_to_all(x, axes, 0, 0, tiled=True)  42.5 us
    all_to_all x2, blocking collectives, swap(): return lax.all_to_all(x, axes, 0, 0, tiled=True)  38.9 us
    pallas_call x9, Pallas kernels, call(): pl.pallas_call(run, out_shape=out_shape, grid_spec=pltpu.PrefetchScalarGr...  30.1 us
    ppermute x6, waiting for transfers between devices, shift(): return lax.ppermute(x, axis, [(i, (i + by) % n) for i in range(n)])  29.2 us
    ppermute x6, starting transfers between devices, shift(): return lax.ppermute(x, axis, [(i, (i + by) % n) for i in range(n)])  22.2 us
  transfers between devices with their start and end apart: 11, of which 6 were waited for; matrix products, arithmetic and copies ran while one was open for 0% of the time, Pallas kernels for 11%

profile of v5, /device:TPU:1, one launch (start us, length us, event | category | flops | bytes accessed | tf_op | source)
XLA Modules:
  0.0 183.5 jit_solution(17161098569499033318)
XLA Ops:
  7.2 2.6 %shard_map.103 = bf16[4,256,128]{2,1,0:T(8,128)(2,1)} custom-call(bf16[512,512]{1,0:T(8,128)(2,1)} %refs_2_.5, bf16[512,512]{1,0:T(8,128)(2,1)} %refs_5_.3, bf16[512,512]{1,0:T(8,128)(2,1)} %refs_3_.5, bf16[512,512]{1,0:T(8,128)(2,1)} %refs_4_.3), custom_call_target="tpu_custom_call" | custom-call | flops 134217728 | bytes 2359296 | tf_op jit(solution)/shard_map/pallas_call | solution.py:56
  9.8 5.0 %all-to-all-start = ((bf16[4,256,128]{2,1,0:T(8,128)(2,1)}), bf16[4,256,128]{2,1,0:T(8,128)(2,1)S(1)}, u32[]{:S(2)}, u32[]{:S(2)}) async-start(bf16[4,256,128]{2,1,0:T(8,128)(2,1)} %shard_map.103), calls=%async_computation | async-start | bytes 524288 | tf_op jit(solution)/shard_map/all_to_all | solution.py:318
  14.8 0.6 pad_add_fusion.refs_0_
  15.4 9.7 %shard_map.102 = (f32[512,512]{1,0:T(8,128)}, bf16[2,2048,128]{2,1,0:T(8,128)(2,1)}, bf16[2,2048,128]{2,1,0:T(8,128)(2,1)}, bf16[2,2048,128]{2,1,0:T(8,128)(2,1)}, bf16[2,2048,128]{2,1,0:T(8,128)(2,1)}) custom-call(s32[4]{0:T(128)} %pad_add_fusion.refs_0_, s32[18,32]{1,0:T(8,128)} %refs_1_.7, bf16[512,512]{1,0:T(8,128)(2,1)} %refs_2_.5, ...), custom_call_target="tpu_custom_call" | custom-call | flops 2550136832 | bytes 8912896 | tf_op jit(solution)/shard_map/pallas_call | solution.py:56
  25.2 0.0 copy-start.2
  25.2 0.0 copy-start.3
  25.2 0.0 all-to-all-done.refs_0_
  25.2 0.0 copy-start.9
  25.2 0.7 copy-done.9
  25.9 1.7 shard_map.104
  27.6 14.9 %all-to-all-start.1 = ((bf16[16,4,16,128]{3,2,1,0:T(8,128)(2,1)}), bf16[16,4,16,128]{3,2,1,0:T(8,128)(2,1)S(1)}, u32[]{:S(2)}, u32[]{:S(2)}) async-start(bf16[16,4,16,128]{3,2,1,0:T(8,128)(2,1)} %get-tuple-element.32), calls=%async_computation.1 | async-start | bytes 524288 | tf_op jit(solution)/shard_map/all_to_all | solution.py:318
  42.5 3.4 %collective-permute-start = (bf16[2,2048,128]{2,1,0:T(8,128)(2,1)}, bf16[2,2048,128]{2,1,0:T(8,128)(2,1)S(1)}, u32[]{:S(2)}, u32[]{:S(2)}) collective-permute-start(bf16[2,2048,128]{2,1,0:T(8,128)(2,1)} %get-tuple-element.29), channel_id=1, source_target_pairs={{0,16},{16,32},{32,48},{48,0},{1,17},{17,33},{33,49},{49,1},{2,18}... | collective-permute-start | bytes 3145736 | tf_op jit(solution)/shard_map/ppermute | solution.py:314
  45.9 4.3 %collective-permute-start.1 = (bf16[2,2048,128]{2,1,0:T(8,128)(2,1)}, bf16[2,2048,128]{2,1,0:T(8,128)(2,1)S(1)}, u32[]{:S(2)}, u32[]{:S(2)}) collective-permute-start(bf16[2,2048,128]{2,1,0:T(8,128)(2,1)} %get-tuple-element.30), channel_id=1, source_target_pairs={{0,32},{16,48},{32,0},{48,16},{1,33},{17,49},{33,1},{49,17},{2,34}... | collective-permute-start | bytes 3145736 | tf_op jit(solution)/shard_map/ppermute | solution.py:314
  50.2 3.1 %collective-permute-start.2 = (bf16[2,2048,128]{2,1,0:T(8,128)(2,1)}, bf16[2,2048,128]{2,1,0:T(8,128)(2,1)}, u32[]{:S(2)}, u32[]{:S(2)}) collective-permute-start(bf16[2,2048,128]{2,1,0:T(8,128)(2,1)} %get-tuple-element.31), channel_id=1, source_target_pairs={{0,48},{16,0},{32,16},{48,32},{1,49},{17,1},{33,17},{49,33},{2,50}... | collective-permute-start | bytes 3145736 | tf_op jit(solution)/shard_map/ppermute | solution.py:314
  53.3 2.2 %all-to-all-done.1.refs_2_ = bf16[16,4,16,128]{3,2,1,0:T(8,128)(2,1)S(1)} async-done(((bf16[16,4,16,128]{3,2,1,0:T(8,128)(2,1)}), bf16[16,4,16,128]{3,2,1,0:T(8,128)(2,1)S(1)}, u32[]{:S(2)}, u32[]{:S(2)}) %all-to-all-start.1) | async-done | bytes 262176 | tf_op jit(solution)/shard_map/all_to_all | solution.py:318
  55.5 0.0 copy-done.2
  55.5 0.0 copy-done.3
  55.5 1.6 shard_map.105
  57.1 11.1 %all-to-all-start.2 = ((bf16[16,4,16,128]{3,2,1,0:T(8,128)(2,1)}), bf16[16,4,16,128]{3,2,1,0:T(8,128)(2,1)S(1)}, u32[]{:S(2)}, u32[]{:S(2)}) async-start(bf16[16,4,16,128]{3,2,1,0:T(8,128)(2,1)} %shard_map.105), calls=%async_computation.2 | async-start | bytes 524288 | tf_op jit(solution)/shard_map/all_to_all | solution.py:318
  68.2 1.1 collective-permute-done.refs_2_
  69.3 23.4 %collective-permute-done.1.refs_3_ = bf16[2,2048,128]{2,1,0:T(8,128)(2,1)S(1)} collective-permute-done((bf16[2,2048,128]{2,1,0:T(8,128)(2,1)}, bf16[2,2048,128]{2,1,0:T(8,128)(2,1)S(1)}, u32[]{:S(2)}, u32[]{:S(2)}) %collective-permute-start.1) | collective-permute-done | bytes 1048608 | tf_op jit(solution)/shard_map/ppermute | solution.py:314
  92.6 2.3 %collective-permute-done.2.refs_4_ = bf16[2,2048,128]{2,1,0:T(8,128)(2,1)} collective-permute-done((bf16[2,2048,128]{2,1,0:T(8,128)(2,1)}, bf16[2,2048,128]{2,1,0:T(8,128)(2,1)}, u32[]{:S(2)}, u32[]{:S(2)}) %collective-permute-start.2) | collective-permute-done | bytes 1048608 | tf_op jit(solution)/shard_map/ppermute | solution.py:314
  95.0 0.0 all-to-all-done.2.refs_5_
  95.0 0.0 copy-done.6
  95.0 0.0 copy-done.7
  95.0 0.7 copy-done.8
  95.7 4.5 %shard_map.106 = (bf16[16,128,128]{2,1,0:T(8,128)(2,1)}, bf16[16,16,128]{2,1,0:T(8,128)(2,1)}, bf16[16,16,128]{2,1,0:T(8,128)(2,1)}, bf16[16,16,128]{2,1,0:T(8,128)(2,1)}, bf16[16,16,128]{2,1,0:T(8,128)(2,1)}) custom-call(s32[4]{0:T(128)} %pad_add_fusion.refs_0_, bf16[2,2048,128]{2,1,0:T(8,128)(2,1)} %get-tuple-element.25.refs_1_, ...), custom_call_target="tpu_custom_call" | custom-call | flops 268435456 | bytes 5242880 | tf_op jit(solution)/shard_map/pallas_call | solution.py:56
  100.2 0.0 copy-start.4
  100.2 11.5 %all-to-all-start.3 = ((bf16[16,128,128]{2,1,0:T(8,128)(2,1)}), bf16[16,128,128]{2,1,0:T(8,128)(2,1)S(1)}, u32[]{:S(2)}, u32[]{:S(2)}) async-start(bf16[16,128,128]{2,1,0:T(8,128)(2,1)} %get-tuple-element.40), calls=%async_computation.3 | async-start | bytes 1048576 | tf_op jit(solution)/shard_map/all_to_all | solution.py:318
  111.6 0.0 reduce-scatter.2.cloned.1.call-start
  111.7 5.3 %collective-permute-start.3 = (bf16[16,16,128]{2,1,0:T(8,128)(2,1)}, bf16[16,16,128]{2,1,0:T(8,128)(2,1)S(1)}, u32[]{:S(2)}, u32[]{:S(2)}) collective-permute-start(bf16[16,16,128]{2,1,0:T(8,128)(2,1)} %get-tuple-element.34), channel_id=1, source_target_pairs={{0,16},{16,32},{32,48},{48,0},{1,17},{17,33},{33,49},{49,1},{2,18}... | collective-permute-start | bytes 196616 | tf_op jit(solution)/shard_map/ppermute | solution.py:314
  117.0 3.1 %collective-permute-start.4 = (bf16[16,16,128]{2,1,0:T(8,128)(2,1)}, bf16[16,16,128]{2,1,0:T(8,128)(2,1)S(1)}, u32[]{:S(2)}, u32[]{:S(2)}) collective-permute-start(bf16[16,16,128]{2,1,0:T(8,128)(2,1)} %get-tuple-element.35), channel_id=1, source_target_pairs={{0,32},{16,48},{32,0},{48,16},{1,33},{17,49},{33,1},{49,17},{2,34}... | collective-permute-start | bytes 196616 | tf_op jit(solution)/shard_map/ppermute | solution.py:314
  120.1 3.1 %collective-permute-start.5 = (bf16[16,16,128]{2,1,0:T(8,128)(2,1)}, bf16[16,16,128]{2,1,0:T(8,128)(2,1)S(1)}, u32[]{:S(2)}, u32[]{:S(2)}) collective-permute-start(bf16[16,16,128]{2,1,0:T(8,128)(2,1)} %get-tuple-element.36), channel_id=1, source_target_pairs={{0,48},{16,0},{32,16},{48,32},{1,49},{17,1},{33,17},{49,33},{2,50}... | collective-permute-start | bytes 196616 | tf_op jit(solution)/shard_map/ppermute | solution.py:314
  123.2 0.0 collective-permute-done.3.refs_8_
  123.2 0.0 copy-start.10
  123.2 0.8 collective-permute-done.4.refs_9_
  124.0 1.6 collective-permute-done.5.refs_10_
  125.6 0.0 copy-done.10
  125.6 0.6 copy-done.12
  126.3 7.9 %shard_map.107 = (bf16[512,512]{1,0:T(8,128)(2,1)}, bf16[512,512]{1,0:T(8,128)(2,1)}, bf16[512,512]{1,0:T(8,128)(2,1)}, f32[8,128]{1,0:T(8,128)}) custom-call(s32[4]{0:T(128)} %pad_add_fusion.refs_0_, s32[18,32]{1,0:T(8,128)} %refs_1_.7, bf16[512,512]{1,0:T(8,128)(2,1)} %refs_2_.5, bf16[512,512]{1,0:T(8,128)(2,1)} %refs_3_.5, bf16[512,512]{1,0:T(8,128)(2,1)} %refs_4_.3, ...), custom_call_target="tpu_custom_call" | custom-call | flops 805306368 | bytes 4984832 | tf_op jit(solution)/shard_map/pallas_call | solution.py:56
  134.2 0.0 all-to-all-done.3.refs_1_
  134.2 0.7 copy-done.5
  134.9 1.3 shard_map.108
  136.2 0.0 reduce-scatter.2.cloned.1.call-update
  136.2 21.7 %all_to_all.30.refs_0_ = f32[32,1,128]{2,1,0:T(1,128)S(1)} all-to-all(f32[32,1,128]{2,1,0:T(1,128)S(1)} %get-tuple-element.43), channel_id=1, replica_groups=mesh['head_0'=4,'head_1'=2,'seq_0'=4,'seq_1'=16] {'head_0','head_1','seq..., dimensions={0} | all-to-all | bytes 32768 | tf_op jit(solution)/shard_map/all_to_all | solution.py:318
  158.0 17.2 %all_to_all.31.refs_2_ = f32[16,1,128]{2,1,0:T(1,128)S(1)} all-to-all(f32[16,1,128]{2,1,0:T(1,128)S(1)} %shard_map.109), channel_id=1, replica_groups=mesh['head_0'=4,'head_1'=2,'seq_0'=4,'seq_1'=16] {'seq_1'}, dimensions={0} | all-to-all | bytes 16384 | tf_op jit(solution)/shard_map/all_to_all | solution.py:318
  175.2 0.8 copy-done.1
  176.0 0.7 shard_map.110
  (13 shorter events, 0.1 us)
Async XLA Ops:
  9.8 15.4 %all-to-all-start = ((bf16[4,256,128]{2,1,0:T(8,128)(2,1)}), bf16[4,256,128]{2,1,0:T(8,128)(2,1)S(1)}, u32[]{:S(2)}, u32[]{:S(2)}) async-start(bf16[4,256,128]{2,1,0:T(8,128)(2,1)} %shard_map.103), calls=%async_computation | async-start | bytes 524288 | tf_op jit(solution)/shard_map/all_to_all | solution.py:318
  25.2 30.3 %copy-start.2 = (s32[18,32]{1,0:T(8,128)S(1)}, s32[18,32]{1,0:T(8,128)}, u32[]{:S(2)}) copy-start(s32[18,32]{1,0:T(8,128)} %refs_1_.7) | copy-start | bytes 6916
  25.2 30.3 %copy-start.3 = (s32[4]{0:T(128)S(1)}, s32[4]{0:T(128)}, u32[]{:S(2)}) copy-start(s32[4]{0:T(128)} %pad_add_fusion.refs_0_) | copy-start | bytes 52
  25.2 0.7 copy-start.9
  27.6 27.9 %all-to-all-start.1 = ((bf16[16,4,16,128]{3,2,1,0:T(8,128)(2,1)}), bf16[16,4,16,128]{3,2,1,0:T(8,128)(2,1)S(1)}, u32[]{:S(2)}, u32[]{:S(2)}) async-start(bf16[16,4,16,128]{3,2,1,0:T(8,128)(2,1)} %get-tuple-element.32), calls=%async_computation.1 | async-start | bytes 524288 | tf_op jit(solution)/shard_map/all_to_all | solution.py:318
  42.5 26.8 %collective-permute-start = (bf16[2,2048,128]{2,1,0:T(8,128)(2,1)}, bf16[2,2048,128]{2,1,0:T(8,128)(2,1)S(1)}, u32[]{:S(2)}, u32[]{:S(2)}) collective-permute-start(bf16[2,2048,128]{2,1,0:T(8,128)(2,1)} %get-tuple-element.29), channel_id=1, source_target_pairs={{0,16},{16,32},{32,48},{48,0},{1,17},{17,33},{33,49},{49,1},{2,18}... | collective-permute-start | bytes 3145736 | tf_op jit(solution)/shard_map/ppermute | solution.py:314
  45.9 46.7 %collective-permute-start.1 = (bf16[2,2048,128]{2,1,0:T(8,128)(2,1)}, bf16[2,2048,128]{2,1,0:T(8,128)(2,1)S(1)}, u32[]{:S(2)}, u32[]{:S(2)}) collective-permute-start(bf16[2,2048,128]{2,1,0:T(8,128)(2,1)} %get-tuple-element.30), channel_id=1, source_target_pairs={{0,32},{16,48},{32,0},{48,16},{1,33},{17,49},{33,1},{49,17},{2,34}... | collective-permute-start | bytes 3145736 | tf_op jit(solution)/shard_map/ppermute | solution.py:314
  50.2 44.8 %collective-permute-start.2 = (bf16[2,2048,128]{2,1,0:T(8,128)(2,1)}, bf16[2,2048,128]{2,1,0:T(8,128)(2,1)}, u32[]{:S(2)}, u32[]{:S(2)}) collective-permute-start(bf16[2,2048,128]{2,1,0:T(8,128)(2,1)} %get-tuple-element.31), channel_id=1, source_target_pairs={{0,48},{16,0},{32,16},{48,32},{1,49},{17,1},{33,17},{49,33},{2,50}... | collective-permute-start | bytes 3145736 | tf_op jit(solution)/shard_map/ppermute | solution.py:314
  57.1 37.9 %all-to-all-start.2 = ((bf16[16,4,16,128]{3,2,1,0:T(8,128)(2,1)}), bf16[16,4,16,128]{3,2,1,0:T(8,128)(2,1)S(1)}, u32[]{:S(2)}, u32[]{:S(2)}) async-start(bf16[16,4,16,128]{3,2,1,0:T(8,128)(2,1)} %shard_map.105), calls=%async_computation.2 | async-start | bytes 524288 | tf_op jit(solution)/shard_map/all_to_all | solution.py:318
  69.3 25.7 %copy-start.6 = (bf16[2,2048,128]{2,1,0:T(8,128)(2,1)}, bf16[2,2048,128]{2,1,0:T(8,128)(2,1)S(1)}, u32[]{:S(2)}) copy-start(bf16[2,2048,128]{2,1,0:T(8,128)(2,1)S(1)} %collective-permute-done.refs_2_) | copy-start | bytes 3145732
  92.6 2.4 %copy-start.7 = (bf16[2,2048,128]{2,1,0:T(8,128)(2,1)}, bf16[2,2048,128]{2,1,0:T(8,128)(2,1)S(1)}, u32[]{:S(2)}) copy-start(bf16[2,2048,128]{2,1,0:T(8,128)(2,1)S(1)} %collective-permute-done.1.refs_3_) | copy-start | bytes 3145732
  95.0 0.7 copy-start.8
  100.2 34.1 %copy-start.4 = (s32[4]{0:T(128)S(1)}, s32[4]{0:T(128)}, u32[]{:S(2)}) copy-start(s32[4]{0:T(128)} %pad_add_fusion.refs_0_) | copy-start | bytes 52
  100.2 34.0 %all-to-all-start.3 = ((bf16[16,128,128]{2,1,0:T(8,128)(2,1)}), bf16[16,128,128]{2,1,0:T(8,128)(2,1)S(1)}, u32[]{:S(2)}, u32[]{:S(2)}) async-start(bf16[16,128,128]{2,1,0:T(8,128)(2,1)} %get-tuple-element.40), calls=%async_computation.3 | async-start | bytes 1048576 | tf_op jit(solution)/shard_map/all_to_all | solution.py:318
  111.6 63.5 %reduce-scatter.2.cloned.1.call-start = ((), (), s32[]{:S(2)}) async-start(), calls=%async_computation.7 | async-start | bytes 327680 | tf_op jit(solution)/shard_map/reduce_scatter | solution.py:429
  111.7 11.5 %collective-permute-start.3 = (bf16[16,16,128]{2,1,0:T(8,128)(2,1)}, bf16[16,16,128]{2,1,0:T(8,128)(2,1)S(1)}, u32[]{:S(2)}, u32[]{:S(2)}) collective-permute-start(bf16[16,16,128]{2,1,0:T(8,128)(2,1)} %get-tuple-element.34), channel_id=1, source_target_pairs={{0,16},{16,32},{32,48},{48,0},{1,17},{17,33},{33,49},{49,1},{2,18}... | collective-permute-start | bytes 196616 | tf_op jit(solution)/shard_map/ppermute | solution.py:314
  117.0 7.0 %collective-permute-start.4 = (bf16[16,16,128]{2,1,0:T(8,128)(2,1)}, bf16[16,16,128]{2,1,0:T(8,128)(2,1)S(1)}, u32[]{:S(2)}, u32[]{:S(2)}) collective-permute-start(bf16[16,16,128]{2,1,0:T(8,128)(2,1)} %get-tuple-element.35), channel_id=1, source_target_pairs={{0,32},{16,48},{32,0},{48,16},{1,33},{17,49},{33,1},{49,17},{2,34}... | collective-permute-start | bytes 196616 | tf_op jit(solution)/shard_map/ppermute | solution.py:314
  120.1 5.5 %collective-permute-start.5 = (bf16[16,16,128]{2,1,0:T(8,128)(2,1)}, bf16[16,16,128]{2,1,0:T(8,128)(2,1)S(1)}, u32[]{:S(2)}, u32[]{:S(2)}) collective-permute-start(bf16[16,16,128]{2,1,0:T(8,128)(2,1)} %get-tuple-element.36), channel_id=1, source_target_pairs={{0,48},{16,0},{32,16},{48,32},{1,49},{17,1},{33,17},{49,33},{2,50}... | collective-permute-start | bytes 196616 | tf_op jit(solution)/shard_map/ppermute | solution.py:314
  123.2 2.4 %copy-start.10 = (bf16[16,16,128]{2,1,0:T(8,128)(2,1)}, bf16[16,16,128]{2,1,0:T(8,128)(2,1)S(1)}, u32[]{:S(2)}) copy-start(bf16[16,16,128]{2,1,0:T(8,128)(2,1)S(1)} %collective-permute-done.3.refs_8_) | copy-start | bytes 196612
  124.0 1.7 copy-start.11
  125.6 0.6 copy-start.12
  126.3 48.9 %copy-start = (f32[32,512]{1,0:T(8,128)S(1)}, f32[32,512]{1,0:T(8,128)}, u32[]{:S(2)}) copy-start(f32[32,512]{1,0:T(8,128)} %refs_0_.3) | copy-start | bytes 196612
  134.2 0.7 copy-start.5
  175.2 0.8 copy-start.1
Sparse Core Ops, SparseCore 0:
  136.4 28.9 reduce-scatter.1

commit v6 on v5

--- a/solution.py
+++ b/solution.py
@@ -132,7 +132,7 @@
         out_ref[h, D:, :] = dot(k_ref[:, s], v_ref[:, s], 0, 0).astype(bf16)
 
 
-def local_kernel(info_ref, weight_ref, q_hbm, k_hbm, g_hbm, x_hbm, loc_ref, *refs):
+def local_kernel(info_ref, weight_ref, q_hbm, k_hbm, g_hbm, x_hbm, *refs):
     out_hbm = refs[:-8]
     q_ref, k_ref, g_ref, x_ref, right_ref, done_ref, in_sems, out_sems = refs[-8:]
     n_y = len(out_hbm)
@@ -157,7 +157,6 @@
             scores = dot(keys[rows], query[j * D :], 1, 1)
             mixed = weighted(scores, j, j, head, weight_ref, diag)
             res = dot(mixed, grad[j * D :], 1, 0)
-            loc_ref[rows, s] = res
             right_ref[rows, lanes(2 * n + 1)] = res.astype(bf16)
     sent = []
     for c in range(chunks):
@@ -174,24 +173,17 @@
         move.wait()
 
 
-def turn_kernel(in_ref, out_ref):
-    each = out_ref.shape[2]
-    for z in range(out_ref.shape[0]):
-        for y in range(out_ref.shape[1]):
-            out_ref[z, y, :, :] = in_ref[y, z * each : (z + 1) * each, :]
-
-
 def tree_kernel(info_ref, weight_ref, in_ref, out_ref):
-    nz, ny = in_ref.shape[:2]
-    count = nz * ny
+    nz, ny = out_ref.shape[:2]
+    count = in_ref.shape[0]
     depth = count.bit_length() - 1
     head = info_ref[0] * ny + info_ref[1]
     is_grad = info_ref[2] < nz // 2
-    sums = [[in_ref[c % nz, c // nz].astype(f32) for c in range(count)]]
+    sums = [[in_ref[c].astype(f32) for c in range(count)]]
     for bit in range(depth - 1):
         last = sums[-1]
         sums.append([last[2 * b] + last[2 * b + 1] for b in range(len(last) // 2)])
-    total = [jnp.zeros(in_ref.shape[2:], f32)]
+    total = [jnp.zeros(in_ref.shape[1:], f32)]
     for bit in reversed(range(depth)):
         w = lam(D.bit_length() + 2 + bit, head, weight_ref)
         later = jnp.where(is_grad, w, f32(0.0))
@@ -254,7 +246,7 @@
 
 
 def outputs_kernel(
-    info_ref, weight_ref, q_ref, k_ref, v_ref, g_ref, loc_ref, r0, r1, r2, r3, dq_ref, dk_ref, dv_ref, end_ref
+    info_ref, weight_ref, q_ref, k_ref, v_ref, g_ref, r0, r1, r2, r3, dq_ref, dk_ref, dv_ref, end_ref
 ):
     states = (r0, r1, r2, r3)
     n_y = len(states)
@@ -267,7 +259,7 @@
         both = states[n][...].reshape(2 * D, D)
         returned, carried = both[:D], both[D:]
         query, keys, values, grad = q_ref[:, s], k_ref[:, s], v_ref[:, s], g_ref[:, s]
-        dv_ref[:, s] = (loc_ref[:, s] + dot(keys, returned, 1, 0)).astype(bf16)
+        base_v = dot(keys, returned, 1, 0)
         base_k = dot(values, returned, 1, 1)
         base_q = dot(grad, carried, 1, 1)
         diag = diagonal(head, weight_ref, False)
@@ -281,6 +273,9 @@
             later = dot(values[rows], grad[i * D :], 1, 1)
             dmix_t = weighted(later, i, i, head, weight_ref, diag_t)
             dk_ref[rows, s] = (base_k[rows] + dot(dmix_t, query[i * D :], 1, 0)).astype(bf16)
+            scores = dot(keys[rows], query[i * D :], 1, 1)
+            mixed_t = weighted(scores, i, i, head, weight_ref, diag_t)
+            dv_ref[rows, s] = (base_v[rows] + dot(mixed_t, grad[i * D :], 1, 0)).astype(bf16)
 
 
 def shard_kernel(info_ref, in_ref, square_ref, out_ref, total_ref):
@@ -342,13 +337,13 @@
     )
     chunk = 512
     chunks = features // chunk
-    local, *keyed = call(
+    keyed = call(
         local_kernel,
-        (sds((length, width), f32),) + tuple(sds((2, features, D), bf16) for _ in range(n_y)),
+        tuple(sds((2, features, D), bf16) for _ in range(n_y)),
         (queries, keys, out_grad, inputs),
         4 * length * width * features + 3 * length * length * width,
         [ANY] * 4,
-        (VMEM,) + (ANY,) * n_y,
+        (ANY,) * n_y,
         scratch=[held] * 3
         + [
             pltpu.VMEM((chunks, length, chunk), bf16),
@@ -360,20 +355,13 @@
         scalars=(info, level_weight),
         vmem=VMEM_ALL,
     )
-    both, *keyed[1:] = call(
-        turn_kernel,
-        sds((n_z, n_y, 2 * D // n_z, D), bf16),
-        (swap(both, Y),),
-        1 << 16,
-        gated=keyed[1:],
-        vmem=VMEM_ALL,
-    )
-    both = swap(both, Z)
+    slices = (n_y * n_z, 2 * D // n_z, D)
+    both = swap(both.reshape(slices), SEQ)
     keyed = [keyed[0]] + [shift(keyed[n], Y, n) for n in range(1, n_y)]
 
     both = call(
         tree_kernel,
-        sds(both.shape, bf16),
+        sds((n_z, n_y) + slices[1:], bf16),
         (both,),
         1 << 21,
         scalars=(info, level_weight),
@@ -408,7 +396,7 @@
     query_grad, key_grad, value_grad, end = call(
         outputs_kernel,
         (sds((length, width), bf16),) * 3 + (sds((8, D), f32),),
-        (queries, keys, values, out_grad, local, *own),
+        (queries, keys, values, out_grad, *own),
         6 * length * length * width,
         scalars=(info, level_weight),
         vmem=VMEM_ALL,

time: 185 us -> 181 us (0.978)
    ppermute x6, waiting for transfers between devices: 29.2 us -> 31.4 us  [shift(): return lax.ppermute(x, axis, [(i, (i + by) % n) for i in range(n)])]
    all_to_all x4 -> x3, waiting for transfers between devices: 2.18 us -> 0.01 us  [swap(): return lax.all_to_all(x, axes, 0, 0, tiled=True)]
    pallas_call x9 -> x8, Pallas kernels: 30.1 us -> 29.1 us  [call(): pl.pallas_call(run, out_shape=out_shape, grid_spec=pltpu.PrefetchScalarGr...]
    all_to_all x4 -> x3, starting transfers between devices: 42.5 us -> 41.7 us  [swap(): return lax.all_to_all(x, axes, 0, 0, tiled=True)]
  transfers between devices with their start and end apart: 11 -> 10, of which waited for: 6 -> 5; matrix products, arithmetic and copies ran while one was open for 0% -> 0% of each run, Pallas kernels for 11% -> 11%
where the time goes in v6:
time: 181 us; the launch traced here: 180 us
  starting transfers between devices  63.7 us (35%)
  blocking collectives  38.5 us (21%)
  waiting for transfers between devices  31.5 us (17%)
  Pallas kernels  29.1 us (16%)
  between operations  14.2 us (8%)
  local copies, waits for them, and re-layouts  2.87 us (2%)
    all_to_all x3, starting transfers between devices, swap(): return lax.all_to_all(x, axes, 0, 0, tiled=True)  41.7 us
    all_to_all x2, blocking collectives, swap(): return lax.all_to_all(x, axes, 0, 0, tiled=True)  38.5 us
    ppermute x6, waiting for transfers between devices, shift(): return lax.ppermute(x, axis, [(i, (i + by) % n) for i in range(n)])  31.4 us
    pallas_call x8, Pallas kernels, call(): pl.pallas_call(run, out_shape=out_shape, grid_spec=pltpu.PrefetchScalarGr...  29.1 us
    ppermute x6, starting transfers between devices, shift(): return lax.ppermute(x, axis, [(i, (i + by) % n) for i in range(n)])  22 us
  transfers between devices with their start and end apart: 10, of which 5 were waited for; matrix products, arithmetic and copies ran while one was open for 0% of the time, Pallas kernels for 11%

profile of v6, /device:TPU:1, one launch (start us, length us, event | category | flops | bytes accessed | tf_op | source)
XLA Modules:
  0.0 180.5 jit_solution(11312405311493153130)
XLA Ops:
  7.2 2.6 %shard_map.103 = bf16[4,256,128]{2,1,0:T(8,128)(2,1)} custom-call(bf16[512,512]{1,0:T(8,128)(2,1)} %refs_2_.5, bf16[512,512]{1,0:T(8,128)(2,1)} %refs_5_.3, bf16[512,512]{1,0:T(8,128)(2,1)} %refs_3_.5, bf16[512,512]{1,0:T(8,128)(2,1)} %refs_4_.3), custom_call_target="tpu_custom_call" | custom-call | flops 134217728 | bytes 2359296 | tf_op jit(solution)/shard_map/pallas_call | solution.py:56
  9.8 19.3 %all-to-all-start = ((bf16[64,16,128]{2,1,0:T(8,128)(2,1)}), bf16[64,16,128]{2,1,0:T(8,128)(2,1)S(1)}, u32[]{:S(2)}, u32[]{:S(2)}) async-start(bf16[64,16,128]{2,1,0:T(8,128)(2,1)} %bitcast.7), calls=%async_computation | async-start | bytes 524288 | tf_op jit(solution)/shard_map/all_to_all | solution.py:313
  29.1 0.7 pad_add_fusion.refs_0_
  29.8 0.0 copy-start.2
  29.8 0.0 copy-start.3
  29.8 8.9 %shard_map.102 = (bf16[2,2048,128]{2,1,0:T(8,128)(2,1)}, bf16[2,2048,128]{2,1,0:T(8,128)(2,1)}, bf16[2,2048,128]{2,1,0:T(8,128)(2,1)}, bf16[2,2048,128]{2,1,0:T(8,128)(2,1)}) custom-call(s32[4]{0:T(128)} %pad_add_fusion.refs_0_, s32[18,32]{1,0:T(8,128)} %refs_1_.7, bf16[512,512]{1,0:T(8,128)(2,1)} %refs_2_.5, bf16[512,512]{1,0:T(8,128)(2,1)} %refs_3_.5, ...), custom_call_target="tpu_custom_call" | custom-call | flops 2550136832 | bytes 7864320 | tf_op jit(solution)/shard_map/pallas_call | solution.py:56
  38.7 2.9 %collective-permute-start = (bf16[2,2048,128]{2,1,0:T(8,128)(2,1)}, bf16[2,2048,128]{2,1,0:T(8,128)(2,1)S(1)}, u32[]{:S(2)}, u32[]{:S(2)}) collective-permute-start(bf16[2,2048,128]{2,1,0:T(8,128)(2,1)} %get-tuple-element.20), channel_id=1, source_target_pairs={{0,16},{16,32},{32,48},{48,0},{1,17},{17,33},{33,49},{49,1},{2,18}... | collective-permute-start | bytes 3145736 | tf_op jit(solution)/shard_map/ppermute | solution.py:309
  41.7 4.5 %collective-permute-start.1 = (bf16[2,2048,128]{2,1,0:T(8,128)(2,1)}, bf16[2,2048,128]{2,1,0:T(8,128)(2,1)S(1)}, u32[]{:S(2)}, u32[]{:S(2)}) collective-permute-start(bf16[2,2048,128]{2,1,0:T(8,128)(2,1)} %get-tuple-element.21), channel_id=1, source_target_pairs={{0,32},{16,48},{32,0},{48,16},{1,33},{17,49},{33,1},{49,17},{2,34}... | collective-permute-start | bytes 3145736 | tf_op jit(solution)/shard_map/ppermute | solution.py:309
  46.2 3.0 %collective-permute-start.2 = (bf16[2,2048,128]{2,1,0:T(8,128)(2,1)}, bf16[2,2048,128]{2,1,0:T(8,128)(2,1)}, u32[]{:S(2)}, u32[]{:S(2)}) collective-permute-start(bf16[2,2048,128]{2,1,0:T(8,128)(2,1)} %get-tuple-element.22), channel_id=1, source_target_pairs={{0,48},{16,0},{32,16},{48,32},{1,49},{17,1},{33,17},{49,33},{2,50}... | collective-permute-start | bytes 3145736 | tf_op jit(solution)/shard_map/ppermute | solution.py:309
  49.2 0.0 all-to-all-done.refs_2_
  49.2 0.0 copy-done.2
  49.2 0.0 copy-done.3
  49.2 1.6 shard_map.104
  50.8 11.3 %all-to-all-start.1 = ((bf16[16,4,16,128]{3,2,1,0:T(8,128)(2,1)}), bf16[16,4,16,128]{3,2,1,0:T(8,128)(2,1)S(1)}, u32[]{:S(2)}, u32[]{:S(2)}) async-start(bf16[16,4,16,128]{3,2,1,0:T(8,128)(2,1)} %shard_map.104), calls=%async_computation.1 | async-start | bytes 524288 | tf_op jit(solution)/shard_map/all_to_all | solution.py:313
  62.1 4.6 %collective-permute-done.refs_2_ = bf16[2,2048,128]{2,1,0:T(8,128)(2,1)S(1)} collective-permute-done((bf16[2,2048,128]{2,1,0:T(8,128)(2,1)}, bf16[2,2048,128]{2,1,0:T(8,128)(2,1)S(1)}, u32[]{:S(2)}, u32[]{:S(2)}) %collective-permute-start) | collective-permute-done | bytes 1048608 | tf_op jit(solution)/shard_map/ppermute | solution.py:309
  66.7 22.5 %collective-permute-done.1.refs_3_ = bf16[2,2048,128]{2,1,0:T(8,128)(2,1)S(1)} collective-permute-done((bf16[2,2048,128]{2,1,0:T(8,128)(2,1)}, bf16[2,2048,128]{2,1,0:T(8,128)(2,1)S(1)}, u32[]{:S(2)}, u32[]{:S(2)}) %collective-permute-start.1) | collective-permute-done | bytes 1048608 | tf_op jit(solution)/shard_map/ppermute | solution.py:309
  89.2 2.1 %collective-permute-done.2.refs_4_ = bf16[2,2048,128]{2,1,0:T(8,128)(2,1)} collective-permute-done((bf16[2,2048,128]{2,1,0:T(8,128)(2,1)}, bf16[2,2048,128]{2,1,0:T(8,128)(2,1)}, u32[]{:S(2)}, u32[]{:S(2)}) %collective-permute-start.2) | collective-permute-done | bytes 1048608 | tf_op jit(solution)/shard_map/ppermute | solution.py:309
  91.2 0.0 all-to-all-done.1.refs_5_
  91.2 0.0 copy-done.6
  91.2 0.0 copy-done.7
  91.2 0.7 copy-done.8
  91.9 4.5 %shard_map.105 = (bf16[16,128,128]{2,1,0:T(8,128)(2,1)}, bf16[16,16,128]{2,1,0:T(8,128)(2,1)}, bf16[16,16,128]{2,1,0:T(8,128)(2,1)}, bf16[16,16,128]{2,1,0:T(8,128)(2,1)}, bf16[16,16,128]{2,1,0:T(8,128)(2,1)}) custom-call(s32[4]{0:T(128)} %pad_add_fusion.refs_0_, bf16[2,2048,128]{2,1,0:T(8,128)(2,1)} %get-tuple-element.19.refs_1_, ...), custom_call_target="tpu_custom_call" | custom-call | flops 268435456 | bytes 5242880 | tf_op jit(solution)/shard_map/pallas_call | solution.py:56
  96.4 0.0 copy-start.4
  96.4 11.1 %all-to-all-start.2 = ((bf16[16,128,128]{2,1,0:T(8,128)(2,1)}), bf16[16,128,128]{2,1,0:T(8,128)(2,1)S(1)}, u32[]{:S(2)}, u32[]{:S(2)}) async-start(bf16[16,128,128]{2,1,0:T(8,128)(2,1)} %get-tuple-element.30), calls=%async_computation.2 | async-start | bytes 1048576 | tf_op jit(solution)/shard_map/all_to_all | solution.py:313
  107.5 0.0 copy-start
  107.5 0.0 reduce-scatter.2.cloned.1.call-start
  107.6 5.2 %collective-permute-start.3 = (bf16[16,16,128]{2,1,0:T(8,128)(2,1)}, bf16[16,16,128]{2,1,0:T(8,128)(2,1)S(1)}, u32[]{:S(2)}, u32[]{:S(2)}) collective-permute-start(bf16[16,16,128]{2,1,0:T(8,128)(2,1)} %get-tuple-element.24), channel_id=1, source_target_pairs={{0,16},{16,32},{32,48},{48,0},{1,17},{17,33},{33,49},{49,1},{2,18}... | collective-permute-start | bytes 196616 | tf_op jit(solution)/shard_map/ppermute | solution.py:309
  112.7 3.3 %collective-permute-start.4 = (bf16[16,16,128]{2,1,0:T(8,128)(2,1)}, bf16[16,16,128]{2,1,0:T(8,128)(2,1)S(1)}, u32[]{:S(2)}, u32[]{:S(2)}) collective-permute-start(bf16[16,16,128]{2,1,0:T(8,128)(2,1)} %get-tuple-element.25), channel_id=1, source_target_pairs={{0,32},{16,48},{32,0},{48,16},{1,33},{17,49},{33,1},{49,17},{2,34}... | collective-permute-start | bytes 196616 | tf_op jit(solution)/shard_map/ppermute | solution.py:309
  116.0 3.1 %collective-permute-start.5 = (bf16[16,16,128]{2,1,0:T(8,128)(2,1)}, bf16[16,16,128]{2,1,0:T(8,128)(2,1)S(1)}, u32[]{:S(2)}, u32[]{:S(2)}) collective-permute-start(bf16[16,16,128]{2,1,0:T(8,128)(2,1)} %get-tuple-element.26), channel_id=1, source_target_pairs={{0,48},{16,0},{32,16},{48,32},{1,49},{17,1},{33,17},{49,33},{2,50}... | collective-permute-start | bytes 196616 | tf_op jit(solution)/shard_map/ppermute | solution.py:309
  119.2 0.0 collective-permute-done.3.refs_7_
  119.2 0.0 copy-start.9
  119.2 0.6 collective-permute-done.4.refs_8_
  119.8 1.8 collective-permute-done.5.refs_9_
  121.5 0.0 copy-done.9
  121.5 0.0 copy-done.10
  121.5 0.6 copy-done.11
  122.1 9.4 %shard_map.106 = (bf16[512,512]{1,0:T(8,128)(2,1)}, bf16[512,512]{1,0:T(8,128)(2,1)}, bf16[512,512]{1,0:T(8,128)(2,1)}, f32[8,128]{1,0:T(8,128)}) custom-call(s32[4]{0:T(128)} %pad_add_fusion.refs_0_, s32[18,32]{1,0:T(8,128)} %refs_1_.7, bf16[512,512]{1,0:T(8,128)(2,1)} %refs_2_.5, bf16[512,512]{1,0:T(8,128)(2,1)} %refs_3_.5, bf16[512,512]{1,0:T(8,128)(2,1)} %refs_4_.3, ...), custom_call_target="tpu_custom_call" | custom-call | flops 805306368 | bytes 3936256 | tf_op jit(solution)/shard_map/pallas_call | solution.py:56
  131.5 0.0 all-to-all-done.2.refs_1_
  131.5 0.0 copy-done.4
  131.5 0.0 copy-start.5
  131.6 0.7 copy-done.5
  132.2 1.3 shard_map.107
  133.6 0.0 reduce-scatter.2.cloned.1.call-update
  133.6 20.3 %all_to_all.25.refs_0_ = f32[32,1,128]{2,1,0:T(1,128)S(1)} all-to-all(f32[32,1,128]{2,1,0:T(1,128)S(1)} %get-tuple-element.33), channel_id=1, replica_groups=mesh['head_0'=4,'head_1'=2,'seq_0'=4,'seq_1'=16] {'head_0','head_1','seq..., dimensions={0} | all-to-all | bytes 32768 | tf_op jit(solution)/shard_map/all_to_all | solution.py:313
  153.9 18.2 %all_to_all.26.refs_2_ = f32[16,1,128]{2,1,0:T(1,128)S(1)} all-to-all(f32[16,1,128]{2,1,0:T(1,128)S(1)} %shard_map.108), channel_id=1, replica_groups=mesh['head_0'=4,'head_1'=2,'seq_0'=4,'seq_1'=16] {'seq_1'}, dimensions={0} | all-to-all | bytes 16384 | tf_op jit(solution)/shard_map/all_to_all | solution.py:313
  172.1 0.0 copy-done
  172.1 0.8 copy-done.1
  173.0 0.7 shard_map.109
  (8 shorter events, 0.0 us)
Async XLA Ops:
  9.8 39.3 %all-to-all-start = ((bf16[64,16,128]{2,1,0:T(8,128)(2,1)}), bf16[64,16,128]{2,1,0:T(8,128)(2,1)S(1)}, u32[]{:S(2)}, u32[]{:S(2)}) async-start(bf16[64,16,128]{2,1,0:T(8,128)(2,1)} %bitcast.7), calls=%async_computation | async-start | bytes 524288 | tf_op jit(solution)/shard_map/all_to_all | solution.py:313
  29.8 19.4 %copy-start.2 = (s32[18,32]{1,0:T(8,128)S(1)}, s32[18,32]{1,0:T(8,128)}, u32[]{:S(2)}) copy-start(s32[18,32]{1,0:T(8,128)} %refs_1_.7) | copy-start | bytes 6916
  29.8 19.4 %copy-start.3 = (s32[4]{0:T(128)S(1)}, s32[4]{0:T(128)}, u32[]{:S(2)}) copy-start(s32[4]{0:T(128)} %pad_add_fusion.refs_0_) | copy-start | bytes 52
  38.7 27.9 %collective-permute-start = (bf16[2,2048,128]{2,1,0:T(8,128)(2,1)}, bf16[2,2048,128]{2,1,0:T(8,128)(2,1)S(1)}, u32[]{:S(2)}, u32[]{:S(2)}) collective-permute-start(bf16[2,2048,128]{2,1,0:T(8,128)(2,1)} %get-tuple-element.20), channel_id=1, source_target_pairs={{0,16},{16,32},{32,48},{48,0},{1,17},{17,33},{33,49},{49,1},{2,18}... | collective-permute-start | bytes 3145736 | tf_op jit(solution)/shard_map/ppermute | solution.py:309
  41.7 47.5 %collective-permute-start.1 = (bf16[2,2048,128]{2,1,0:T(8,128)(2,1)}, bf16[2,2048,128]{2,1,0:T(8,128)(2,1)S(1)}, u32[]{:S(2)}, u32[]{:S(2)}) collective-permute-start(bf16[2,2048,128]{2,1,0:T(8,128)(2,1)} %get-tuple-element.21), channel_id=1, source_target_pairs={{0,32},{16,48},{32,0},{48,16},{1,33},{17,49},{33,1},{49,17},{2,34}... | collective-permute-start | bytes 3145736 | tf_op jit(solution)/shard_map/ppermute | solution.py:309
  46.2 45.1 %collective-permute-start.2 = (bf16[2,2048,128]{2,1,0:T(8,128)(2,1)}, bf16[2,2048,128]{2,1,0:T(8,128)(2,1)}, u32[]{:S(2)}, u32[]{:S(2)}) collective-permute-start(bf16[2,2048,128]{2,1,0:T(8,128)(2,1)} %get-tuple-element.22), channel_id=1, source_target_pairs={{0,48},{16,0},{32,16},{48,32},{1,49},{17,1},{33,17},{49,33},{2,50}... | collective-permute-start | bytes 3145736 | tf_op jit(solution)/shard_map/ppermute | solution.py:309
  50.8 40.5 %all-to-all-start.1 = ((bf16[16,4,16,128]{3,2,1,0:T(8,128)(2,1)}), bf16[16,4,16,128]{3,2,1,0:T(8,128)(2,1)S(1)}, u32[]{:S(2)}, u32[]{:S(2)}) async-start(bf16[16,4,16,128]{3,2,1,0:T(8,128)(2,1)} %shard_map.104), calls=%async_computation.1 | async-start | bytes 524288 | tf_op jit(solution)/shard_map/all_to_all | solution.py:313
  66.7 24.6 %copy-start.6 = (bf16[2,2048,128]{2,1,0:T(8,128)(2,1)}, bf16[2,2048,128]{2,1,0:T(8,128)(2,1)S(1)}, u32[]{:S(2)}) copy-start(bf16[2,2048,128]{2,1,0:T(8,128)(2,1)S(1)} %collective-permute-done.refs_2_) | copy-start | bytes 3145732
  89.2 2.1 %copy-start.7 = (bf16[2,2048,128]{2,1,0:T(8,128)(2,1)}, bf16[2,2048,128]{2,1,0:T(8,128)(2,1)S(1)}, u32[]{:S(2)}) copy-start(bf16[2,2048,128]{2,1,0:T(8,128)(2,1)S(1)} %collective-permute-done.1.refs_3_) | copy-start | bytes 3145732
  91.2 0.7 copy-start.8
  96.4 35.1 %copy-start.4 = (s32[4]{0:T(128)S(1)}, s32[4]{0:T(128)}, u32[]{:S(2)}) copy-start(s32[4]{0:T(128)} %pad_add_fusion.refs_0_) | copy-start | bytes 52
  96.4 35.1 %all-to-all-start.2 = ((bf16[16,128,128]{2,1,0:T(8,128)(2,1)}), bf16[16,128,128]{2,1,0:T(8,128)(2,1)S(1)}, u32[]{:S(2)}, u32[]{:S(2)}) async-start(bf16[16,128,128]{2,1,0:T(8,128)(2,1)} %get-tuple-element.30), calls=%async_computation.2 | async-start | bytes 1048576 | tf_op jit(solution)/shard_map/all_to_all | solution.py:313
  107.5 64.6 %copy-start = (f32[32,512]{1,0:T(8,128)S(1)}, f32[32,512]{1,0:T(8,128)}, u32[]{:S(2)}) copy-start(f32[32,512]{1,0:T(8,128)} %refs_0_.3) | copy-start | bytes 196612
  107.5 64.6 %reduce-scatter.2.cloned.1.call-start = ((), (), s32[]{:S(2)}) async-start(), calls=%async_computation.6 | async-start | bytes 327680 | tf_op jit(solution)/shard_map/reduce_scatter | solution.py:417
  107.6 11.6 %collective-permute-start.3 = (bf16[16,16,128]{2,1,0:T(8,128)(2,1)}, bf16[16,16,128]{2,1,0:T(8,128)(2,1)S(1)}, u32[]{:S(2)}, u32[]{:S(2)}) collective-permute-start(bf16[16,16,128]{2,1,0:T(8,128)(2,1)} %get-tuple-element.24), channel_id=1, source_target_pairs={{0,16},{16,32},{32,48},{48,0},{1,17},{17,33},{33,49},{49,1},{2,18}... | collective-permute-start | bytes 196616 | tf_op jit(solution)/shard_map/ppermute | solution.py:309
  112.7 7.0 %collective-permute-start.4 = (bf16[16,16,128]{2,1,0:T(8,128)(2,1)}, bf16[16,16,128]{2,1,0:T(8,128)(2,1)S(1)}, u32[]{:S(2)}, u32[]{:S(2)}) collective-permute-start(bf16[16,16,128]{2,1,0:T(8,128)(2,1)} %get-tuple-element.25), channel_id=1, source_target_pairs={{0,32},{16,48},{32,0},{48,16},{1,33},{17,49},{33,1},{49,17},{2,34}... | collective-permute-start | bytes 196616 | tf_op jit(solution)/shard_map/ppermute | solution.py:309
  116.0 5.5 %collective-permute-start.5 = (bf16[16,16,128]{2,1,0:T(8,128)(2,1)}, bf16[16,16,128]{2,1,0:T(8,128)(2,1)S(1)}, u32[]{:S(2)}, u32[]{:S(2)}) collective-permute-start(bf16[16,16,128]{2,1,0:T(8,128)(2,1)} %get-tuple-element.26), channel_id=1, source_target_pairs={{0,48},{16,0},{32,16},{48,32},{1,49},{17,1},{33,17},{49,33},{2,50}... | collective-permute-start | bytes 196616 | tf_op jit(solution)/shard_map/ppermute | solution.py:309
  119.2 2.4 %copy-start.9 = (bf16[16,16,128]{2,1,0:T(8,128)(2,1)}, bf16[16,16,128]{2,1,0:T(8,128)(2,1)S(1)}, u32[]{:S(2)}) copy-start(bf16[16,16,128]{2,1,0:T(8,128)(2,1)S(1)} %collective-permute-done.3.refs_7_) | copy-start | bytes 196612
  119.8 1.8 copy-start.10
  121.5 0.6 copy-start.11
  131.5 0.7 copy-start.5
  172.1 0.8 copy-start.1
Sparse Core Ops, SparseCore 0:
  133.7 28.5 reduce-scatter.1

commit v7 on v6

--- a/solution.py
+++ b/solution.py
@@ -353,7 +353,7 @@
             dma((chunks, n_y)),
         ],
         scalars=(info, level_weight),
-        vmem=VMEM_ALL,
+        vmem=52,
     )
     slices = (n_y * n_z, 2 * D // n_z, D)
     both = swap(both.reshape(slices), SEQ)
@@ -402,7 +402,7 @@
         vmem=VMEM_ALL,
     )
 
-    near, rest = HEAD + (Y,), (Z,)
+    near, rest = SEQ, HEAD
     rows = momentum.shape[0]
     square, shard = call(
         shard_kernel,

time: 181 us -> 181 us (level)
  transfers between devices with their start and end apart: 10 -> 10, of which waited for: 5 -> 6; matrix products, arithmetic and copies ran while one was open for 0% -> 0% of each run, Pallas kernels for 11% -> 10%
where the time goes in v7:
time: 181 us; the launch traced here: 180 us
  starting transfers between devices  62.4 us (34%)
  blocking collectives  40.3 us (22%)
  waiting for transfers between devices  32.8 us (18%)
  Pallas kernels  27.7 us (15%)
  between operations  14.2 us (8%)
  local copies, waits for them, and re-layouts  2.88 us (2%)
    all_to_all x3, starting transfers between devices, swap(): return lax.all_to_all(x, axes, 0, 0, tiled=True)  40.4 us
    all_to_all x2, blocking collectives, swap(): return lax.all_to_all(x, axes, 0, 0, tiled=True)  40.3 us
    ppermute x6, waiting for transfers between devices, shift(): return lax.ppermute(x, axis, [(i, (i + by) % n) for i in range(n)])  31.7 us
    pallas_call x8, Pallas kernels, call(): pl.pallas_call(run, out_shape=out_shape, grid_spec=pltpu.PrefetchScalarGr...  27.7 us
    ppermute x6, starting transfers between devices, shift(): return lax.ppermute(x, axis, [(i, (i + by) % n) for i in range(n)])  22 us
  transfers between devices with their start and end apart: 10, of which 6 were waited for; matrix products, arithmetic and copies ran while one was open for 0% of the time, Pallas kernels for 10%

profile of v7, /device:TPU:1, one launch (start us, length us, event | category | flops | bytes accessed | tf_op | source)
XLA Modules:
  0.0 180.4 jit_solution(5888910752280652924)
XLA Ops:
  7.2 0.0 copy-start.2
  7.2 0.0 copy-start
  7.2 0.0 copy-start.1
  7.2 0.0 copy-start.5
  7.2 2.8 %shard_map.103 = bf16[4,256,128]{2,1,0:T(8,128)(2,1)} custom-call(bf16[512,512]{1,0:T(8,128)(2,1)} %refs_2_.5, bf16[512,512]{1,0:T(8,128)(2,1)} %refs_5_.3, bf16[512,512]{1,0:T(8,128)(2,1)} %refs_3_.5, bf16[512,512]{1,0:T(8,128)(2,1)} %refs_4_.3), custom_call_target="tpu_custom_call" | custom-call | flops 134217728 | bytes 2359296 | tf_op jit(solution)/shard_map/pallas_call | solution.py:56
  10.0 19.3 %all-to-all-start = ((bf16[64,16,128]{2,1,0:T(8,128)(2,1)}), bf16[64,16,128]{2,1,0:T(8,128)(2,1)S(1)}, u32[]{:S(2)}, u32[]{:S(2)}) async-start(bf16[64,16,128]{2,1,0:T(8,128)(2,1)} %bitcast.7), calls=%async_computation | async-start | bytes 524288 | tf_op jit(solution)/shard_map/all_to_all | solution.py:313
  29.3 0.1 pad_add_fusion.refs_0_
  29.4 0.0 copy-done.2
  29.4 0.0 copy-done
  29.4 0.0 copy-done.1
  29.4 0.0 copy-done.5
  29.4 0.0 copy-start.6
  29.4 7.4 %shard_map.102 = (bf16[2,2048,128]{2,1,0:T(8,128)(2,1)}, bf16[2,2048,128]{2,1,0:T(8,128)(2,1)}, bf16[2,2048,128]{2,1,0:T(8,128)(2,1)}, bf16[2,2048,128]{2,1,0:T(8,128)(2,1)}) custom-call(s32[4]{0:T(128)S(1)} %pad_add_fusion.refs_0_, s32[18,32]{1,0:T(8,128)S(1)} %copy-done.5, bf16[512,512]{1,0:T(8,128)(2,1)S(1)} %copy-done, bf16[512,512]{1,0:T(8,128)(2,1)S(1)} %copy-done.1, ...), custom_call_target="tpu_custom_call" | custom-call | flops 2550136832 | bytes 7864320 | tf_op jit(solution)/shard_map/pallas_call | solution.py:56
  36.8 2.9 %collective-permute-start = (bf16[2,2048,128]{2,1,0:T(8,128)(2,1)}, bf16[2,2048,128]{2,1,0:T(8,128)(2,1)S(1)}, u32[]{:S(2)}, u32[]{:S(2)}) collective-permute-start(bf16[2,2048,128]{2,1,0:T(8,128)(2,1)} %get-tuple-element.20), channel_id=1, source_target_pairs={{0,16},{16,32},{32,48},{48,0},{1,17},{17,33},{33,49},{49,1},{2,18}... | collective-permute-start | bytes 3145736 | tf_op jit(solution)/shard_map/ppermute | solution.py:309
  39.7 4.5 %collective-permute-start.1 = (bf16[2,2048,128]{2,1,0:T(8,128)(2,1)}, bf16[2,2048,128]{2,1,0:T(8,128)(2,1)S(1)}, u32[]{:S(2)}, u32[]{:S(2)}) collective-permute-start(bf16[2,2048,128]{2,1,0:T(8,128)(2,1)} %get-tuple-element.21), channel_id=1, source_target_pairs={{0,32},{16,48},{32,0},{48,16},{1,33},{17,49},{33,1},{49,17},{2,34}... | collective-permute-start | bytes 3145736 | tf_op jit(solution)/shard_map/ppermute | solution.py:309
  44.2 3.0 %collective-permute-start.2 = (bf16[2,2048,128]{2,1,0:T(8,128)(2,1)}, bf16[2,2048,128]{2,1,0:T(8,128)(2,1)}, u32[]{:S(2)}, u32[]{:S(2)}) collective-permute-start(bf16[2,2048,128]{2,1,0:T(8,128)(2,1)} %get-tuple-element.22), channel_id=1, source_target_pairs={{0,48},{16,0},{32,16},{48,32},{1,49},{17,1},{33,17},{49,33},{2,50}... | collective-permute-start | bytes 3145736 | tf_op jit(solution)/shard_map/ppermute | solution.py:309
  47.2 1.1 all-to-all-done.refs_2_
  48.3 1.6 shard_map.104
  49.9 10.2 %all-to-all-start.1 = ((bf16[16,4,16,128]{3,2,1,0:T(8,128)(2,1)}), bf16[16,4,16,128]{3,2,1,0:T(8,128)(2,1)S(1)}, u32[]{:S(2)}, u32[]{:S(2)}) async-start(bf16[16,4,16,128]{3,2,1,0:T(8,128)(2,1)} %shard_map.104), calls=%async_computation.1 | async-start | bytes 524288 | tf_op jit(solution)/shard_map/all_to_all | solution.py:313
  60.2 5.0 %collective-permute-done.refs_2_ = bf16[2,2048,128]{2,1,0:T(8,128)(2,1)S(1)} collective-permute-done((bf16[2,2048,128]{2,1,0:T(8,128)(2,1)}, bf16[2,2048,128]{2,1,0:T(8,128)(2,1)S(1)}, u32[]{:S(2)}, u32[]{:S(2)}) %collective-permute-start) | collective-permute-done | bytes 1048608 | tf_op jit(solution)/shard_map/ppermute | solution.py:309
  65.2 22.9 %collective-permute-done.1.refs_3_ = bf16[2,2048,128]{2,1,0:T(8,128)(2,1)S(1)} collective-permute-done((bf16[2,2048,128]{2,1,0:T(8,128)(2,1)}, bf16[2,2048,128]{2,1,0:T(8,128)(2,1)S(1)}, u32[]{:S(2)}, u32[]{:S(2)}) %collective-permute-start.1) | collective-permute-done | bytes 1048608 | tf_op jit(solution)/shard_map/ppermute | solution.py:309
  88.1 1.4 collective-permute-done.2.refs_4_
  89.5 0.0 all-to-all-done.1.refs_5_
  89.5 0.0 copy-done.10
  89.5 0.7 copy-done.11
  90.2 4.5 %shard_map.105 = (bf16[16,128,128]{2,1,0:T(8,128)(2,1)}, bf16[16,16,128]{2,1,0:T(8,128)(2,1)}, bf16[16,16,128]{2,1,0:T(8,128)(2,1)}, bf16[16,16,128]{2,1,0:T(8,128)(2,1)}, bf16[16,16,128]{2,1,0:T(8,128)(2,1)}) custom-call(s32[4]{0:T(128)} %copy-done.6, bf16[2,2048,128]{2,1,0:T(8,128)(2,1)} %get-tuple-element.19.refs_1_, bf16[2,2048,128]{2,1,0:T(8,128)(2,1)} %copy-done.9, ...), custom_call_target="tpu_custom_call" | custom-call | flops 268435456 | bytes 5242880 | tf_op jit(solution)/shard_map/pallas_call | solution.py:56
  94.7 10.9 %all-to-all-start.2 = ((bf16[16,128,128]{2,1,0:T(8,128)(2,1)}), bf16[16,128,128]{2,1,0:T(8,128)(2,1)S(1)}, u32[]{:S(2)}, u32[]{:S(2)}) async-start(bf16[16,128,128]{2,1,0:T(8,128)(2,1)} %get-tuple-element.30), calls=%async_computation.2 | async-start | bytes 1048576 | tf_op jit(solution)/shard_map/all_to_all | solution.py:313
  105.6 0.0 copy-start.3
  105.6 0.0 reduce-scatter.2.cloned.1.call-start
  105.6 5.2 %collective-permute-start.3 = (bf16[16,16,128]{2,1,0:T(8,128)(2,1)}, bf16[16,16,128]{2,1,0:T(8,128)(2,1)S(1)}, u32[]{:S(2)}, u32[]{:S(2)}) collective-permute-start(bf16[16,16,128]{2,1,0:T(8,128)(2,1)} %get-tuple-element.24), channel_id=1, source_target_pairs={{0,16},{16,32},{32,48},{48,0},{1,17},{17,33},{33,49},{49,1},{2,18}... | collective-permute-start | bytes 196616 | tf_op jit(solution)/shard_map/ppermute | solution.py:309
  110.8 3.3 %collective-permute-start.4 = (bf16[16,16,128]{2,1,0:T(8,128)(2,1)}, bf16[16,16,128]{2,1,0:T(8,128)(2,1)S(1)}, u32[]{:S(2)}, u32[]{:S(2)}) collective-permute-start(bf16[16,16,128]{2,1,0:T(8,128)(2,1)} %get-tuple-element.25), channel_id=1, source_target_pairs={{0,32},{16,48},{32,0},{48,16},{1,33},{17,49},{33,1},{49,17},{2,34}... | collective-permute-start | bytes 196616 | tf_op jit(solution)/shard_map/ppermute | solution.py:309
  114.1 3.1 %collective-permute-start.5 = (bf16[16,16,128]{2,1,0:T(8,128)(2,1)}, bf16[16,16,128]{2,1,0:T(8,128)(2,1)S(1)}, u32[]{:S(2)}, u32[]{:S(2)}) collective-permute-start(bf16[16,16,128]{2,1,0:T(8,128)(2,1)} %get-tuple-element.26), channel_id=1, source_target_pairs={{0,48},{16,0},{32,16},{48,32},{1,49},{17,1},{33,17},{49,33},{2,50}... | collective-permute-start | bytes 196616 | tf_op jit(solution)/shard_map/ppermute | solution.py:309
  117.2 0.0 collective-permute-done.3.refs_7_
  117.2 0.6 collective-permute-done.4.refs_8_
  117.8 1.8 collective-permute-done.5.refs_9_
  119.6 0.0 copy-done.12
  119.6 0.6 copy-done.14
  120.2 9.4 %shard_map.106 = (bf16[512,512]{1,0:T(8,128)(2,1)}, bf16[512,512]{1,0:T(8,128)(2,1)}, bf16[512,512]{1,0:T(8,128)(2,1)}, f32[8,128]{1,0:T(8,128)}) custom-call(s32[4]{0:T(128)} %copy-done.6, s32[18,32]{1,0:T(8,128)} %refs_1_.7, bf16[512,512]{1,0:T(8,128)(2,1)} %refs_2_.5, bf16[512,512]{1,0:T(8,128)(2,1)} %refs_3_.5, bf16[512,512]{1,0:T(8,128)(2,1)} %refs_4_.3, ...), custom_call_target="tpu_custom_call" | custom-call | flops 805306368 | bytes 3936256 | tf_op jit(solution)/shard_map/pallas_call | solution.py:56
  129.6 0.0 all-to-all-done.2.refs_1_
  129.6 0.0 copy-done.7
  129.6 0.7 copy-done.8
  130.3 1.3 shard_map.107
  131.6 0.0 reduce-scatter.2.cloned.1.call-update
  131.6 28.7 %all_to_all.25.refs_0_ = f32[64,1,128]{2,1,0:T(1,128)S(1)} all-to-all(f32[64,1,128]{2,1,0:T(1,128)S(1)} %get-tuple-element.33), channel_id=1, replica_groups=mesh['head_0'=4,'head_1'=2,'seq_0'=4,'seq_1'=16] {'seq_0','seq_1'}, dimensions={0} | all-to-all | bytes 65536 | tf_op jit(solution)/shard_map/all_to_all | solution.py:313
  160.3 0.1 shard_map.108
  160.4 11.6 %all_to_all.26.refs_2_ = f32[8,1,128]{2,1,0:T(1,128)S(1)} all-to-all(f32[8,1,128]{2,1,0:T(1,128)S(1)} %shard_map.108), channel_id=1, replica_groups=mesh['head_0'=4,'head_1'=2,'seq_0'=4,'seq_1'=16] {'head_0','head_1'}, dimensions={0} | all-to-all | bytes 8192 | tf_op jit(solution)/shard_map/all_to_all | solution.py:313
  172.0 0.8 copy-done.4
  172.9 0.7 shard_map.109
  (14 shorter events, 0.0 us)
Async XLA Ops:
  7.2 22.2 %copy-start.2 = (bf16[512,512]{1,0:T(8,128)(2,1)S(1)}, bf16[512,512]{1,0:T(8,128)(2,1)}, u32[]{:S(2)}) copy-start(bf16[512,512]{1,0:T(8,128)(2,1)} %refs_5_.3) | copy-start | bytes 1572868
  7.2 22.2 %copy-start = (bf16[512,512]{1,0:T(8,128)(2,1)S(1)}, bf16[512,512]{1,0:T(8,128)(2,1)}, u32[]{:S(2)}) copy-start(bf16[512,512]{1,0:T(8,128)(2,1)} %refs_2_.5) | copy-start | bytes 1572868
  7.2 22.2 %copy-start.1 = (bf16[512,512]{1,0:T(8,128)(2,1)S(1)}, bf16[512,512]{1,0:T(8,128)(2,1)}, u32[]{:S(2)}) copy-start(bf16[512,512]{1,0:T(8,128)(2,1)} %refs_3_.5) | copy-start | bytes 1572868
  7.2 22.2 %copy-start.5 = (s32[18,32]{1,0:T(8,128)S(1)}, s32[18,32]{1,0:T(8,128)}, u32[]{:S(2)}) copy-start(s32[18,32]{1,0:T(8,128)} %refs_1_.7) | copy-start | bytes 6916
  10.0 38.4 %all-to-all-start = ((bf16[64,16,128]{2,1,0:T(8,128)(2,1)}), bf16[64,16,128]{2,1,0:T(8,128)(2,1)S(1)}, u32[]{:S(2)}, u32[]{:S(2)}) async-start(bf16[64,16,128]{2,1,0:T(8,128)(2,1)} %bitcast.7), calls=%async_computation | async-start | bytes 524288 | tf_op jit(solution)/shard_map/all_to_all | solution.py:313
  29.4 19.0 %copy-start.6 = (s32[4]{0:T(128)}, s32[4]{0:T(128)S(1)}, u32[]{:S(2)}) copy-start(s32[4]{0:T(128)S(1)} %pad_add_fusion.refs_0_) | copy-start | bytes 52
  36.8 28.4 %collective-permute-start = (bf16[2,2048,128]{2,1,0:T(8,128)(2,1)}, bf16[2,2048,128]{2,1,0:T(8,128)(2,1)S(1)}, u32[]{:S(2)}, u32[]{:S(2)}) collective-permute-start(bf16[2,2048,128]{2,1,0:T(8,128)(2,1)} %get-tuple-element.20), channel_id=1, source_target_pairs={{0,16},{16,32},{32,48},{48,0},{1,17},{17,33},{33,49},{49,1},{2,18}... | collective-permute-start | bytes 3145736 | tf_op jit(solution)/shard_map/ppermute | solution.py:309
  39.7 48.4 %collective-permute-start.1 = (bf16[2,2048,128]{2,1,0:T(8,128)(2,1)}, bf16[2,2048,128]{2,1,0:T(8,128)(2,1)S(1)}, u32[]{:S(2)}, u32[]{:S(2)}) collective-permute-start(bf16[2,2048,128]{2,1,0:T(8,128)(2,1)} %get-tuple-element.21), channel_id=1, source_target_pairs={{0,32},{16,48},{32,0},{48,16},{1,33},{17,49},{33,1},{49,17},{2,34}... | collective-permute-start | bytes 3145736 | tf_op jit(solution)/shard_map/ppermute | solution.py:309
  44.2 45.3 %collective-permute-start.2 = (bf16[2,2048,128]{2,1,0:T(8,128)(2,1)}, bf16[2,2048,128]{2,1,0:T(8,128)(2,1)}, u32[]{:S(2)}, u32[]{:S(2)}) collective-permute-start(bf16[2,2048,128]{2,1,0:T(8,128)(2,1)} %get-tuple-element.22), channel_id=1, source_target_pairs={{0,48},{16,0},{32,16},{48,32},{1,49},{17,1},{33,17},{49,33},{2,50}... | collective-permute-start | bytes 3145736 | tf_op jit(solution)/shard_map/ppermute | solution.py:309
  49.9 39.6 %all-to-all-start.1 = ((bf16[16,4,16,128]{3,2,1,0:T(8,128)(2,1)}), bf16[16,4,16,128]{3,2,1,0:T(8,128)(2,1)S(1)}, u32[]{:S(2)}, u32[]{:S(2)}) async-start(bf16[16,4,16,128]{3,2,1,0:T(8,128)(2,1)} %shard_map.104), calls=%async_computation.1 | async-start | bytes 524288 | tf_op jit(solution)/shard_map/all_to_all | solution.py:313
  65.2 24.3 %copy-start.9 = (bf16[2,2048,128]{2,1,0:T(8,128)(2,1)}, bf16[2,2048,128]{2,1,0:T(8,128)(2,1)S(1)}, u32[]{:S(2)}) copy-start(bf16[2,2048,128]{2,1,0:T(8,128)(2,1)S(1)} %collective-permute-done.refs_2_) | copy-start | bytes 3145732
  88.1 1.4 copy-start.10
  89.5 0.7 copy-start.11
  94.7 34.9 %copy-start.7 = (s32[4]{0:T(128)S(1)}, s32[4]{0:T(128)}, u32[]{:S(2)}) copy-start(s32[4]{0:T(128)} %copy-done.6) | copy-start | bytes 52
  94.7 34.9 %all-to-all-start.2 = ((bf16[16,128,128]{2,1,0:T(8,128)(2,1)}), bf16[16,128,128]{2,1,0:T(8,128)(2,1)S(1)}, u32[]{:S(2)}, u32[]{:S(2)}) async-start(bf16[16,128,128]{2,1,0:T(8,128)(2,1)} %get-tuple-element.30), calls=%async_computation.2 | async-start | bytes 1048576 | tf_op jit(solution)/shard_map/all_to_all | solution.py:313
  105.6 66.4 %copy-start.3 = (f32[32,512]{1,0:T(8,128)S(1)}, f32[32,512]{1,0:T(8,128)}, u32[]{:S(2)}) copy-start(f32[32,512]{1,0:T(8,128)} %refs_0_.3) | copy-start | bytes 196612
  105.6 66.4 %reduce-scatter.2.cloned.1.call-start = ((), (), s32[]{:S(2)}) async-start(), calls=%async_computation.6 | async-start | bytes 327680 | tf_op jit(solution)/shard_map/reduce_scatter | solution.py:417
  105.6 11.6 %collective-permute-start.3 = (bf16[16,16,128]{2,1,0:T(8,128)(2,1)}, bf16[16,16,128]{2,1,0:T(8,128)(2,1)S(1)}, u32[]{:S(2)}, u32[]{:S(2)}) collective-permute-start(bf16[16,16,128]{2,1,0:T(8,128)(2,1)} %get-tuple-element.24), channel_id=1, source_target_pairs={{0,16},{16,32},{32,48},{48,0},{1,17},{17,33},{33,49},{49,1},{2,18}... | collective-permute-start | bytes 196616 | tf_op jit(solution)/shard_map/ppermute | solution.py:309
  110.8 7.0 %collective-permute-start.4 = (bf16[16,16,128]{2,1,0:T(8,128)(2,1)}, bf16[16,16,128]{2,1,0:T(8,128)(2,1)S(1)}, u32[]{:S(2)}, u32[]{:S(2)}) collective-permute-start(bf16[16,16,128]{2,1,0:T(8,128)(2,1)} %get-tuple-element.25), channel_id=1, source_target_pairs={{0,32},{16,48},{32,0},{48,16},{1,33},{17,49},{33,1},{49,17},{2,34}... | collective-permute-start | bytes 196616 | tf_op jit(solution)/shard_map/ppermute | solution.py:309
  114.1 5.5 %collective-permute-start.5 = (bf16[16,16,128]{2,1,0:T(8,128)(2,1)}, bf16[16,16,128]{2,1,0:T(8,128)(2,1)S(1)}, u32[]{:S(2)}, u32[]{:S(2)}) collective-permute-start(bf16[16,16,128]{2,1,0:T(8,128)(2,1)} %get-tuple-element.26), channel_id=1, source_target_pairs={{0,48},{16,0},{32,16},{48,32},{1,49},{17,1},{33,17},{49,33},{2,50}... | collective-permute-start | bytes 196616 | tf_op jit(solution)/shard_map/ppermute | solution.py:309
  117.2 2.4 %copy-start.12 = (bf16[16,16,128]{2,1,0:T(8,128)(2,1)}, bf16[16,16,128]{2,1,0:T(8,128)(2,1)S(1)}, u32[]{:S(2)}) copy-start(bf16[16,16,128]{2,1,0:T(8,128)(2,1)S(1)} %collective-permute-done.3.refs_7_) | copy-start | bytes 196612
  117.8 1.8 copy-start.13
  119.6 0.6 copy-start.14
  129.6 0.7 copy-start.8
  172.0 0.8 copy-start.4
Sparse Core Ops, SparseCore 0:
  131.8 29.1 reduce-scatter.1

commit v8 on v7

--- a/solution.py
+++ b/solution.py
@@ -357,7 +357,8 @@
     )
     slices = (n_y * n_z, 2 * D // n_z, D)
     both = swap(both.reshape(slices), SEQ)
-    keyed = [keyed[0]] + [shift(keyed[n], Y, n) for n in range(1, n_y)]
+    gone = {n: shift(keyed[n], Y, n) for n in sorted(range(1, n_y), key=lambda n: abs(n - n_y // 2))}
+    keyed = [keyed[0]] + [gone[n] for n in range(1, n_y)]
 
     both = call(
         tree_kernel,
@@ -388,7 +389,7 @@
             dma((n_y,)),
         ],
         scalars=(info,),
-        vmem=VMEM_ALL,
+        vmem=52,
     )
     parts = swap(parts, Z)
 
@@ -399,10 +400,10 @@
         (queries, keys, values, out_grad, *own),
         6 * length * length * width,
         scalars=(info, level_weight),
-        vmem=VMEM_ALL,
-    )
-
-    near, rest = SEQ, HEAD
+        vmem=52,
+    )
+
+    near, rest = HEAD + (Y,), (Z,)
     rows = momentum.shape[0]
     square, shard = call(
         shard_kernel,

time: 181 us -> 176 us (0.972)
  local copies, waits for them, and re-layouts: 2.88 us -> 0.87 us
    unnamed x30 -> x16, local copies, waits for them, and re-layouts: 2.88 us -> 0.87 us
where the time goes in v8:
time: 176 us
  starting transfers between devices  62.4 us (35%)
  blocking collectives  38.9 us (22%)
  waiting for transfers between devices  32.6 us (19%)
  Pallas kernels  26.5 us (15%)
  between operations  14.2 us (8%)
    all_to_all x3, starting transfers between devices, swap(): return lax.all_to_all(x, axes, 0, 0, tiled=True)  40.4 us
    all_to_all x2, blocking collectives, swap(): return lax.all_to_all(x, axes, 0, 0, tiled=True)  38.9 us
    ppermute x6, waiting for transfers between devices, shift(): return lax.ppermute(x, axis, [(i, (i + by) % n) for i in range(n)])  31.5 us
    pallas_call x8, Pallas kernels, call(): pl.pallas_call(run, out_shape=out_shape, grid_spec=pltpu.PrefetchScalarGr...  26.5 us
    ppermute x6, starting transfers between devices, shift(): return lax.ppermute(x, axis, [(i, (i + by) % n) for i in range(n)])  22 us
  transfers between devices with their start and end apart: 10, of which 6 were waited for; matrix products, arithmetic and copies ran while one was open for 0% of the time, Pallas kernels for 10%

profile of v8, /device:TPU:1, one launch (start us, length us, event | category | flops | bytes accessed | tf_op | source)
XLA Modules:
  0.0 175.6 jit_solution(15238932453294488129)
XLA Ops:
  7.2 0.0 copy-start.3
  7.2 0.0 copy-start
  7.2 0.0 copy-start.1
  7.2 0.0 copy-start.6
  7.2 2.8 %shard_map.103 = bf16[4,256,128]{2,1,0:T(8,128)(2,1)} custom-call(bf16[512,512]{1,0:T(8,128)(2,1)} %refs_2_.5, bf16[512,512]{1,0:T(8,128)(2,1)} %refs_5_.3, bf16[512,512]{1,0:T(8,128)(2,1)} %refs_3_.5, bf16[512,512]{1,0:T(8,128)(2,1)} %refs_4_.3), custom_call_target="tpu_custom_call" | custom-call | flops 134217728 | bytes 2359296 | tf_op jit(solution)/shard_map/pallas_call | solution.py:56
  10.0 19.3 %all-to-all-start = ((bf16[64,16,128]{2,1,0:T(8,128)(2,1)}), bf16[64,16,128]{2,1,0:T(8,128)(2,1)S(1)}, u32[]{:S(2)}, u32[]{:S(2)}) async-start(bf16[64,16,128]{2,1,0:T(8,128)(2,1)} %bitcast.7), calls=%async_computation | async-start | bytes 524288 | tf_op jit(solution)/shard_map/all_to_all | solution.py:313
  29.3 0.1 pad_add_fusion.refs_0_
  29.4 0.0 copy-done.3
  29.4 0.0 copy-done
  29.4 0.0 copy-done.1
  29.4 0.0 copy-done.6
  29.4 7.4 %shard_map.102 = (bf16[2,2048,128]{2,1,0:T(8,128)(2,1)}, bf16[2,2048,128]{2,1,0:T(8,128)(2,1)}, bf16[2,2048,128]{2,1,0:T(8,128)(2,1)}, bf16[2,2048,128]{2,1,0:T(8,128)(2,1)}) custom-call(s32[4]{0:T(128)S(1)} %pad_add_fusion.refs_0_, s32[18,32]{1,0:T(8,128)S(1)} %copy-done.6, bf16[512,512]{1,0:T(8,128)(2,1)S(1)} %copy-done, bf16[512,512]{1,0:T(8,128)(2,1)S(1)} %copy-done.1, ...), custom_call_target="tpu_custom_call" | custom-call | flops 2550136832 | bytes 7864320 | tf_op jit(solution)/shard_map/pallas_call | solution.py:56
  36.8 2.9 %collective-permute-start = (bf16[2,2048,128]{2,1,0:T(8,128)(2,1)}, bf16[2,2048,128]{2,1,0:T(8,128)(2,1)S(1)}, u32[]{:S(2)}, u32[]{:S(2)}) collective-permute-start(bf16[2,2048,128]{2,1,0:T(8,128)(2,1)} %get-tuple-element.20), channel_id=1, source_target_pairs={{0,16},{16,32},{32,48},{48,0},{1,17},{17,33},{33,49},{49,1},{2,18}... | collective-permute-start | bytes 3145736 | tf_op jit(solution)/shard_map/ppermute | solution.py:309
  39.7 4.5 %collective-permute-start.1 = (bf16[2,2048,128]{2,1,0:T(8,128)(2,1)}, bf16[2,2048,128]{2,1,0:T(8,128)(2,1)}, u32[]{:S(2)}, u32[]{:S(2)}) collective-permute-start(bf16[2,2048,128]{2,1,0:T(8,128)(2,1)} %get-tuple-element.21), channel_id=1, source_target_pairs={{0,32},{16,48},{32,0},{48,16},{1,33},{17,49},{33,1},{49,17},{2,34}... | collective-permute-start | bytes 3145736 | tf_op jit(solution)/shard_map/ppermute | solution.py:309
  44.2 3.0 %collective-permute-start.2 = (bf16[2,2048,128]{2,1,0:T(8,128)(2,1)}, bf16[2,2048,128]{2,1,0:T(8,128)(2,1)}, u32[]{:S(2)}, u32[]{:S(2)}) collective-permute-start(bf16[2,2048,128]{2,1,0:T(8,128)(2,1)} %get-tuple-element.22), channel_id=1, source_target_pairs={{0,48},{16,0},{32,16},{48,32},{1,49},{17,1},{33,17},{49,33},{2,50}... | collective-permute-start | bytes 3145736 | tf_op jit(solution)/shard_map/ppermute | solution.py:309
  47.2 1.1 all-to-all-done.refs_2_
  48.3 1.6 shard_map.104
  49.9 10.2 %all-to-all-start.1 = ((bf16[16,4,16,128]{3,2,1,0:T(8,128)(2,1)}), bf16[16,4,16,128]{3,2,1,0:T(8,128)(2,1)S(1)}, u32[]{:S(2)}, u32[]{:S(2)}) async-start(bf16[16,4,16,128]{3,2,1,0:T(8,128)(2,1)} %shard_map.104), calls=%async_computation.1 | async-start | bytes 524288 | tf_op jit(solution)/shard_map/all_to_all | solution.py:313
  60.1 5.0 %collective-permute-done.refs_2_ = bf16[2,2048,128]{2,1,0:T(8,128)(2,1)S(1)} collective-permute-done((bf16[2,2048,128]{2,1,0:T(8,128)(2,1)}, bf16[2,2048,128]{2,1,0:T(8,128)(2,1)S(1)}, u32[]{:S(2)}, u32[]{:S(2)}) %collective-permute-start) | collective-permute-done | bytes 1048608 | tf_op jit(solution)/shard_map/ppermute | solution.py:309
  65.2 0.0 copy-start.7
  65.2 23.0 %collective-permute-done.1.refs_3_ = bf16[2,2048,128]{2,1,0:T(8,128)(2,1)} collective-permute-done((bf16[2,2048,128]{2,1,0:T(8,128)(2,1)}, bf16[2,2048,128]{2,1,0:T(8,128)(2,1)}, u32[]{:S(2)}, u32[]{:S(2)}) %collective-permute-start.1) | collective-permute-done | bytes 1048608 | tf_op jit(solution)/shard_map/ppermute | solution.py:309
  88.2 1.3 collective-permute-done.2.refs_4_
  89.5 0.0 all-to-all-done.1.refs_5_
  89.5 0.0 copy-done.7
  89.5 0.0 copy-start.2
  89.5 4.0 %shard_map.105 = (bf16[16,128,128]{2,1,0:T(8,128)(2,1)}, bf16[16,16,128]{2,1,0:T(8,128)(2,1)S(1)}, bf16[16,16,128]{2,1,0:T(8,128)(2,1)S(1)}, bf16[16,16,128]{2,1,0:T(8,128)(2,1)S(1)}, bf16[16,16,128]{2,1,0:T(8,128)(2,1)S(1)}) custom-call(s32[4]{0:T(128)S(1)} %pad_add_fusion.refs_0_, bf16[2,2048,128]{2,1,0:T(8,128)(2,1)} %get-tuple-element.19.refs_1_, ...), custom_call_target="tpu_custom_call" | custom-call | flops 268435456 | bytes 5242880 | tf_op jit(solution)/shard_map/pallas_call | solution.py:56
  93.5 10.9 %all-to-all-start.2 = ((bf16[16,128,128]{2,1,0:T(8,128)(2,1)}), bf16[16,128,128]{2,1,0:T(8,128)(2,1)S(1)}, u32[]{:S(2)}, u32[]{:S(2)}) async-start(bf16[16,128,128]{2,1,0:T(8,128)(2,1)} %get-tuple-element.30), calls=%async_computation.2 | async-start | bytes 1048576 | tf_op jit(solution)/shard_map/all_to_all | solution.py:313
  104.4 0.0 copy-start.4
  104.4 0.0 reduce-scatter.2.cloned.1.call-start
  104.4 5.2 %collective-permute-start.3 = (bf16[16,16,128]{2,1,0:T(8,128)(2,1)S(1)}, bf16[16,16,128]{2,1,0:T(8,128)(2,1)S(1)}, u32[]{:S(2)}, u32[]{:S(2)}) collective-permute-start(bf16[16,16,128]{2,1,0:T(8,128)(2,1)S(1)} %get-tuple-element.24), channel_id=1, source_target_pairs={{0,16},{16,32},{32,48},{48,0},{1,17},{17,33},{33,49},{49,1},{2,18}... | collective-permute-start | bytes 196616 | tf_op jit(solution)/shard_map/ppermute | solution.py:309
  109.6 3.2 %collective-permute-start.4 = (bf16[16,16,128]{2,1,0:T(8,128)(2,1)S(1)}, bf16[16,16,128]{2,1,0:T(8,128)(2,1)S(1)}, u32[]{:S(2)}, u32[]{:S(2)}) collective-permute-start(bf16[16,16,128]{2,1,0:T(8,128)(2,1)S(1)} %get-tuple-element.25), channel_id=1, source_target_pairs={{0,32},{16,48},{32,0},{48,16},{1,33},{17,49},{33,1},{49,17},{2,34}... | collective-permute-start | bytes 196616 | tf_op jit(solution)/shard_map/ppermute | solution.py:309
  112.9 3.2 %collective-permute-start.5 = (bf16[16,16,128]{2,1,0:T(8,128)(2,1)S(1)}, bf16[16,16,128]{2,1,0:T(8,128)(2,1)S(1)}, u32[]{:S(2)}, u32[]{:S(2)}) collective-permute-start(bf16[16,16,128]{2,1,0:T(8,128)(2,1)S(1)} %get-tuple-element.26), channel_id=1, source_target_pairs={{0,48},{16,0},{32,16},{48,32},{1,49},{17,1},{33,17},{49,33},{2,50}... | collective-permute-start | bytes 196616 | tf_op jit(solution)/shard_map/ppermute | solution.py:309
  116.0 0.0 collective-permute-done.3.refs_7_
  116.1 0.4 collective-permute-done.4.refs_8_
  116.4 1.8 collective-permute-done.5.refs_9_
  118.2 0.0 copy-done.2
  118.2 8.8 %shard_map.106 = (bf16[512,512]{1,0:T(8,128)(2,1)}, bf16[512,512]{1,0:T(8,128)(2,1)}, bf16[512,512]{1,0:T(8,128)(2,1)}, f32[8,128]{1,0:T(8,128)S(1)}) custom-call(s32[4]{0:T(128)S(1)} %pad_add_fusion.refs_0_, s32[18,32]{1,0:T(8,128)S(1)} %copy-done.6, bf16[512,512]{1,0:T(8,128)(2,1)S(1)} %copy-done, bf16[512,512]{1,0:T(8,128)(2,1)S(1)} %copy-done.1, ...), custom_call_target="tpu_custom_call" | custom-call | flops 805306368 | bytes 3936256 | tf_op jit(solution)/shard_map/pallas_call | solution.py:56
  126.9 0.0 all-to-all-done.2.refs_1_
  126.9 1.3 shard_map.107
  128.3 0.0 reduce-scatter.2.cloned.1.call-update
  128.3 21.7 %all_to_all.25.refs_0_ = f32[32,1,128]{2,1,0:T(1,128)S(1)} all-to-all(f32[32,1,128]{2,1,0:T(1,128)S(1)} %get-tuple-element.33), channel_id=1, replica_groups=mesh['head_0'=4,'head_1'=2,'seq_0'=4,'seq_1'=16] {'head_0','head_1','seq..., dimensions={0} | all-to-all | bytes 32768 | tf_op jit(solution)/shard_map/all_to_all | solution.py:313
  150.1 17.2 %all_to_all.26.refs_2_ = f32[16,1,128]{2,1,0:T(1,128)S(1)} all-to-all(f32[16,1,128]{2,1,0:T(1,128)S(1)} %shard_map.108), channel_id=1, replica_groups=mesh['head_0'=4,'head_1'=2,'seq_0'=4,'seq_1'=16] {'seq_1'}, dimensions={0} | all-to-all | bytes 16384 | tf_op jit(solution)/shard_map/all_to_all | solution.py:313
  167.3 0.0 reduce-scatter.2.cloned.1.call-done
  167.3 0.0 copy-done.4
  167.3 0.0 copy-start.5
  167.3 0.8 copy-done.5
  168.1 0.7 shard_map.109
  (1 shorter events, 0.0 us)
Async XLA Ops:
  7.2 22.2 %copy-start.3 = (bf16[512,512]{1,0:T(8,128)(2,1)S(1)}, bf16[512,512]{1,0:T(8,128)(2,1)}, u32[]{:S(2)}) copy-start(bf16[512,512]{1,0:T(8,128)(2,1)} %refs_5_.3) | copy-start | bytes 1572868
  7.2 22.2 %copy-start = (bf16[512,512]{1,0:T(8,128)(2,1)S(1)}, bf16[512,512]{1,0:T(8,128)(2,1)}, u32[]{:S(2)}) copy-start(bf16[512,512]{1,0:T(8,128)(2,1)} %refs_2_.5) | copy-start | bytes 1572868
  7.2 22.2 %copy-start.1 = (bf16[512,512]{1,0:T(8,128)(2,1)S(1)}, bf16[512,512]{1,0:T(8,128)(2,1)}, u32[]{:S(2)}) copy-start(bf16[512,512]{1,0:T(8,128)(2,1)} %refs_3_.5) | copy-start | bytes 1572868
  7.2 22.2 %copy-start.6 = (s32[18,32]{1,0:T(8,128)S(1)}, s32[18,32]{1,0:T(8,128)}, u32[]{:S(2)}) copy-start(s32[18,32]{1,0:T(8,128)} %refs_1_.7) | copy-start | bytes 6916
  10.0 38.4 %all-to-all-start = ((bf16[64,16,128]{2,1,0:T(8,128)(2,1)}), bf16[64,16,128]{2,1,0:T(8,128)(2,1)S(1)}, u32[]{:S(2)}, u32[]{:S(2)}) async-start(bf16[64,16,128]{2,1,0:T(8,128)(2,1)} %bitcast.7), calls=%async_computation | async-start | bytes 524288 | tf_op jit(solution)/shard_map/all_to_all | solution.py:313
  36.8 28.4 %collective-permute-start = (bf16[2,2048,128]{2,1,0:T(8,128)(2,1)}, bf16[2,2048,128]{2,1,0:T(8,128)(2,1)S(1)}, u32[]{:S(2)}, u32[]{:S(2)}) collective-permute-start(bf16[2,2048,128]{2,1,0:T(8,128)(2,1)} %get-tuple-element.20), channel_id=1, source_target_pairs={{0,16},{16,32},{32,48},{48,0},{1,17},{17,33},{33,49},{49,1},{2,18}... | collective-permute-start | bytes 3145736 | tf_op jit(solution)/shard_map/ppermute | solution.py:309
  39.7 48.5 %collective-permute-start.1 = (bf16[2,2048,128]{2,1,0:T(8,128)(2,1)}, bf16[2,2048,128]{2,1,0:T(8,128)(2,1)}, u32[]{:S(2)}, u32[]{:S(2)}) collective-permute-start(bf16[2,2048,128]{2,1,0:T(8,128)(2,1)} %get-tuple-element.21), channel_id=1, source_target_pairs={{0,32},{16,48},{32,0},{48,16},{1,33},{17,49},{33,1},{49,17},{2,34}... | collective-permute-start | bytes 3145736 | tf_op jit(solution)/shard_map/ppermute | solution.py:309
  44.2 45.3 %collective-permute-start.2 = (bf16[2,2048,128]{2,1,0:T(8,128)(2,1)}, bf16[2,2048,128]{2,1,0:T(8,128)(2,1)}, u32[]{:S(2)}, u32[]{:S(2)}) collective-permute-start(bf16[2,2048,128]{2,1,0:T(8,128)(2,1)} %get-tuple-element.22), channel_id=1, source_target_pairs={{0,48},{16,0},{32,16},{48,32},{1,49},{17,1},{33,17},{49,33},{2,50}... | collective-permute-start | bytes 3145736 | tf_op jit(solution)/shard_map/ppermute | solution.py:309
  49.9 39.6 %all-to-all-start.1 = ((bf16[16,4,16,128]{3,2,1,0:T(8,128)(2,1)}), bf16[16,4,16,128]{3,2,1,0:T(8,128)(2,1)S(1)}, u32[]{:S(2)}, u32[]{:S(2)}) async-start(bf16[16,4,16,128]{3,2,1,0:T(8,128)(2,1)} %shard_map.104), calls=%async_computation.1 | async-start | bytes 524288 | tf_op jit(solution)/shard_map/all_to_all | solution.py:313
  65.2 24.3 %copy-start.7 = (bf16[2,2048,128]{2,1,0:T(8,128)(2,1)}, bf16[2,2048,128]{2,1,0:T(8,128)(2,1)S(1)}, u32[]{:S(2)}) copy-start(bf16[2,2048,128]{2,1,0:T(8,128)(2,1)S(1)} %collective-permute-done.refs_2_) | copy-start | bytes 3145732
  89.5 28.7 %copy-start.2 = (bf16[512,512]{1,0:T(8,128)(2,1)S(1)}, bf16[512,512]{1,0:T(8,128)(2,1)}, u32[]{:S(2)}) copy-start(bf16[512,512]{1,0:T(8,128)(2,1)} %refs_4_.3) | copy-start | bytes 1572868
  93.5 33.4 %all-to-all-start.2 = ((bf16[16,128,128]{2,1,0:T(8,128)(2,1)}), bf16[16,128,128]{2,1,0:T(8,128)(2,1)S(1)}, u32[]{:S(2)}, u32[]{:S(2)}) async-start(bf16[16,128,128]{2,1,0:T(8,128)(2,1)} %get-tuple-element.30), calls=%async_computation.2 | async-start | bytes 1048576 | tf_op jit(solution)/shard_map/all_to_all | solution.py:313
  104.4 62.9 %copy-start.4 = (f32[32,512]{1,0:T(8,128)S(1)}, f32[32,512]{1,0:T(8,128)}, u32[]{:S(2)}) copy-start(f32[32,512]{1,0:T(8,128)} %refs_0_.3) | copy-start | bytes 196612
  104.4 62.9 %reduce-scatter.2.cloned.1.call-start = ((), (), s32[]{:S(2)}) async-start(), calls=%async_computation.6 | async-start | bytes 327680 | tf_op jit(solution)/shard_map/reduce_scatter | solution.py:418
  104.4 11.6 %collective-permute-start.3 = (bf16[16,16,128]{2,1,0:T(8,128)(2,1)S(1)}, bf16[16,16,128]{2,1,0:T(8,128)(2,1)S(1)}, u32[]{:S(2)}, u32[]{:S(2)}) collective-permute-start(bf16[16,16,128]{2,1,0:T(8,128)(2,1)S(1)} %get-tuple-element.24), channel_id=1, source_target_pairs={{0,16},{16,32},{32,48},{48,0},{1,17},{17,33},{33,49},{49,1},{2,18}... | collective-permute-start | bytes 196616 | tf_op jit(solution)/shard_map/ppermute | solution.py:309
  109.6 6.8 %collective-permute-start.4 = (bf16[16,16,128]{2,1,0:T(8,128)(2,1)S(1)}, bf16[16,16,128]{2,1,0:T(8,128)(2,1)S(1)}, u32[]{:S(2)}, u32[]{:S(2)}) collective-permute-start(bf16[16,16,128]{2,1,0:T(8,128)(2,1)S(1)} %get-tuple-element.25), channel_id=1, source_target_pairs={{0,32},{16,48},{32,0},{48,16},{1,33},{17,49},{33,1},{49,17},{2,34}... | collective-permute-start | bytes 196616 | tf_op jit(solution)/shard_map/ppermute | solution.py:309
  112.9 5.3 %collective-permute-start.5 = (bf16[16,16,128]{2,1,0:T(8,128)(2,1)S(1)}, bf16[16,16,128]{2,1,0:T(8,128)(2,1)S(1)}, u32[]{:S(2)}, u32[]{:S(2)}) collective-permute-start(bf16[16,16,128]{2,1,0:T(8,128)(2,1)S(1)} %get-tuple-element.26), channel_id=1, source_target_pairs={{0,48},{16,0},{32,16},{48,32},{1,49},{17,1},{33,17},{49,33},{2,50}... | collective-permute-start | bytes 196616 | tf_op jit(solution)/shard_map/ppermute | solution.py:309
  167.3 0.8 copy-start.5
Sparse Core Ops, SparseCore 0:
  128.4 28.9 reduce-scatter.1

commit v9 on v8

--- a/solution.py
+++ b/solution.py
@@ -403,7 +403,7 @@
         vmem=52,
     )
 
-    near, rest = HEAD + (Y,), (Z,)
+    near, rest = (Z,), HEAD + (Y,)
     rows = momentum.shape[0]
     square, shard = call(
         shard_kernel,

time: 176 us -> 178 us (1.011)
  no operation moved by 1% of the time
where the time goes in v9:
time: 178 us; the launch traced here: 177 us
  starting transfers between devices  62.4 us (35%)
  blocking collectives  40.3 us (23%)
  waiting for transfers between devices  32.6 us (18%)
  Pallas kernels  26.5 us (15%)
  between operations  14.2 us (8%)
    all_to_all x3, starting transfers between devices, swap(): return lax.all_to_all(x, axes, 0, 0, tiled=True)  40.4 us
    all_to_all x2, blocking collectives, swap(): return lax.all_to_all(x, axes, 0, 0, tiled=True)  40.3 us
    ppermute x6, waiting for transfers between devices, shift(): return lax.ppermute(x, axis, [(i, (i + by) % n) for i in range(n)])  31.5 us
    pallas_call x8, Pallas kernels, call(): pl.pallas_call(run, out_shape=out_shape, grid_spec=pltpu.PrefetchScalarGr...  26.5 us
    ppermute x6, starting transfers between devices, shift(): return lax.ppermute(x, axis, [(i, (i + by) % n) for i in range(n)])  22 us
  transfers between devices with their start and end apart: 10, of which 6 were waited for; matrix products, arithmetic and copies ran while one was open for 0% of the time, Pallas kernels for 10%

profile of v9, /device:TPU:1, one launch (start us, length us, event | category | flops | bytes accessed | tf_op | source)
XLA Modules:
  0.0 177.1 jit_solution(10330145315220625193)
XLA Ops:
  7.2 0.0 copy-start.3
  7.2 0.0 copy-start
  7.2 0.0 copy-start.1
  7.2 0.0 copy-start.6
  7.2 2.8 %shard_map.103 = bf16[4,256,128]{2,1,0:T(8,128)(2,1)} custom-call(bf16[512,512]{1,0:T(8,128)(2,1)} %refs_2_.5, bf16[512,512]{1,0:T(8,128)(2,1)} %refs_5_.3, bf16[512,512]{1,0:T(8,128)(2,1)} %refs_3_.5, bf16[512,512]{1,0:T(8,128)(2,1)} %refs_4_.3), custom_call_target="tpu_custom_call" | custom-call | flops 134217728 | bytes 2359296 | tf_op jit(solution)/shard_map/pallas_call | solution.py:56
  10.0 19.3 %all-to-all-start = ((bf16[64,16,128]{2,1,0:T(8,128)(2,1)}), bf16[64,16,128]{2,1,0:T(8,128)(2,1)S(1)}, u32[]{:S(2)}, u32[]{:S(2)}) async-start(bf16[64,16,128]{2,1,0:T(8,128)(2,1)} %bitcast.7), calls=%async_computation | async-start | bytes 524288 | tf_op jit(solution)/shard_map/all_to_all | solution.py:313
  29.3 0.1 pad_add_fusion.refs_0_
  29.4 0.0 copy-done.3
  29.4 0.0 copy-done
  29.4 0.0 copy-done.1
  29.4 0.0 copy-done.6
  29.4 7.4 %shard_map.102 = (bf16[2,2048,128]{2,1,0:T(8,128)(2,1)}, bf16[2,2048,128]{2,1,0:T(8,128)(2,1)}, bf16[2,2048,128]{2,1,0:T(8,128)(2,1)}, bf16[2,2048,128]{2,1,0:T(8,128)(2,1)}) custom-call(s32[4]{0:T(128)S(1)} %pad_add_fusion.refs_0_, s32[18,32]{1,0:T(8,128)S(1)} %copy-done.6, bf16[512,512]{1,0:T(8,128)(2,1)S(1)} %copy-done, bf16[512,512]{1,0:T(8,128)(2,1)S(1)} %copy-done.1, ...), custom_call_target="tpu_custom_call" | custom-call | flops 2550136832 | bytes 7864320 | tf_op jit(solution)/shard_map/pallas_call | solution.py:56
  36.8 2.9 %collective-permute-start = (bf16[2,2048,128]{2,1,0:T(8,128)(2,1)}, bf16[2,2048,128]{2,1,0:T(8,128)(2,1)S(1)}, u32[]{:S(2)}, u32[]{:S(2)}) collective-permute-start(bf16[2,2048,128]{2,1,0:T(8,128)(2,1)} %get-tuple-element.20), channel_id=1, source_target_pairs={{0,16},{16,32},{32,48},{48,0},{1,17},{17,33},{33,49},{49,1},{2,18}... | collective-permute-start | bytes 3145736 | tf_op jit(solution)/shard_map/ppermute | solution.py:309
  39.7 4.5 %collective-permute-start.1 = (bf16[2,2048,128]{2,1,0:T(8,128)(2,1)}, bf16[2,2048,128]{2,1,0:T(8,128)(2,1)}, u32[]{:S(2)}, u32[]{:S(2)}) collective-permute-start(bf16[2,2048,128]{2,1,0:T(8,128)(2,1)} %get-tuple-element.21), channel_id=1, source_target_pairs={{0,32},{16,48},{32,0},{48,16},{1,33},{17,49},{33,1},{49,17},{2,34}... | collective-permute-start | bytes 3145736 | tf_op jit(solution)/shard_map/ppermute | solution.py:309
  44.2 3.0 %collective-permute-start.2 = (bf16[2,2048,128]{2,1,0:T(8,128)(2,1)}, bf16[2,2048,128]{2,1,0:T(8,128)(2,1)}, u32[]{:S(2)}, u32[]{:S(2)}) collective-permute-start(bf16[2,2048,128]{2,1,0:T(8,128)(2,1)} %get-tuple-element.22), channel_id=1, source_target_pairs={{0,48},{16,0},{32,16},{48,32},{1,49},{17,1},{33,17},{49,33},{2,50}... | collective-permute-start | bytes 3145736 | tf_op jit(solution)/shard_map/ppermute | solution.py:309
  47.2 1.1 all-to-all-done.refs_2_
  48.3 1.6 shard_map.104
  49.9 10.2 %all-to-all-start.1 = ((bf16[16,4,16,128]{3,2,1,0:T(8,128)(2,1)}), bf16[16,4,16,128]{3,2,1,0:T(8,128)(2,1)S(1)}, u32[]{:S(2)}, u32[]{:S(2)}) async-start(bf16[16,4,16,128]{3,2,1,0:T(8,128)(2,1)} %shard_map.104), calls=%async_computation.1 | async-start | bytes 524288 | tf_op jit(solution)/shard_map/all_to_all | solution.py:313
  60.1 5.0 %collective-permute-done.refs_2_ = bf16[2,2048,128]{2,1,0:T(8,128)(2,1)S(1)} collective-permute-done((bf16[2,2048,128]{2,1,0:T(8,128)(2,1)}, bf16[2,2048,128]{2,1,0:T(8,128)(2,1)S(1)}, u32[]{:S(2)}, u32[]{:S(2)}) %collective-permute-start) | collective-permute-done | bytes 1048608 | tf_op jit(solution)/shard_map/ppermute | solution.py:309
  65.2 0.0 copy-start.7
  65.2 23.0 %collective-permute-done.1.refs_3_ = bf16[2,2048,128]{2,1,0:T(8,128)(2,1)} collective-permute-done((bf16[2,2048,128]{2,1,0:T(8,128)(2,1)}, bf16[2,2048,128]{2,1,0:T(8,128)(2,1)}, u32[]{:S(2)}, u32[]{:S(2)}) %collective-permute-start.1) | collective-permute-done | bytes 1048608 | tf_op jit(solution)/shard_map/ppermute | solution.py:309
  88.2 1.3 collective-permute-done.2.refs_4_
  89.5 0.0 all-to-all-done.1.refs_5_
  89.5 0.0 copy-done.7
  89.5 0.0 copy-start.2
  89.5 4.0 %shard_map.105 = (bf16[16,128,128]{2,1,0:T(8,128)(2,1)}, bf16[16,16,128]{2,1,0:T(8,128)(2,1)S(1)}, bf16[16,16,128]{2,1,0:T(8,128)(2,1)S(1)}, bf16[16,16,128]{2,1,0:T(8,128)(2,1)S(1)}, bf16[16,16,128]{2,1,0:T(8,128)(2,1)S(1)}) custom-call(s32[4]{0:T(128)S(1)} %pad_add_fusion.refs_0_, bf16[2,2048,128]{2,1,0:T(8,128)(2,1)} %get-tuple-element.19.refs_1_, ...), custom_call_target="tpu_custom_call" | custom-call | flops 268435456 | bytes 5242880 | tf_op jit(solution)/shard_map/pallas_call | solution.py:56
  93.5 10.9 %all-to-all-start.2 = ((bf16[16,128,128]{2,1,0:T(8,128)(2,1)}), bf16[16,128,128]{2,1,0:T(8,128)(2,1)S(1)}, u32[]{:S(2)}, u32[]{:S(2)}) async-start(bf16[16,128,128]{2,1,0:T(8,128)(2,1)} %get-tuple-element.30), calls=%async_computation.2 | async-start | bytes 1048576 | tf_op jit(solution)/shard_map/all_to_all | solution.py:313
  104.4 0.0 copy-start.4
  104.4 0.0 reduce-scatter.2.cloned.1.call-start
  104.4 5.2 %collective-permute-start.3 = (bf16[16,16,128]{2,1,0:T(8,128)(2,1)S(1)}, bf16[16,16,128]{2,1,0:T(8,128)(2,1)S(1)}, u32[]{:S(2)}, u32[]{:S(2)}) collective-permute-start(bf16[16,16,128]{2,1,0:T(8,128)(2,1)S(1)} %get-tuple-element.24), channel_id=1, source_target_pairs={{0,16},{16,32},{32,48},{48,0},{1,17},{17,33},{33,49},{49,1},{2,18}... | collective-permute-start | bytes 196616 | tf_op jit(solution)/shard_map/ppermute | solution.py:309
  109.6 3.2 %collective-permute-start.4 = (bf16[16,16,128]{2,1,0:T(8,128)(2,1)S(1)}, bf16[16,16,128]{2,1,0:T(8,128)(2,1)S(1)}, u32[]{:S(2)}, u32[]{:S(2)}) collective-permute-start(bf16[16,16,128]{2,1,0:T(8,128)(2,1)S(1)} %get-tuple-element.25), channel_id=1, source_target_pairs={{0,32},{16,48},{32,0},{48,16},{1,33},{17,49},{33,1},{49,17},{2,34}... | collective-permute-start | bytes 196616 | tf_op jit(solution)/shard_map/ppermute | solution.py:309
  112.9 3.2 %collective-permute-start.5 = (bf16[16,16,128]{2,1,0:T(8,128)(2,1)S(1)}, bf16[16,16,128]{2,1,0:T(8,128)(2,1)S(1)}, u32[]{:S(2)}, u32[]{:S(2)}) collective-permute-start(bf16[16,16,128]{2,1,0:T(8,128)(2,1)S(1)} %get-tuple-element.26), channel_id=1, source_target_pairs={{0,48},{16,0},{32,16},{48,32},{1,49},{17,1},{33,17},{49,33},{2,50}... | collective-permute-start | bytes 196616 | tf_op jit(solution)/shard_map/ppermute | solution.py:309
  116.0 0.0 collective-permute-done.3.refs_7_
  116.1 0.4 collective-permute-done.4.refs_8_
  116.4 1.8 collective-permute-done.5.refs_9_
  118.2 0.0 copy-done.2
  118.2 8.8 %shard_map.106 = (bf16[512,512]{1,0:T(8,128)(2,1)}, bf16[512,512]{1,0:T(8,128)(2,1)}, bf16[512,512]{1,0:T(8,128)(2,1)}, f32[8,128]{1,0:T(8,128)S(1)}) custom-call(s32[4]{0:T(128)S(1)} %pad_add_fusion.refs_0_, s32[18,32]{1,0:T(8,128)S(1)} %copy-done.6, bf16[512,512]{1,0:T(8,128)(2,1)S(1)} %copy-done, bf16[512,512]{1,0:T(8,128)(2,1)S(1)} %copy-done.1, ...), custom_call_target="tpu_custom_call" | custom-call | flops 805306368 | bytes 3936256 | tf_op jit(solution)/shard_map/pallas_call | solution.py:56
  126.9 0.0 all-to-all-done.2.refs_1_
  126.9 1.3 shard_map.107
  128.3 0.0 reduce-scatter.2.cloned.1.call-update
  128.3 23.5 %all_to_all.25.refs_0_ = f32[16,1,128]{2,1,0:T(1,128)S(1)} all-to-all(f32[16,1,128]{2,1,0:T(1,128)S(1)} %get-tuple-element.33), channel_id=1, replica_groups=mesh['head_0'=4,'head_1'=2,'seq_0'=4,'seq_1'=16] {'seq_1'}, dimensions={0} | all-to-all | bytes 16384 | tf_op jit(solution)/shard_map/all_to_all | solution.py:313
  151.8 16.8 %all_to_all.26.refs_2_ = f32[32,1,128]{2,1,0:T(1,128)S(1)} all-to-all(f32[32,1,128]{2,1,0:T(1,128)S(1)} %shard_map.108), channel_id=1, replica_groups=mesh['head_0'=4,'head_1'=2,'seq_0'=4,'seq_1'=16] {'head_0','head_1','seq..., dimensions={0} | all-to-all | bytes 32768 | tf_op jit(solution)/shard_map/all_to_all | solution.py:313
  168.7 0.0 reduce-scatter.2.cloned.1.call-done
  168.7 0.0 copy-done.4
  168.7 0.0 copy-start.5
  168.7 0.8 copy-done.5
  169.5 0.7 shard_map.109
  (1 shorter events, 0.0 us)
Async XLA Ops:
  7.2 22.2 %copy-start.3 = (bf16[512,512]{1,0:T(8,128)(2,1)S(1)}, bf16[512,512]{1,0:T(8,128)(2,1)}, u32[]{:S(2)}) copy-start(bf16[512,512]{1,0:T(8,128)(2,1)} %refs_5_.3) | copy-start | bytes 1572868
  7.2 22.2 %copy-start = (bf16[512,512]{1,0:T(8,128)(2,1)S(1)}, bf16[512,512]{1,0:T(8,128)(2,1)}, u32[]{:S(2)}) copy-start(bf16[512,512]{1,0:T(8,128)(2,1)} %refs_2_.5) | copy-start | bytes 1572868
  7.2 22.2 %copy-start.1 = (bf16[512,512]{1,0:T(8,128)(2,1)S(1)}, bf16[512,512]{1,0:T(8,128)(2,1)}, u32[]{:S(2)}) copy-start(bf16[512,512]{1,0:T(8,128)(2,1)} %refs_3_.5) | copy-start | bytes 1572868
  7.2 22.2 %copy-start.6 = (s32[18,32]{1,0:T(8,128)S(1)}, s32[18,32]{1,0:T(8,128)}, u32[]{:S(2)}) copy-start(s32[18,32]{1,0:T(8,128)} %refs_1_.7) | copy-start | bytes 6916
  10.0 38.4 %all-to-all-start = ((bf16[64,16,128]{2,1,0:T(8,128)(2,1)}), bf16[64,16,128]{2,1,0:T(8,128)(2,1)S(1)}, u32[]{:S(2)}, u32[]{:S(2)}) async-start(bf16[64,16,128]{2,1,0:T(8,128)(2,1)} %bitcast.7), calls=%async_computation | async-start | bytes 524288 | tf_op jit(solution)/shard_map/all_to_all | solution.py:313
  36.8 28.4 %collective-permute-start = (bf16[2,2048,128]{2,1,0:T(8,128)(2,1)}, bf16[2,2048,128]{2,1,0:T(8,128)(2,1)S(1)}, u32[]{:S(2)}, u32[]{:S(2)}) collective-permute-start(bf16[2,2048,128]{2,1,0:T(8,128)(2,1)} %get-tuple-element.20), channel_id=1, source_target_pairs={{0,16},{16,32},{32,48},{48,0},{1,17},{17,33},{33,49},{49,1},{2,18}... | collective-permute-start | bytes 3145736 | tf_op jit(solution)/shard_map/ppermute | solution.py:309
  39.7 48.5 %collective-permute-start.1 = (bf16[2,2048,128]{2,1,0:T(8,128)(2,1)}, bf16[2,2048,128]{2,1,0:T(8,128)(2,1)}, u32[]{:S(2)}, u32[]{:S(2)}) collective-permute-start(bf16[2,2048,128]{2,1,0:T(8,128)(2,1)} %get-tuple-element.21), channel_id=1, source_target_pairs={{0,32},{16,48},{32,0},{48,16},{1,33},{17,49},{33,1},{49,17},{2,34}... | collective-permute-start | bytes 3145736 | tf_op jit(solution)/shard_map/ppermute | solution.py:309
  44.2 45.3 %collective-permute-start.2 = (bf16[2,2048,128]{2,1,0:T(8,128)(2,1)}, bf16[2,2048,128]{2,1,0:T(8,128)(2,1)}, u32[]{:S(2)}, u32[]{:S(2)}) collective-permute-start(bf16[2,2048,128]{2,1,0:T(8,128)(2,1)} %get-tuple-element.22), channel_id=1, source_target_pairs={{0,48},{16,0},{32,16},{48,32},{1,49},{17,1},{33,17},{49,33},{2,50}... | collective-permute-start | bytes 3145736 | tf_op jit(solution)/shard_map/ppermute | solution.py:309
  49.9 39.6 %all-to-all-start.1 = ((bf16[16,4,16,128]{3,2,1,0:T(8,128)(2,1)}), bf16[16,4,16,128]{3,2,1,0:T(8,128)(2,1)S(1)}, u32[]{:S(2)}, u32[]{:S(2)}) async-start(bf16[16,4,16,128]{3,2,1,0:T(8,128)(2,1)} %shard_map.104), calls=%async_computation.1 | async-start | bytes 524288 | tf_op jit(solution)/shard_map/all_to_all | solution.py:313
  65.2 24.3 %copy-start.7 = (bf16[2,2048,128]{2,1,0:T(8,128)(2,1)}, bf16[2,2048,128]{2,1,0:T(8,128)(2,1)S(1)}, u32[]{:S(2)}) copy-start(bf16[2,2048,128]{2,1,0:T(8,128)(2,1)S(1)} %collective-permute-done.refs_2_) | copy-start | bytes 3145732
  89.5 28.7 %copy-start.2 = (bf16[512,512]{1,0:T(8,128)(2,1)S(1)}, bf16[512,512]{1,0:T(8,128)(2,1)}, u32[]{:S(2)}) copy-start(bf16[512,512]{1,0:T(8,128)(2,1)} %refs_4_.3) | copy-start | bytes 1572868
  93.5 33.4 %all-to-all-start.2 = ((bf16[16,128,128]{2,1,0:T(8,128)(2,1)}), bf16[16,128,128]{2,1,0:T(8,128)(2,1)S(1)}, u32[]{:S(2)}, u32[]{:S(2)}) async-start(bf16[16,128,128]{2,1,0:T(8,128)(2,1)} %get-tuple-element.30), calls=%async_computation.2 | async-start | bytes 1048576 | tf_op jit(solution)/shard_map/all_to_all | solution.py:313
  104.4 64.3 %copy-start.4 = (f32[32,512]{1,0:T(8,128)S(1)}, f32[32,512]{1,0:T(8,128)}, u32[]{:S(2)}) copy-start(f32[32,512]{1,0:T(8,128)} %refs_0_.3) | copy-start | bytes 196612
  104.4 64.3 %reduce-scatter.2.cloned.1.call-start = ((), (), s32[]{:S(2)}) async-start(), calls=%async_computation.6 | async-start | bytes 327680 | tf_op jit(solution)/shard_map/reduce_scatter | solution.py:418
  104.4 11.6 %collective-permute-start.3 = (bf16[16,16,128]{2,1,0:T(8,128)(2,1)S(1)}, bf16[16,16,128]{2,1,0:T(8,128)(2,1)S(1)}, u32[]{:S(2)}, u32[]{:S(2)}) collective-permute-start(bf16[16,16,128]{2,1,0:T(8,128)(2,1)S(1)} %get-tuple-element.24), channel_id=1, source_target_pairs={{0,16},{16,32},{32,48},{48,0},{1,17},{17,33},{33,49},{49,1},{2,18}... | collective-permute-start | bytes 196616 | tf_op jit(solution)/shard_map/ppermute | solution.py:309
  109.6 6.8 %collective-permute-start.4 = (bf16[16,16,128]{2,1,0:T(8,128)(2,1)S(1)}, bf16[16,16,128]{2,1,0:T(8,128)(2,1)S(1)}, u32[]{:S(2)}, u32[]{:S(2)}) collective-permute-start(bf16[16,16,128]{2,1,0:T(8,128)(2,1)S(1)} %get-tuple-element.25), channel_id=1, source_target_pairs={{0,32},{16,48},{32,0},{48,16},{1,33},{17,49},{33,1},{49,17},{2,34}... | collective-permute-start | bytes 196616 | tf_op jit(solution)/shard_map/ppermute | solution.py:309
  112.9 5.3 %collective-permute-start.5 = (bf16[16,16,128]{2,1,0:T(8,128)(2,1)S(1)}, bf16[16,16,128]{2,1,0:T(8,128)(2,1)S(1)}, u32[]{:S(2)}, u32[]{:S(2)}) collective-permute-start(bf16[16,16,128]{2,1,0:T(8,128)(2,1)S(1)} %get-tuple-element.26), channel_id=1, source_target_pairs={{0,48},{16,0},{32,16},{48,32},{1,49},{17,1},{33,17},{49,33},{2,50}... | collective-permute-start | bytes 196616 | tf_op jit(solution)/shard_map/ppermute | solution.py:309
  168.7 0.8 copy-start.5
Sparse Core Ops, SparseCore 0:
  128.4 29.3 reduce-scatter.1

commit v10 on v8

--- a/solution.py
+++ b/solution.py
@@ -198,8 +198,7 @@
 
 
 def project_kernel(info_ref, a0, a1, a2, a3, r_hbm, out_hbm, *refs):
-    own_hbm = refs[:-7]
-    a_ref, r_ref, done_ref, r_sem, a_sems, out_sems, own_sems = refs[-7:]
+    own_hbm, a_ref, r_ref, zero_ref, done_ref, r_sem, a_sems, out_sems, own_sems = refs
     keyed = (a0, a1, a2, a3)
     n_y = len(keyed)
     chunks, _, _, rows, _ = a_ref.shape
@@ -216,10 +215,16 @@
     half = r_ref.shape[0] // 2
     nz = out_hbm.shape[0]
     each = out_hbm.shape[1] // n_y
+    zero_ref[...] = jnp.zeros_like(zero_ref)
     got[0].wait()
+    sent = []
+    for d in range(n_y):
+        sources = [r_ref.at[:, d]] + [zero_ref] * (n_y - 1)
+        sent += start_all(
+            [(x, own_hbm.at[d, lax.rem(y + n, n_y)]) for n, x in enumerate(sources)], own_sems.at[d]
+        )
     states = [r_ref[:half, lax.rem(y + n_y - n, n_y)].reshape(D, D) for n in range(n_y)]
     states = jnp.concatenate(states, axis=0)
-    sent = []
     for c in range(chunks):
         for move in moves[c]:
             move.wait()
@@ -238,25 +243,20 @@
             [(done_ref.at[c], out_hbm.at[:, pl.ds(c * inner * each, inner * each), :])],
             out_sems.at[pl.ds(c, 1)],
         )
-    sent += start_all(
-        [(r_ref.at[:, lax.rem(y + n, n_y)], own_hbm[n]) for n in range(n_y)], own_sems
-    )
     for move in sent:
         move.wait()
 
 
 def outputs_kernel(
-    info_ref, weight_ref, q_ref, k_ref, v_ref, g_ref, r0, r1, r2, r3, dq_ref, dk_ref, dv_ref, end_ref
+    info_ref, weight_ref, q_ref, k_ref, v_ref, g_ref, r_ref, dq_ref, dk_ref, dv_ref, end_ref
 ):
-    states = (r0, r1, r2, r3)
-    n_y = len(states)
+    n_y = r_ref.shape[0]
     end_ref[...] = jnp.zeros_like(end_ref)
     blocks = q_ref.shape[0] // D
-    for n in range(n_y):
-        h = lax.rem(info_ref[1] + n_y - n, n_y)
+    for h in range(n_y):
         s = lanes(h)
         head = info_ref[0] * n_y + h
-        both = states[n][...].reshape(2 * D, D)
+        both = r_ref[h].reshape(2 * D, D)
         returned, carried = both[:D], both[D:]
         query, keys, values, grad = q_ref[:, s], k_ref[:, s], v_ref[:, s], g_ref[:, s]
         base_v = dot(keys, returned, 1, 0)
@@ -371,33 +371,37 @@
     both = swap(both, Z)
 
     rows = features // 2
-    parts, *own = call(
+    parts, own = call(
         project_kernel,
-        (sds((n_z, features // n_z, D), bf16),)
-        + tuple(sds((n_z, 2 * D // n_z, D), bf16) for _ in range(n_y)),
+        (
+            sds((n_z, features // n_z, D), bf16),
+            sds((n_y, n_y, n_z, 2 * D // n_z, D), bf16),
+        ),
         (*keyed, both),
         2 * features * n_y * D * D,
         [ANY] * (n_y + 1),
-        (ANY,) * (n_y + 1),
+        (ANY,) * 2,
         scratch=[
             pltpu.VMEM((2, n_y, 2, rows, D), bf16),
             pltpu.VMEM(both.shape, bf16),
+            pltpu.VMEM((n_z, 2 * D // n_z, D), bf16),
             pltpu.VMEM((2, n_z, rows // n_z, D), bf16),
             dma((1,)),
             dma((2, n_y)),
             dma((2,)),
-            dma((n_y,)),
+            dma((n_y, n_y)),
         ],
         scalars=(info,),
         vmem=52,
     )
     parts = swap(parts, Z)
 
-    own = [own[0]] + [shift(own[n], Y, n) for n in range(1, n_y)]
+    own = lax.psum_scatter(own.reshape(n_y * n_y * 2 * D, D), Y, scatter_dimension=0, tiled=True)
+    own = own.reshape(n_y, n_z, 2 * D // n_z, D)
     query_grad, key_grad, value_grad, end = call(
         outputs_kernel,
         (sds((length, width), bf16),) * 3 + (sds((8, D), f32),),
-        (queries, keys, values, out_grad, *own),
+        (queries, keys, values, out_grad, own),
         6 * length * length * width,
         scalars=(info, level_weight),
         vmem=52,
@@ -412,7 +416,6 @@
         1 << 20,
         scratch=[pltpu.VMEM((n_y * rows, D), f32)],
         scalars=(info,),
-        after=(end,),
         vmem=8,
     )
     shard = lax.psum_scatter(
@@ -420,7 +423,12 @@
     ).reshape(heads, rows, D)
     square = swap(square, near)
     total = call(
-        stage_kernel, sds((lax.axis_size(rest), 1, D), f32), (square,), 1 << 16, vmem=8
+        stage_kernel,
+        sds((lax.axis_size(rest), 1, D), f32),
+        (square,),
+        1 << 16,
+        after=(end,),
+        vmem=8,
     )
     total = swap(total, rest)
     new_momentum = call(

time: 176 us -> 179 us (1.017)
  blocking collectives: 38.9 us -> 50.5 us
  starting transfers between devices: 62.4 us -> 55 us
  waiting for transfers between devices: 32.6 us -> 30.5 us
    ppermute x6 -> x3, starting transfers between devices: 22 us -> 10.4 us  [shift(): return lax.ppermute(x, axis, [(i, (i + by) % n) for i in range(n)])]
    all_to_all x2, blocking collectives: 38.9 us -> 50.5 us  [swap(): return lax.all_to_all(x, axes, 0, 0, tiled=True)]
    all_to_all x3, starting transfers between devices: 40.4 us -> 44.6 us  [swap(): return lax.all_to_all(x, axes, 0, 0, tiled=True)]
    ppermute x6 -> x3, waiting for transfers between devices: 31.5 us -> 29.3 us  [shift(): return lax.ppermute(x, axis, [(i, (i + by) % n) for i in range(n)])]
  transfers between devices with their start and end apart: 10 -> 8, of which waited for: 6 -> 4; matrix products, arithmetic and copies ran while one was open for 0% -> 0% of each run, Pallas kernels for 10% -> 11%
where the time goes in v10:
time: 179 us; the launch traced here: 178 us
  starting transfers between devices  55 us (31%)
  blocking collectives  50.5 us (28%)
  waiting for transfers between devices  30.5 us (17%)
  Pallas kernels  26.3 us (15%)
  between operations  14.2 us (8%)
  local copies, waits for them, and re-layouts  1.82 us (1%)
    all_to_all x2, blocking collectives, swap(): return lax.all_to_all(x, axes, 0, 0, tiled=True)  50.5 us
    all_to_all x3, starting transfers between devices, swap(): return lax.all_to_all(x, axes, 0, 0, tiled=True)  44.6 us
    ppermute x3, waiting for transfers between devices, shift(): return lax.ppermute(x, axis, [(i, (i + by) % n) for i in range(n)])  29.3 us
    pallas_call x8, Pallas kernels, call(): pl.pallas_call(run, out_shape=out_shape, grid_spec=pltpu.PrefetchScalarGr...  26.3 us
    ppermute x3, starting transfers between devices, shift(): return lax.ppermute(x, axis, [(i, (i + by) % n) for i in range(n)])  10.4 us
  transfers between devices with their start and end apart: 8, of which 4 were waited for; matrix products, arithmetic and copies ran while one was open for 0% of the time, Pallas kernels for 11%

profile of v10, /device:TPU:1, one launch (start us, length us, event | category | flops | bytes accessed | tf_op | source)
XLA Modules:
  0.0 178.5 jit_solution(4870039860699706716)
XLA Ops:
  7.2 0.0 copy-start.3
  7.2 0.0 copy-start.1
  7.2 0.0 copy-start
  7.2 0.0 copy-start.6
  7.2 2.8 %shard_map.103 = bf16[4,256,128]{2,1,0:T(8,128)(2,1)} custom-call(bf16[512,512]{1,0:T(8,128)(2,1)} %refs_2_.5, bf16[512,512]{1,0:T(8,128)(2,1)} %refs_5_.3, bf16[512,512]{1,0:T(8,128)(2,1)} %refs_3_.5, bf16[512,512]{1,0:T(8,128)(2,1)} %refs_4_.3), custom_call_target="tpu_custom_call" | custom-call | flops 134217728 | bytes 2359296 | tf_op jit(solution)/shard_map/pallas_call | solution.py:56
  10.0 19.3 %all-to-all-start = ((bf16[64,16,128]{2,1,0:T(8,128)(2,1)}), bf16[64,16,128]{2,1,0:T(8,128)(2,1)S(1)}, u32[]{:S(2)}, u32[]{:S(2)}) async-start(bf16[64,16,128]{2,1,0:T(8,128)(2,1)} %bitcast.10), calls=%async_computation | async-start | bytes 524288 | tf_op jit(solution)/shard_map/all_to_all | solution.py:313
  29.3 0.1 pad_add_fusion.refs_0_
  29.4 0.0 copy-done.3
  29.4 0.0 copy-done.1
  29.4 0.0 copy-done
  29.4 0.0 copy-done.6
  29.4 7.4 %shard_map.102 = (bf16[2,2048,128]{2,1,0:T(8,128)(2,1)}, bf16[2,2048,128]{2,1,0:T(8,128)(2,1)}, bf16[2,2048,128]{2,1,0:T(8,128)(2,1)}, bf16[2,2048,128]{2,1,0:T(8,128)(2,1)}) custom-call(s32[4]{0:T(128)S(1)} %pad_add_fusion.refs_0_, s32[18,32]{1,0:T(8,128)S(1)} %copy-done.6, bf16[512,512]{1,0:T(8,128)(2,1)S(1)} %copy-done, bf16[512,512]{1,0:T(8,128)(2,1)S(1)} %copy-done.1, ...), custom_call_target="tpu_custom_call" | custom-call | flops 2550136832 | bytes 7864320 | tf_op jit(solution)/shard_map/pallas_call | solution.py:56
  36.8 2.9 %collective-permute-start = (bf16[2,2048,128]{2,1,0:T(8,128)(2,1)}, bf16[2,2048,128]{2,1,0:T(8,128)(2,1)S(1)}, u32[]{:S(2)}, u32[]{:S(2)}) collective-permute-start(bf16[2,2048,128]{2,1,0:T(8,128)(2,1)} %get-tuple-element.17), channel_id=1, source_target_pairs={{0,16},{16,32},{32,48},{48,0},{1,17},{17,33},{33,49},{49,1},{2,18}... | collective-permute-start | bytes 3145736 | tf_op jit(solution)/shard_map/ppermute | solution.py:309
  39.7 4.5 %collective-permute-start.1 = (bf16[2,2048,128]{2,1,0:T(8,128)(2,1)}, bf16[2,2048,128]{2,1,0:T(8,128)(2,1)}, u32[]{:S(2)}, u32[]{:S(2)}) collective-permute-start(bf16[2,2048,128]{2,1,0:T(8,128)(2,1)} %get-tuple-element.18), channel_id=1, source_target_pairs={{0,32},{16,48},{32,0},{48,16},{1,33},{17,49},{33,1},{49,17},{2,34}... | collective-permute-start | bytes 3145736 | tf_op jit(solution)/shard_map/ppermute | solution.py:309
  44.2 3.0 %collective-permute-start.2 = (bf16[2,2048,128]{2,1,0:T(8,128)(2,1)}, bf16[2,2048,128]{2,1,0:T(8,128)(2,1)}, u32[]{:S(2)}, u32[]{:S(2)}) collective-permute-start(bf16[2,2048,128]{2,1,0:T(8,128)(2,1)} %get-tuple-element.19), channel_id=1, source_target_pairs={{0,48},{16,0},{32,16},{48,32},{1,49},{17,1},{33,17},{49,33},{2,50}... | collective-permute-start | bytes 3145736 | tf_op jit(solution)/shard_map/ppermute | solution.py:309
  47.2 1.1 all-to-all-done.refs_2_
  48.3 1.6 shard_map.104
  49.9 10.2 %all-to-all-start.1 = ((bf16[16,4,16,128]{3,2,1,0:T(8,128)(2,1)}), bf16[16,4,16,128]{3,2,1,0:T(8,128)(2,1)S(1)}, u32[]{:S(2)}, u32[]{:S(2)}) async-start(bf16[16,4,16,128]{3,2,1,0:T(8,128)(2,1)} %shard_map.104), calls=%async_computation.1 | async-start | bytes 524288 | tf_op jit(solution)/shard_map/all_to_all | solution.py:313
  60.1 0.0 reduce-scatter.3.cloned.1.call-start
  60.2 5.0 %collective-permute-done.refs_2_ = bf16[2,2048,128]{2,1,0:T(8,128)(2,1)S(1)} collective-permute-done((bf16[2,2048,128]{2,1,0:T(8,128)(2,1)}, bf16[2,2048,128]{2,1,0:T(8,128)(2,1)S(1)}, u32[]{:S(2)}, u32[]{:S(2)}) %collective-permute-start) | collective-permute-done | bytes 1048608 | tf_op jit(solution)/shard_map/ppermute | solution.py:309
  65.1 0.0 copy-start.8
  65.1 23.1 %collective-permute-done.1.refs_3_ = bf16[2,2048,128]{2,1,0:T(8,128)(2,1)} collective-permute-done((bf16[2,2048,128]{2,1,0:T(8,128)(2,1)}, bf16[2,2048,128]{2,1,0:T(8,128)(2,1)}, u32[]{:S(2)}, u32[]{:S(2)}) %collective-permute-start.1) | collective-permute-done | bytes 1048608 | tf_op jit(solution)/shard_map/ppermute | solution.py:309
  88.2 1.3 collective-permute-done.2.refs_4_
  89.5 0.0 all-to-all-done.1.refs_5_
  89.5 0.0 copy-done.8
  89.5 3.8 %shard_map.105 = (bf16[16,128,128]{2,1,0:T(8,128)(2,1)S(1)}, bf16[4,4,16,16,128]{4,3,2,1,0:T(8,128)(2,1)}) custom-call(s32[4]{0:T(128)S(1)} %pad_add_fusion.refs_0_, bf16[2,2048,128]{2,1,0:T(8,128)(2,1)} %get-tuple-element.16.refs_1_, bf16[2,2048,128]{2,1,0:T(8,128)(2,1)} %copy-done.8, bf16[2,2048,128]{2,1,0:T(8,128)(2,1)} %collective-permute-done.1.refs_3_, ...), custom_call_target="tpu_custom_call" | custom-call | flops 268435456 | bytes 6029312 | tf_op jit(solution)/shard_map/pallas_call | solution.py:56
  93.3 0.0 copy-start.2
  93.3 0.0 reduce-scatter.3.cloned.1.call-update
  93.3 0.0 reduce-scatter.5.cloned.1.call-start
  93.4 33.3 %all_to_all.25.refs_1_ = bf16[16,128,128]{2,1,0:T(8,128)(2,1)S(1)} all-to-all(bf16[16,128,128]{2,1,0:T(8,128)(2,1)S(1)} %get-tuple-element.24), channel_id=1, replica_groups=mesh['head_0'=4,'head_1'=2,'seq_0'=4,'seq_1'=16] {'seq_1'}, dimensions={0} | all-to-all | bytes 1048576 | tf_op jit(solution)/shard_map/all_to_all | solution.py:313
  126.6 0.0 copy-start.4
  126.6 1.3 shard_map.107
  128.0 0.0 reduce-scatter.5.cloned.1.call-update
  128.0 15.1 %all-to-all-start.3 = ((f32[32,1,128]{2,1,0:T(1,128)}), f32[32,1,128]{2,1,0:T(1,128)S(1)}, u32[]{:S(2)}, u32[]{:S(2)}) async-start(f32[32,1,128]{2,1,0:T(1,128)} %get-tuple-element.26), calls=%async_computation.5 | async-start | bytes 32768 | tf_op jit(solution)/shard_map/all_to_all | solution.py:313
  143.1 0.0 reduce-scatter.3.cloned.1.call-done
  143.1 0.0 copy-done.2
  143.1 0.0 copy-start.7
  143.1 0.9 copy-done.7
  144.1 8.8 %shard_map.106 = (bf16[512,512]{1,0:T(8,128)(2,1)}, bf16[512,512]{1,0:T(8,128)(2,1)}, bf16[512,512]{1,0:T(8,128)(2,1)}, f32[8,128]{1,0:T(8,128)S(1)}) custom-call(s32[4]{0:T(128)S(1)} %pad_add_fusion.refs_0_, s32[18,32]{1,0:T(8,128)S(1)} %copy-done.6, bf16[512,512]{1,0:T(8,128)(2,1)S(1)} %copy-done, bf16[512,512]{1,0:T(8,128)(2,1)S(1)} %copy-done.1, ...), custom_call_target="tpu_custom_call" | custom-call | flops 805306368 | bytes 3936256 | tf_op jit(solution)/shard_map/pallas_call | solution.py:56
  152.9 0.0 all-to-all-done.3.refs_0_
  152.9 17.2 %all_to_all.26.refs_2_ = f32[16,1,128]{2,1,0:T(1,128)S(1)} all-to-all(f32[16,1,128]{2,1,0:T(1,128)S(1)} %shard_map.108), channel_id=1, replica_groups=mesh['head_0'=4,'head_1'=2,'seq_0'=4,'seq_1'=16] {'seq_1'}, dimensions={0} | all-to-all | bytes 16384 | tf_op jit(solution)/shard_map/all_to_all | solution.py:313
  170.1 0.0 reduce-scatter.5.cloned.1.call-done
  170.1 0.0 copy-done.4
  170.1 0.0 copy-start.5
  170.1 0.8 copy-done.5
  170.9 0.7 shard_map.109
  (1 shorter events, 0.0 us)
Async XLA Ops:
  7.2 22.2 %copy-start.3 = (bf16[512,512]{1,0:T(8,128)(2,1)S(1)}, bf16[512,512]{1,0:T(8,128)(2,1)}, u32[]{:S(2)}) copy-start(bf16[512,512]{1,0:T(8,128)(2,1)} %refs_5_.3) | copy-start | bytes 1572868
  7.2 22.2 %copy-start.1 = (bf16[512,512]{1,0:T(8,128)(2,1)S(1)}, bf16[512,512]{1,0:T(8,128)(2,1)}, u32[]{:S(2)}) copy-start(bf16[512,512]{1,0:T(8,128)(2,1)} %refs_3_.5) | copy-start | bytes 1572868
  7.2 22.2 %copy-start = (bf16[512,512]{1,0:T(8,128)(2,1)S(1)}, bf16[512,512]{1,0:T(8,128)(2,1)}, u32[]{:S(2)}) copy-start(bf16[512,512]{1,0:T(8,128)(2,1)} %refs_2_.5) | copy-start | bytes 1572868
  7.2 22.2 %copy-start.6 = (s32[18,32]{1,0:T(8,128)S(1)}, s32[18,32]{1,0:T(8,128)}, u32[]{:S(2)}) copy-start(s32[18,32]{1,0:T(8,128)} %refs_1_.7) | copy-start | bytes 6916
  10.0 38.4 %all-to-all-start = ((bf16[64,16,128]{2,1,0:T(8,128)(2,1)}), bf16[64,16,128]{2,1,0:T(8,128)(2,1)S(1)}, u32[]{:S(2)}, u32[]{:S(2)}) async-start(bf16[64,16,128]{2,1,0:T(8,128)(2,1)} %bitcast.10), calls=%async_computation | async-start | bytes 524288 | tf_op jit(solution)/shard_map/all_to_all | solution.py:313
  36.8 28.4 %collective-permute-start = (bf16[2,2048,128]{2,1,0:T(8,128)(2,1)}, bf16[2,2048,128]{2,1,0:T(8,128)(2,1)S(1)}, u32[]{:S(2)}, u32[]{:S(2)}) collective-permute-start(bf16[2,2048,128]{2,1,0:T(8,128)(2,1)} %get-tuple-element.17), channel_id=1, source_target_pairs={{0,16},{16,32},{32,48},{48,0},{1,17},{17,33},{33,49},{49,1},{2,18}... | collective-permute-start | bytes 3145736 | tf_op jit(solution)/shard_map/ppermute | solution.py:309
  39.7 48.5 %collective-permute-start.1 = (bf16[2,2048,128]{2,1,0:T(8,128)(2,1)}, bf16[2,2048,128]{2,1,0:T(8,128)(2,1)}, u32[]{:S(2)}, u32[]{:S(2)}) collective-permute-start(bf16[2,2048,128]{2,1,0:T(8,128)(2,1)} %get-tuple-element.18), channel_id=1, source_target_pairs={{0,32},{16,48},{32,0},{48,16},{1,33},{17,49},{33,1},{49,17},{2,34}... | collective-permute-start | bytes 3145736 | tf_op jit(solution)/shard_map/ppermute | solution.py:309
  44.2 45.3 %collective-permute-start.2 = (bf16[2,2048,128]{2,1,0:T(8,128)(2,1)}, bf16[2,2048,128]{2,1,0:T(8,128)(2,1)}, u32[]{:S(2)}, u32[]{:S(2)}) collective-permute-start(bf16[2,2048,128]{2,1,0:T(8,128)(2,1)} %get-tuple-element.19), channel_id=1, source_target_pairs={{0,48},{16,0},{32,16},{48,32},{1,49},{17,1},{33,17},{49,33},{2,50}... | collective-permute-start | bytes 3145736 | tf_op jit(solution)/shard_map/ppermute | solution.py:309
  49.9 39.6 %all-to-all-start.1 = ((bf16[16,4,16,128]{3,2,1,0:T(8,128)(2,1)}), bf16[16,4,16,128]{3,2,1,0:T(8,128)(2,1)S(1)}, u32[]{:S(2)}, u32[]{:S(2)}) async-start(bf16[16,4,16,128]{3,2,1,0:T(8,128)(2,1)} %shard_map.104), calls=%async_computation.1 | async-start | bytes 524288 | tf_op jit(solution)/shard_map/all_to_all | solution.py:313
  60.1 83.0 %reduce-scatter.3.cloned.1.call-start = ((), (), s32[]{:S(2)}) async-start(), calls=%async_computation.7 | async-start | bytes 1310720 | tf_op jit(solution)/shard_map/reduce_scatter | solution.py:399
  65.1 24.3 %copy-start.8 = (bf16[2,2048,128]{2,1,0:T(8,128)(2,1)}, bf16[2,2048,128]{2,1,0:T(8,128)(2,1)S(1)}, u32[]{:S(2)}) copy-start(bf16[2,2048,128]{2,1,0:T(8,128)(2,1)S(1)} %collective-permute-done.refs_2_) | copy-start | bytes 3145732
  93.3 49.8 %copy-start.2 = (bf16[512,512]{1,0:T(8,128)(2,1)S(1)}, bf16[512,512]{1,0:T(8,128)(2,1)}, u32[]{:S(2)}) copy-start(bf16[512,512]{1,0:T(8,128)(2,1)} %refs_4_.3) | copy-start | bytes 1572868
  93.3 76.8 %reduce-scatter.5.cloned.1.call-start = ((), (), s32[]{:S(2)}) async-start(), calls=%async_computation.8 | async-start | bytes 327680 | tf_op jit(solution)/shard_map/reduce_scatter | solution.py:421
  126.6 43.5 %copy-start.4 = (f32[32,512]{1,0:T(8,128)S(1)}, f32[32,512]{1,0:T(8,128)}, u32[]{:S(2)}) copy-start(f32[32,512]{1,0:T(8,128)} %refs_0_.3) | copy-start | bytes 196612
  128.0 24.9 %all-to-all-start.3 = ((f32[32,1,128]{2,1,0:T(1,128)}), f32[32,1,128]{2,1,0:T(1,128)S(1)}, u32[]{:S(2)}, u32[]{:S(2)}) async-start(f32[32,1,128]{2,1,0:T(1,128)} %get-tuple-element.26), calls=%async_computation.5 | async-start | bytes 32768 | tf_op jit(solution)/shard_map/all_to_all | solution.py:313
  143.1 1.0 copy-start.7
  170.1 0.8 copy-start.5
Sparse Core Ops, SparseCore 0:
  93.4 30.9 reduce-scatter.2
  128.1 28.9 reduce-scatter.4
